TPU v7x, 32 devices: a whole 2x2x4 slice. The times are simulated.
32 devices in a mesh: fsdp: 4 (over x, core), seq: 8 (over z, y).
Axes of the slice: x: 2, y: 2, z: 4, core: 2. Of those that a mesh axis runs over, the one named last changes fastest.
Arguments:
- inputs: bfloat16 [8192, 768], P(('fsdp', 'seq')), may hold values from -6 to 6
- cotangent: bfloat16 [8192, 768], P(('fsdp', 'seq')), may hold values from -6 to 6
- span_order: int32 [4, 8], P('fsdp'), may hold values from 0 to 7, each once within a row
- query_weight: float32 [768, 768], P(('fsdp', 'seq')), may hold values from -0.3125 to 0.3125
- keyval_weight: float32 [768, 128], P(('fsdp', 'seq')), may hold values from -0.21875 to 0.21875
- output_weight: float32 [768, 768], P(('fsdp', 'seq')), may hold values from -1.75 to 1.75
- up_weight: float32 [768, 3072], P(('fsdp', 'seq')), may hold values from -0.21875 to 0.21875
- down_weight: float32 [3072, 768], P(('fsdp', 'seq')), may hold values from -0.109375 to 0.109375
- vectors: float32 [11, 768], P(None, ('fsdp', 'seq')), may hold values from -0.3 to 2.3, as said below
- kv_bias: float32 [128], P('seq'), may hold values from -1.8 to 1.8
- first_query: float32 [768, 768], P(('fsdp', 'seq')), may hold values from -0.00024414062 to 0.00024414062
- first_keyval: float32 [768, 128], P(('fsdp', 'seq')), may hold values from -0.00024414062 to 0.00024414062
- first_output: float32 [768, 768], P(('fsdp', 'seq')), may hold values from -7.6293945e-05 to 7.6293945e-05
- first_up: float32 [768, 3072], P(('fsdp', 'seq')), may hold values from -7.6293945e-05 to 7.6293945e-05
- first_down: float32 [3072, 768], P(('fsdp', 'seq')), may hold values from -0.00024414062 to 0.00024414062
- first_vectors: float32 [11, 768], P(None, ('fsdp', 'seq')), may hold values from -0.0008544922 to 0.0008544922
- first_kv_bias: float32 [128], P('seq'), may hold values from -0.0008544922 to 0.0008544922
- second_query: float32 [768, 768], P(('fsdp', 'seq')), may hold values from 8.3262286e-11 to 1.3321966e-09
- second_keyval: float32 [768, 128], P(('fsdp', 'seq')), may hold values from 8.3262286e-11 to 1.3321966e-09
- second_output: float32 [768, 768], P(('fsdp', 'seq')), may hold values from 9.991474e-12 to 1.4987211e-10
- second_up: float32 [768, 3072], P(('fsdp', 'seq')), may hold values from 9.991474e-12 to 1.4987211e-10
- second_down: float32 [3072, 768], P(('fsdp', 'seq')), may hold values from 8.3262286e-11 to 1.3321966e-09
- second_vectors: float32 [11, 768], P(None, ('fsdp', 'seq')), may hold values from 7.493605e-10 to 1.1989768e-08
- second_kv_bias: float32 [128], P('seq'), may hold values from 7.493605e-10 to 1.1989768e-08
Outputs:
- block_output: bfloat16 [8192, 768], P(('fsdp', 'seq'))
- input_grad: float32 [8192, 768], P(('fsdp', 'seq'))
- grad_norm: float32 [], replicated
- new_query_weight: float32 [768, 768], P(('fsdp', 'seq'))
- new_keyval_weight: float32 [768, 128], P(('fsdp', 'seq'))
- new_output_weight: float32 [768, 768], P(('fsdp', 'seq'))
- new_up_weight: float32 [768, 3072], P(('fsdp', 'seq'))
- new_down_weight: float32 [3072, 768], P(('fsdp', 'seq'))
- new_vectors: float32 [11, 768], P(None, ('fsdp', 'seq'))
- new_kv_bias: float32 [128], P('seq')
- next_first_query: float32 [768, 768], P(('fsdp', 'seq'))
- next_first_keyval: float32 [768, 128], P(('fsdp', 'seq'))
- next_first_output: float32 [768, 768], P(('fsdp', 'seq'))
- next_first_up: float32 [768, 3072], P(('fsdp', 'seq'))
- next_first_down: float32 [3072, 768], P(('fsdp', 'seq'))
- next_first_vectors: float32 [11, 768], P(None, ('fsdp', 'seq'))
- next_first_kv_bias: float32 [128], P('seq')
- next_second_query: float32 [768, 768], P(('fsdp', 'seq'))
- next_second_keyval: float32 [768, 128], P(('fsdp', 'seq'))
- next_second_output: float32 [768, 768], P(('fsdp', 'seq'))
- next_second_up: float32 [768, 3072], P(('fsdp', 'seq'))
- next_second_down: float32 [3072, 768], P(('fsdp', 'seq'))
- next_second_vectors: float32 [11, 768], P(None, ('fsdp', 'seq'))
- next_second_kv_bias: float32 [128], P('seq')
- residual_bias_grads: float32 [2, 768], P(None, ('fsdp', 'seq'))
Inputs may be any that keep to these rules, and one draw needn't show every extreme that they name: `span_order`: each row holds every block index of one sequence exactly once. `vectors`: rows 0 and 2 are positive gains; the other rows are biases.
All inputs are finite; a program needn't handle non-finite values.
Results may differ from a plain program's by a relative error of at most 0.018.
The roundings to bfloat16 on the way count: a program that leaves them out, or rounds other values in their place, can miss the bound.
Values may be sent and summed in bfloat16 or wider, within the bound.
A program may use at most 128 MiB of HBM per device.

v0:
```python
import math

import jax
import jax.numpy as jnp
from jax import lax
from jax.sharding import PartitionSpec as P

D = 768
HQ = 12
HD = 64
ROT_DIMS = 16
FF = 3072
KEY_BLOCK = 512
STEP = 10


NORM_EPS = 1e-05
MASKED = -1e30
CLIP_NORM = 1.0
BETA_ONE = 0.9
BETA_TWO = 0.999
ADAM_EPS = 1e-08
MATRIX_DECAY = 0.1
MATRIX_RATE = 0.1
VECTOR_RATE = 0.3


def layer_norm(tensor, gain_row, shift_row):
    centre = tensor - jnp.mean(tensor, -1, keepdims=True)
    spread = jnp.mean(centre * centre, -1, keepdims=True)
    return centre * lax.rsqrt(spread + NORM_EPS) * gain_row + shift_row


def rotary_tables(places):
    half_steps = jnp.arange(ROT_DIMS // 2, dtype=jnp.float32)
    inverse = jnp.exp(half_steps * (-2.0 * math.log(10000.0) / ROT_DIMS))
    angles = places.astype(jnp.float32)[:, None] * (0.25 * inverse)[None, :]
    angles = jnp.concatenate([angles, angles], 1)
    return (jnp.cos(angles), jnp.sin(angles))


def rotate(tensor, cosine, sine_table):
    rotary_part = tensor[..., :ROT_DIMS]
    lower_half = rotary_part[..., : ROT_DIMS // 2]
    upper_half = rotary_part[..., ROT_DIMS // 2 :]
    turned = jnp.concatenate([-upper_half, lower_half], -1)
    return jnp.concatenate([rotary_part * cosine + turned * sine_table, tensor[..., ROT_DIMS:]], -1)


def adamw(master, clipped, first_old, second_old, step_rate, decay_rate):
    first_new = BETA_ONE * first_old + (1.0 - BETA_ONE) * clipped
    second_new = BETA_TWO * second_old + (1.0 - BETA_TWO) * clipped * clipped
    ascent = (
        first_new
        / (1.0 - BETA_ONE**STEP)
        / (jnp.sqrt(second_new / (1.0 - BETA_TWO**STEP)) + ADAM_EPS)
    )
    return (master - step_rate * (ascent + decay_rate * master), first_new, second_new)


def gelu_exact(tensor):
    return jax.nn.gelu(tensor, approximate=False)


def across_tokens(left_side, right_side):
    return lax.dot_general(
        left_side, right_side, (((0,), (0,)), ((), ())), preferred_element_type=jnp.float32
    )


def against(left_side, right_side):
    return lax.dot_general(
        left_side, right_side, (((1,), (1,)), ((), ())), preferred_element_type=jnp.float32
    )


def masked_scores(query_rows, row_places, key_block, key_places):
    scores = against(query_rows, key_block) * HD ** (-0.5)
    return jnp.where(key_places[None, :] <= row_places[:, None], scores, MASKED)


def body(
    inputs,
    cotangent,
    span_order,
    query_weight,
    keyval_weight,
    output_weight,
    up_weight,
    down_weight,
    vectors,
    kv_bias,
    first_query,
    first_keyval,
    first_output,
    first_up,
    first_down,
    first_vectors,
    first_kv_bias,
    second_query,
    second_keyval,
    second_output,
    second_up,
    second_down,
    second_vectors,
    second_kv_bias,
):
    tok_rows = inputs.shape[0]
    seq_count = lax.axis_size("seq")
    seq_rank = lax.axis_index("seq")
    order_row = span_order[0]
    token_steps = jnp.arange(tok_rows, dtype=jnp.int32)
    all_places = (order_row[:, None] * tok_rows + token_steps[None, :]).reshape(
        seq_count * tok_rows
    )
    own_span = jnp.sum(jnp.where(jnp.arange(seq_count, dtype=jnp.int32) == seq_rank, order_row, 0))
    own_places = own_span * tok_rows + token_steps
    query_rows_count = tok_rows * HQ
    query_full, keyval_full, output_full, up_full, down_full, vector_full = (
        lax.all_gather(query_weight.astype(jnp.bfloat16), ("fsdp", "seq"), axis=0, tiled=True),
        lax.all_gather(keyval_weight.astype(jnp.bfloat16), ("fsdp", "seq"), axis=0, tiled=True),
        lax.all_gather(output_weight.astype(jnp.bfloat16), ("fsdp", "seq"), axis=0, tiled=True),
        lax.all_gather(up_weight.astype(jnp.bfloat16), ("fsdp", "seq"), axis=0, tiled=True),
        lax.all_gather(down_weight.astype(jnp.bfloat16), ("fsdp", "seq"), axis=0, tiled=True),
        lax.all_gather(vectors.astype(jnp.bfloat16), ("fsdp", "seq"), axis=1, tiled=True),
    )
    kv_shift = lax.all_gather(kv_bias.astype(jnp.bfloat16), "seq", axis=0, tiled=True).astype(
        jnp.float32
    )
    gains = vector_full.astype(jnp.float32)
    states = inputs.astype(jnp.float32)
    normed_one = layer_norm(states, gains[0], gains[1])
    normed_low = normed_one.astype(jnp.bfloat16)
    query_pre = jnp.dot(normed_low, query_full, preferred_element_type=jnp.float32) + gains[4]
    keyval_pre = jnp.dot(normed_low, keyval_full, preferred_element_type=jnp.float32) + kv_shift
    cosine, sine_table = rotary_tables(own_places)

    def turn_queries(tensor):
        return rotate(tensor.reshape(tok_rows, HQ, HD), cosine[:, None, :], sine_table[:, None, :])

    def turn_keys(tensor):
        return jnp.concatenate([rotate(tensor[:, :HD], cosine, sine_table), tensor[:, HD:]], 1)

    query_rows = turn_queries(query_pre).astype(jnp.bfloat16).reshape(query_rows_count, HD)
    local_pairs = turn_keys(keyval_pre).astype(jnp.bfloat16)
    row_places = jnp.broadcast_to(own_places[:, None], (tok_rows, HQ)).reshape(query_rows_count)
    all_pairs = lax.all_gather(local_pairs, "seq", axis=0, tiled=True)
    block_count = all_pairs.shape[0] // KEY_BLOCK
    place_blocks = all_places.reshape(block_count, KEY_BLOCK)

    def lse_step(carry_pair, block_pair):
        running_top, running_total = carry_pair
        pair_block, key_places = block_pair
        scores = masked_scores(query_rows, row_places, pair_block[:, :HD], key_places)
        new_top = jnp.maximum(running_top, jnp.max(scores, 1, keepdims=True))
        running_total = running_total * jnp.exp(running_top - new_top) + jnp.sum(
            jnp.exp(scores - new_top), 1, keepdims=True
        )
        return ((new_top, running_total), None)

    start_carry = (
        jnp.full((query_rows_count, 1), MASKED, jnp.float32),
        jnp.zeros((query_rows_count, 1), jnp.float32),
    )
    (row_top, row_total), _ = lax.scan(
        lse_step, start_carry, (all_pairs.reshape(block_count, KEY_BLOCK, 2 * HD), place_blocks)
    )
    log_total = row_top + jnp.log(row_total)

    def mix_step(mixed_acc, block_pair):
        pair_block, key_places = block_pair
        probs_low = jnp.exp(
            masked_scores(query_rows, row_places, pair_block[:, :HD], key_places) - log_total
        ).astype(jnp.bfloat16)
        return (
            mixed_acc + jnp.dot(probs_low, pair_block[:, HD:], preferred_element_type=jnp.float32),
            None,
        )

    mixed, _ = lax.scan(
        mix_step,
        jnp.zeros((query_rows_count, HD), jnp.float32),
        (all_pairs.reshape(block_count, KEY_BLOCK, 2 * HD), place_blocks),
    )
    mixed_low = mixed.reshape(tok_rows, D).astype(jnp.bfloat16)
    attention_out = jnp.dot(mixed_low, output_full, preferred_element_type=jnp.float32) + gains[5]
    normed_two = layer_norm(states, gains[2], gains[3])
    normed_two_low = normed_two.astype(jnp.bfloat16)
    lifted = jnp.dot(normed_two_low, up_full, preferred_element_type=jnp.float32) + gains[
        7:
    ].reshape(FF)
    active_low = gelu_exact(lifted).astype(jnp.bfloat16)
    block_output = (
        states
        + attention_out
        + jnp.dot(active_low, down_full, preferred_element_type=jnp.float32)
        + gains[6]
    ).astype(jnp.bfloat16)
    back_rows = cotangent.astype(jnp.float32)
    query_back, keyval_back, output_back, up_back, down_back = (
        lax.all_gather(query_weight.astype(jnp.bfloat16), ("fsdp", "seq"), axis=0, tiled=True),
        lax.all_gather(keyval_weight.astype(jnp.bfloat16), ("fsdp", "seq"), axis=0, tiled=True),
        lax.all_gather(output_weight.astype(jnp.bfloat16), ("fsdp", "seq"), axis=0, tiled=True),
        lax.all_gather(up_weight.astype(jnp.bfloat16), ("fsdp", "seq"), axis=0, tiled=True),
        lax.all_gather(down_weight.astype(jnp.bfloat16), ("fsdp", "seq"), axis=0, tiled=True),
    )
    grad_down = across_tokens(active_low, cotangent)
    grad_output = across_tokens(mixed_low, cotangent)
    out_bias_grad = jnp.sum(back_rows, 0)
    active_grad = against(cotangent, down_back)
    _, gelu_pull = jax.vjp(gelu_exact, lifted)
    (lifted_grad,) = gelu_pull(active_grad)
    lifted_low = lifted_grad.astype(jnp.bfloat16)
    grad_up = across_tokens(normed_two_low, lifted_low)
    normed_two_grad = against(lifted_low, up_back)
    mixed_grad = against(cotangent, output_back).astype(jnp.bfloat16).reshape(query_rows_count, HD)
    row_delta = jnp.sum(mixed_grad.astype(jnp.float32) * mixed, 1, keepdims=True)
    pairs_back = lax.all_gather(local_pairs, "seq", axis=0, tiled=True)

    def grad_step(query_acc, block_pair):
        pair_block, key_places = block_pair
        key_block = pair_block[:, :HD]
        probs = jnp.exp(masked_scores(query_rows, row_places, key_block, key_places) - log_total)
        prob_grad = against(mixed_grad, pair_block[:, HD:])
        score_low = (probs * (prob_grad - row_delta)).astype(jnp.bfloat16)
        query_acc = query_acc + jnp.dot(score_low, key_block, preferred_element_type=jnp.float32)
        key_grad = across_tokens(score_low, query_rows) * HD ** (-0.5)
        value_grad = across_tokens(probs.astype(jnp.bfloat16), mixed_grad)
        return (query_acc, jnp.concatenate([key_grad, value_grad], 1))

    query_sum, pair_grads = lax.scan(
        grad_step,
        jnp.zeros((query_rows_count, HD), jnp.float32),
        (pairs_back.reshape(block_count, KEY_BLOCK, 2 * HD), place_blocks),
    )
    query_rot_grad = (query_sum * HD ** (-0.5)).reshape(tok_rows, HQ, HD)
    own_pair_grad = lax.psum_scatter(
        pair_grads.reshape(block_count * KEY_BLOCK, 2 * HD).astype(jnp.bfloat16),
        "seq",
        scatter_dimension=0,
        tiled=True,
    ).astype(jnp.float32)
    _, key_pull = jax.vjp(turn_keys, keyval_pre)
    (keyval_grad,) = key_pull(own_pair_grad)
    keyval_low = keyval_grad.astype(jnp.bfloat16)
    _, query_pull = jax.vjp(turn_queries, query_pre)
    (query_pre_grad,) = query_pull(query_rot_grad)
    query_low = query_pre_grad.astype(jnp.bfloat16)
    grad_query = across_tokens(normed_low, query_low)
    grad_keyval = across_tokens(normed_low, keyval_low)
    kv_bias_part = jnp.sum(keyval_low.astype(jnp.float32), 0)
    normed_one_grad = against(query_low, query_back) + against(keyval_low, keyval_back)
    _, first_pull = jax.vjp(layer_norm, states, gains[0], gains[1])
    input_one, gain_one_grad, shift_one_grad = first_pull(normed_one_grad)
    _, second_pull = jax.vjp(layer_norm, states, gains[2], gains[3])
    input_two, gain_two_grad, shift_two_grad = second_pull(normed_two_grad)
    input_grad = back_rows + input_one + input_two
    vector_grad = jnp.concatenate(
        [
            jnp.stack(
                [
                    gain_one_grad,
                    shift_one_grad,
                    gain_two_grad,
                    shift_two_grad,
                    jnp.sum(query_low.astype(jnp.float32), 0),
                    out_bias_grad,
                    out_bias_grad,
                ]
            ),
            jnp.sum(lifted_low.astype(jnp.float32), 0).reshape(FF // D, D),
        ],
        0,
    )
    reduced = (
        lax.psum_scatter(grad_query, ("fsdp", "seq"), scatter_dimension=0, tiled=True),
        lax.psum_scatter(grad_keyval, ("fsdp", "seq"), scatter_dimension=0, tiled=True),
        lax.psum_scatter(grad_output, ("fsdp", "seq"), scatter_dimension=0, tiled=True),
        lax.psum_scatter(grad_up, ("fsdp", "seq"), scatter_dimension=0, tiled=True),
        lax.psum_scatter(grad_down, ("fsdp", "seq"), scatter_dimension=0, tiled=True),
        lax.psum_scatter(vector_grad, ("fsdp", "seq"), scatter_dimension=1, tiled=True),
    )
    reduced = tuple(reduced)
    local_squares = sum((jnp.sum(gradient * gradient) for gradient in reduced))
    global_squares, kv_bias_total = lax.psum((local_squares, kv_bias_part), ("fsdp", "seq"))
    grad_norm = jnp.sqrt(global_squares + jnp.sum(kv_bias_total * kv_bias_total))
    piece_width = kv_bias.shape[0]
    kv_bias_grad = lax.dynamic_slice_in_dim(kv_bias_total, seq_rank * piece_width, piece_width)
    factor = jnp.minimum(1.0, CLIP_NORM / (grad_norm + 1e-06))
    masters = (query_weight, keyval_weight, output_weight, up_weight, down_weight, vectors, kv_bias)
    all_grads = reduced + (kv_bias_grad,)
    firsts = (
        first_query,
        first_keyval,
        first_output,
        first_up,
        first_down,
        first_vectors,
        first_kv_bias,
    )
    seconds = (
        second_query,
        second_keyval,
        second_output,
        second_up,
        second_down,
        second_vectors,
        second_kv_bias,
    )
    step_rates = (MATRIX_RATE,) * 5 + (VECTOR_RATE, VECTOR_RATE)
    decays = (MATRIX_DECAY,) * 5 + (0.0, 0.0)
    updated = [
        adamw(master, gradient * factor, first_old, second_old, step_rate, decay_rate)
        for master, gradient, first_old, second_old, step_rate, decay_rate in zip(
            masters, all_grads, firsts, seconds, step_rates, decays
        )
    ]
    residual_bias_grads = (reduced[5] * factor)[5:7]
    return (
        block_output,
        input_grad,
        grad_norm,
        updated[0][0],
        updated[1][0],
        updated[2][0],
        updated[3][0],
        updated[4][0],
        updated[5][0],
        updated[6][0],
        updated[0][1],
        updated[1][1],
        updated[2][1],
        updated[3][1],
        updated[4][1],
        updated[5][1],
        updated[6][1],
        updated[0][2],
        updated[1][2],
        updated[2][2],
        updated[3][2],
        updated[4][2],
        updated[5][2],
        updated[6][2],
        residual_bias_grads,
    )


def solution(mesh):
    return jax.shard_map(
        body,
        mesh=mesh,
        in_specs=(
            P(("fsdp", "seq"), None),
            P(("fsdp", "seq"), None),
            P("fsdp", None),
            P(("fsdp", "seq"), None),
            P(("fsdp", "seq"), None),
            P(("fsdp", "seq"), None),
            P(("fsdp", "seq"), None),
            P(("fsdp", "seq"), None),
            P(None, ("fsdp", "seq")),
            P("seq"),
            P(("fsdp", "seq"), None),
            P(("fsdp", "seq"), None),
            P(("fsdp", "seq"), None),
            P(("fsdp", "seq"), None),
            P(("fsdp", "seq"), None),
            P(None, ("fsdp", "seq")),
            P("seq"),
            P(("fsdp", "seq"), None),
            P(("fsdp", "seq"), None),
            P(("fsdp", "seq"), None),
            P(("fsdp", "seq"), None),
            P(("fsdp", "seq"), None),
            P(None, ("fsdp", "seq")),
            P("seq"),
        ),
        out_specs=(
            P(("fsdp", "seq"), None),
            P(("fsdp", "seq"), None),
            P(),
            P(("fsdp", "seq"), None),
            P(("fsdp", "seq"), None),
            P(("fsdp", "seq"), None),
            P(("fsdp", "seq"), None),
            P(("fsdp", "seq"), None),
            P(None, ("fsdp", "seq")),
            P("seq"),
            P(("fsdp", "seq"), None),
            P(("fsdp", "seq"), None),
            P(("fsdp", "seq"), None),
            P(("fsdp", "seq"), None),
            P(("fsdp", "seq"), None),
            P(None, ("fsdp", "seq")),
            P("seq"),
            P(("fsdp", "seq"), None),
            P(("fsdp", "seq"), None),
            P(("fsdp", "seq"), None),
            P(("fsdp", "seq"), None),
            P(("fsdp", "seq"), None),
            P(None, ("fsdp", "seq")),
            P("seq"),
            P(None, ("fsdp", "seq")),
        ),
        check_vma=False,
    )
```

profile of v0, /device:TPU:0, one launch (start us, length us, event | category | flops | bytes accessed | tf_op | source)
XLA Modules:
  0.0 1191.0 jit_solution(5755652887950418151)
XLA Ops:
  11.2 70.7 %all-gather = bf16[32,24,11]{1,2,0:T(8,128)(2,1)S(1)} all-gather(bf16[1,24,11]{1,2,0:T(8,128)(2,1)S(1)} %convert_bitcast_fusion.1), channel_id=1, replica_groups=mesh['fsdp'=4,'seq'=8] {'fsdp','seq'}, dimensions={0}, use_global_device_ids=true | all-gather | bytes 17424 | tf_op jit(solution)/shard_map/all_gather | solution.py:125
  86.1 64.6 %all_gather.31 = bf16[768,128]{1,0:T(8,128)(2,1)S(1)} all-gather(bf16[24,128]{1,0:T(8,128)(2,1)S(1)} %convert_element_type.117), channel_id=1, replica_groups=mesh['fsdp'=4,'seq'=8] {'fsdp','seq'}, dimensions={0}, use_global_device_ids=true | all-gather | bytes 202752 | tf_op jit(solution)/shard_map/all_gather | solution.py:121
  153.5 19.3 %all-reduce.10 = bf16[128]{0:T(256)(128)(2,1)S(1)} all-reduce(bf16[128]{0:T(256)(128)(2,1)S(1)} %dynamic-update-slice), channel_id=1, replica_groups=mesh['fsdp'=4,'seq'=8] {'seq'}, use_global_device_ids=true, to_apply=%add.10 | all-reduce | flops 128 | bytes 512
  176.5 31.4 %all_gather.33 = bf16[2048,128]{0,1:T(8,128)(2,1)S(1)} all-gather(bf16[256,128]{0,1:T(8,128)(2,1)S(1)} %pad_maximum_fusion.1), channel_id=1, replica_groups=mesh['fsdp'=4,'seq'=8] {'seq'}, dimensions={0}, use_global_device_ids=true | all-gather | bytes 589824 | tf_op jit(solution)/shard_map/all_gather | solution.py:147
  216.7 41.8 %while.37 = (s32[]{:T(128)}, f32[3072,1]{0,1:T(1,128)S(1)}, f32[3072,1]{0,1:T(1,128)S(1)}, s32[4,512]{1,0:T(4,128)S(1)}, bf16[4,512,128]{2,1,0:T(8,128)(2,1)}, /...) while((s32[]{:T(128)}, f32[3072,1]{0,1:T(1,128)S(1)}, ...), condition=%wide.region_6.7_spmd.clone, body=%wide.region_3.6_spmd.clone.sunk | while | flops 215497728 | bytes 13599864 | solution.py:165
  218.1 4.8 fusion.153
  228.5 4.8 fusion.153
  249.3 4.8 fusion.153
  258.6 17.7 %while.38 = (s32[]{:T(128)}, f32[3072,64]{0,1:T(8,128)S(1)}, s32[4,512]{1,0:T(4,128)S(1)}, bf16[4,512,128]{2,1,0:T(8,128)(2,1)}, bf16[3072,64]{1,0:T(8,128)(2,1)...) while((s32[]{:T(128)}, f32[3072,64]{0,1:T(8,128)S(1)}, ...), condition=%wide.region_8.9_spmd.clone, body=%wide.region_7.8_spmd.clone.sunk | while | flops 410910720 | bytes 2559095 | solution.py:180
  281.7 59.2 %while.39 = (s32[]{:T(128)}, f32[3072,64]{0,1:T(8,128)}, bf16[4,512,128]{1,2,0:T(8,128)(2,1)}, s32[4,512]{1,0:T(4,128)S(1)}, bf16[4,512,128]{2,1,0:T(8,128)(2,1)...) while((s32[]{:T(128)}, f32[3072,64]{0,1:T(8,128)}, ...), condition=%wide.region_11.12_spmd.clone, body=%wide.region_10.11_spmd.clone.sunk | while | flops 1019936768 | bytes 82918600 | solution.py:231
  350.7 51.3 %reduce-scatter.10.cloned.1.call-done = bf16[256,128]{0,1:T(8,128)(2,1)} async-done(((bf16[2048,128]{0,1:T(8,128)(2,1)}), bf16[256,128]{0,1:T(8,128)(2,1)}) %reduce-scatter.10.cloned.1.call-update) | async-done | bytes 65552 | tf_op jit(solution)/shard_map/reduce_scatter | solution.py:237
  417.4 51.0 %all-gather.10.cloned.1.call-done = bf16[768,3072]{1,0:T(8,128)(2,1)} async-done(((bf16[24,3072]{1,0:T(8,128)(2,1)}), bf16[768,3072]{1,0:T(8,128)(2,1)}) %all-gather.10.cloned.1.call-update) | async-done | bytes 4718608 | tf_op jit(solution)/shard_map/all_gather | solution.py:123
  468.4 5.5 convolution_add_fusion.2
  473.9 60.8 %all-gather.12.cloned.1.call-done = bf16[3072,768]{1,0:T(8,128)(2,1)} async-done(((bf16[96,768]{1,0:T(8,128)(2,1)}), bf16[3072,768]{1,0:T(8,128)(2,1)}) %all-gather.12.cloned.1.call-update) | async-done | bytes 4718608 | tf_op jit(solution)/shard_map/all_gather | solution.py:124
  534.7 12.1 %convert_reduce_fusion = (f32[3072]{0:T(1024)}, bf16[256,3072]{1,0:T(8,128)(2,1)S(1)}, f32[256,3072]{1,0:T(8,128)}) fusion(f32[256,3072]{1,0:T(8,128)} %convolution_add_fusion.2, bf16[256,768]{1,0:T(8,128)(2,1)S(1)} %copy-done.6, bf16[3072,768]{1,0:T(8,128)(2,1)} %all-gather.12.cloned.1.call-done), kind=kOutput, calls=%fused_computation.45 | convolution fusion | flops 1266152448 | bytes 12988416 | tf_op jit(solution)/shard_map/dot_general | solution.py:72
  546.7 5.2 fusion.76
  555.7 5.1 fusion.100
  564.8 69.6 %reduce-scatter.20.cloned.1.call-done = f32[24,128]{1,0:T(8,128)} async-done(((f32[768,128]{1,0:T(8,128)}), f32[24,128]{1,0:T(8,128)}) %reduce-scatter.20.cloned.1.call-update) | async-done | bytes 12304
  635.7 102.1 %reduce-scatter.12.cloned.1.call-done = f32[24,768]{1,0:T(8,128)} async-done(((f32[768,768]{1,0:T(8,128)}), f32[24,768]{1,0:T(8,128)}) %reduce-scatter.12.cloned.1.call-update) | async-done | bytes 73744 | tf_op jit(solution)/shard_map/reduce_scatter | solution.py:276
  740.6 101.4 %reduce-scatter.14.cloned.1.call-done = f32[24,768]{1,0:T(8,128)} async-done(((f32[768,768]{1,0:T(8,128)}), f32[24,768]{1,0:T(8,128)}) %reduce-scatter.14.cloned.1.call-update) | async-done | bytes 73744 | tf_op jit(solution)/shard_map/reduce_scatter | solution.py:278
  851.6 40.3 %all-reduce.12 = f32[11,768]{1,0:T(8,128)S(1)} all-reduce(f32[11,768]{1,0:T(8,128)S(1)} %concatenate.44), channel_id=8, replica_groups=mesh['fsdp'=4,'seq'=8] {'fsdp','seq'}, use_global_device_ids=true, to_apply=%region_34.35.clone | all-reduce | flops 8448 | bytes 67584
  898.1 84.3 %reduce-scatter.16.cloned.1.call-done = f32[24,3072]{1,0:T(8,128)} async-done(((f32[768,3072]{1,0:T(8,128)}), f32[24,3072]{1,0:T(8,128)}) %reduce-scatter.16.cloned.1.call-update) | async-done | bytes 294928 | tf_op jit(solution)/shard_map/reduce_scatter | solution.py:279
  984.7 139.1 %reduce-scatter.18.cloned.1.call-done = f32[96,768]{1,0:T(8,128)} async-done(((f32[3072,768]{1,0:T(8,128)}), f32[96,768]{1,0:T(8,128)}) %reduce-scatter.18.cloned.1.call-update) | async-done | bytes 294928 | tf_op jit(solution)/shard_map/reduce_scatter | solution.py:280
  1129.3 40.1 %all-reduce.13 = (f32[]{:T(128)}, f32[128]{0:T(128)S(1)}) all-reduce(f32[]{:T(128)S(6)} %add.357, f32[128]{0:T(128)} %convert_reduce_fusion.4), channel_id=1, replica_groups=mesh['fsdp'=4,'seq'=8] {'fsdp','seq'}, use_global_device_ids=true, to_apply=%region_36.37 | all-reduce | flops 129 | bytes 1032 | tf_op jit(solution)/shard_map/psum | solution.py:285
  (345 shorter events, 198.6 us)
Async XLA Ops:
  7.2 201.7 %copy-start.3 = (bf16[256,768]{1,0:T(8,128)(2,1)S(1)}, bf16[256,768]{1,0:T(8,128)(2,1)}, u32[]{:S(2)}) copy-start(bf16[256,768]{1,0:T(8,128)(2,1)} %param.30) | copy-start | bytes 1179652
  7.2 167.0 %copy-start.49 = (s32[1,8]{1,0:T(1,128)S(1)}, s32[1,8]{1,0:T(1,128)}, u32[]{:S(2)}) copy-start(s32[1,8]{1,0:T(1,128)} %param.32) | copy-start | bytes 100
  7.2 201.7 %all-gather.6.cloned.1.call-start = ((), (), s32[]{:S(2)}) async-start(), calls=%async_computation.6 | async-start | bytes 1216512 | tf_op jit(solution)/shard_map/all_gather | solution.py:120
  8.8 267.4 %all-gather.8.cloned.1.call-start = ((), (), s32[]{:S(2)}) async-start(), calls=%async_computation.7 | async-start | bytes 1216512 | tf_op jit(solution)/shard_map/all_gather | solution.py:122
  10.4 391.5 %reduce-scatter.10.cloned.1.call-start = ((), (), s32[]{:S(2)}) async-start(), calls=%async_computation.10 | async-start | bytes 589824 | tf_op jit(solution)/shard_map/reduce_scatter | solution.py:237
  82.9 127.8 %copy-start.42 = (f32[768]{0:T(1024)}, f32[768]{0:T(1024)S(1)}, u32[]{:S(2)}) copy-start(f32[768]{0:T(1024)S(1)} %get-tuple-element.359) | copy-start | bytes 9220
  84.1 126.7 %copy-start.34 = (f32[256]{0:T(256)}, f32[256]{0:T(256)S(1)}, u32[]{:S(2)}) copy-start(f32[256]{0:T(256)S(1)} %broadcast_multiply_fusion.3) | copy-start | bytes 3076
  342.9 125.5 %all-gather.10.cloned.1.call-start = ((), (), s32[]{:S(2)}) async-start(), calls=%async_computation.8 | async-start | bytes 4866048 | tf_op jit(solution)/shard_map/all_gather | solution.py:123
  344.6 190.0 %all-gather.12.cloned.1.call-start = ((), (), s32[]{:S(2)}) async-start(), calls=%async_computation.9 | async-start | bytes 4866048 | tf_op jit(solution)/shard_map/all_gather | solution.py:124
  346.4 288.1 %reduce-scatter.20.cloned.1.call-start = ((), (), s32[]{:S(2)}) async-start(), calls=%async_computation.15 | async-start | bytes 405504
  406.8 331.0 %reduce-scatter.12.cloned.1.call-start = ((), (), s32[]{:S(2)}) async-start(), calls=%async_computation.11 | async-start | bytes 2433024 | tf_op jit(solution)/shard_map/reduce_scatter | solution.py:276
  413.6 428.5 %reduce-scatter.14.cloned.1.call-start = ((), (), s32[]{:S(2)}) async-start(), calls=%async_computation.12 | async-start | bytes 2433024 | tf_op jit(solution)/shard_map/reduce_scatter | solution.py:278
  417.4 565.0 %reduce-scatter.16.cloned.1.call-start = ((), (), s32[]{:S(2)}) async-start(), calls=%async_computation.13 | async-start | bytes 9732096 | tf_op jit(solution)/shard_map/reduce_scatter | solution.py:279
  552.0 571.9 %reduce-scatter.18.cloned.1.call-start = ((), (), s32[]{:S(2)}) async-start(), calls=%async_computation.14 | async-start | bytes 9732096 | tf_op jit(solution)/shard_map/reduce_scatter | solution.py:280
  893.3 233.5 %copy-start.10 = (bf16[256,768]{1,0:T(8,128)(2,1)S(1)}, bf16[256,768]{1,0:T(8,128)(2,1)}, u32[]{:S(2)}) copy-start(bf16[256,768]{1,0:T(8,128)(2,1)} %copy-done.9) | copy-start | bytes 1179652
  893.3 233.5 %copy-start.16 = (bf16[768,768]{1,0:T(8,128)(2,1)S(1)}, bf16[768,768]{1,0:T(8,128)(2,1)}, u32[]{:S(2)}) copy-start(bf16[768,768]{1,0:T(8,128)(2,1)} %all-gather.8.cloned.1.call-done) | copy-start | bytes 3538948
  898.0 273.4 %copy-start.41 = (f32[11,24]{1,0:T(8,128)S(1)}, f32[11,24]{1,0:T(8,128)}, u32[]{:S(2)}) copy-start(f32[11,24]{1,0:T(8,128)} %param.38) | copy-start | bytes 3172
  898.0 273.4 %copy-start.48 = (f32[11,24]{1,0:T(8,128)S(1)}, f32[11,24]{1,0:T(8,128)}, u32[]{:S(2)}) copy-start(f32[11,24]{1,0:T(8,128)} %param.45) | copy-start | bytes 3172
  898.0 276.7 %copy-start.26 = (f32[24,768]{1,0:T(8,128)S(1)}, f32[24,768]{1,0:T(8,128)}, u32[]{:S(2)}) copy-start(f32[24,768]{1,0:T(8,128)} %param.33) | copy-start | bytes 221188
  898.0 278.4 %copy-start.36 = (f32[24,128]{1,0:T(8,128)S(1)}, f32[24,128]{1,0:T(8,128)}, u32[]{:S(2)}) copy-start(f32[24,128]{1,0:T(8,128)} %param.34) | copy-start | bytes 36868
  898.0 278.4 %copy-start.37 = (f32[24,128]{1,0:T(8,128)S(1)}, f32[24,128]{1,0:T(8,128)}, u32[]{:S(2)}) copy-start(f32[24,128]{1,0:T(8,128)} %reduce-scatter.20.cloned.1.call-done) | copy-start | bytes 36868
  898.0 281.4 %copy-start.12 = (f32[24,3072]{1,0:T(8,128)S(1)}, f32[24,3072]{1,0:T(8,128)}, u32[]{:S(2)}) copy-start(f32[24,3072]{1,0:T(8,128)} %param.36) | copy-start | bytes 884740
  898.1 281.4 %copy-start.23 = (f32[24,3072]{1,0:T(8,128)S(1)}, f32[24,3072]{1,0:T(8,128)}, u32[]{:S(2)}) copy-start(f32[24,3072]{1,0:T(8,128)} %param.43) | copy-start | bytes 884740
  982.4 197.1 %copy-start.14 = (f32[24,3072]{1,0:T(8,128)S(1)}, f32[24,3072]{1,0:T(8,128)}, u32[]{:S(2)}) copy-start(f32[24,3072]{1,0:T(8,128)} %reduce-scatter.16.cloned.1.call-done) | copy-start | bytes 884740
  (42 other events, 1097.3 us)
Sparse Core Ops, SparseCore 0:
  11.5 56.8 all-gather.5
  71.9 53.0 all-gather.7
  343.0 58.8 reduce-scatter.9
  405.7 62.6 all-gather.9
  472.2 62.4 all-gather.11
  540.8 93.5 reduce-scatter.19
  639.7 98.0 reduce-scatter.11
  744.0 98.0 reduce-scatter.13
  848.0 134.3 reduce-scatter.15
  989.1 134.6 reduce-scatter.17
where the time goes:
time: 1200 us; the launch traced here: 1190 us
  waiting for transfers between devices  660 us (55%)
  blocking collectives  266 us (22%)
  matrix products  134 us (11%)
  other arithmetic  64.9 us (5%)
  local copies, waits for them, and re-layouts  41 us (3%)
  between operations  23.2 us (2%)
    reduce_scatter x1, waiting for transfers between devices, body(): lax.psum_scatter(grad_down, ('fsdp', 'seq'), scatter_dimension=0, tiled=T...  139 us
    reduce_scatter x1, waiting for transfers between devices, body(): lax.psum_scatter(grad_query, ('fsdp', 'seq'), scatter_dimension=0, tiled=...  102 us
    reduce_scatter x1, waiting for transfers between devices, body(): lax.psum_scatter(grad_output, ('fsdp', 'seq'), scatter_dimension=0, tiled...  101 us
    reduce_scatter x1, waiting for transfers between devices, body(): lax.psum_scatter(grad_up, ('fsdp', 'seq'), scatter_dimension=0, tiled=True)  84.3 us
    all_gather x1, blocking collectives, body(): lax.all_gather(vectors.astype(jnp.bfloat16), ('fsdp', 'seq'), axis=1, til...  70.7 us
    unnamed x11, waiting for transfers between devices  69.8 us
    all_gather x1, blocking collectives, body(): lax.all_gather(keyval_weight.astype(jnp.bfloat16), ('fsdp', 'seq'), axis=...  64.6 us
    dot_general x17, matrix products, against(): lax.dot_general(left_side, right_side, (((1,), (1,)), ((), ())), preferre...  61.6 us
  transfers between devices with their start and end apart: 10, of which 8 were waited for; matrix products, arithmetic and copies ran while one was open for 13% of the time, Pallas kernels for 0%

commit v1 on v0

--- a/solution.py
+++ b/solution.py
@@ -3,6 +3,8 @@
 import jax
 import jax.numpy as jnp
 from jax import lax
+from jax.experimental import pallas as pl
+from jax.experimental.pallas import tpu as pltpu
 from jax.sharding import PartitionSpec as P
 
 D = 768
@@ -12,6 +14,8 @@
 FF = 3072
 KEY_BLOCK = 512
 STEP = 10
+F32 = jnp.float32
+BF16 = jnp.bfloat16
 
 
 NORM_EPS = 1e-05
@@ -345,9 +349,796 @@
     )
 
 
+def dot_nn(left, right):
+    return lax.dot_general(left, right, (((1,), (0,)), ((), ())), preferred_element_type=F32)
+
+
+def dot_nt(left, right):
+    return lax.dot_general(left, right, (((1,), (1,)), ((), ())), preferred_element_type=F32)
+
+
+def dot_tn(left, right):
+    return lax.dot_general(left, right, (((0,), (0,)), ((), ())), preferred_element_type=F32)
+
+
+def normalise(rows):
+    centre = rows - jnp.mean(rows, -1, keepdims=True)
+    scale = lax.rsqrt(jnp.mean(centre * centre, -1, keepdims=True) + NORM_EPS)
+    return centre * scale, scale
+
+
+def norm_back(grad, hat, scale, gain):
+    inner = grad * gain
+    return scale * (
+        inner
+        - jnp.mean(inner, -1, keepdims=True)
+        - hat * jnp.mean(inner * hat, -1, keepdims=True)
+    )
+
+
+class Copies:
+    def __init__(self, send_sems, recv_sems):
+        self.send_sems, self.recv_sems, self.all = send_sems, recv_sems, []
+
+    def make(self, source, target, device):
+        index = len(self.all)
+        copy = pltpu.make_async_remote_copy(
+            src_ref=source,
+            dst_ref=target,
+            send_sem=self.send_sems.at[index],
+            recv_sem=self.recv_sems.at[index],
+            device_id=device,
+            device_id_type=pl.DeviceIdType.MESH,
+        )
+        self.all.append(copy)
+        return copy
+
+
+def slab_rows(block, index):
+    return pl.ds(pl.multiple_of((block * 8 + index) * 24, 8), 24)
+
+
+class Panels:
+    def __init__(self, ref, height):
+        self.ref, self.height, self.count = ref, height, ref.shape[0] // height
+
+    def rows(self, panel, block, index):
+        return pl.ds(pl.multiple_of(panel * self.height + (block * 8 + index) * 24, 8), 24)
+
+    def get(self, block, index):
+        parts = [self.ref[self.rows(p, block, index), :] for p in range(self.count)]
+        return parts[0] if self.count == 1 else jnp.concatenate(parts, 1)
+
+    def put(self, block, index, value):
+        for p in range(self.count):
+            self.ref[self.rows(p, block, index), :] = value[:, p * 256 : p * 256 + 256]
+
+
+N_COPIES = 130
+QO = 1536
+AW = 1664
+
+
+def layer_kernel(
+    span, x, cot, qw, kw, ow, uw, dw, vec, kvb,
+    bo, ig, g_qo, g_vp, g_up, g_dn, g_small,
+    A, U, Dn, VT, X, C, KV, ub, WA, WU, gains, vsq,
+    n1, hat1, scale1, N2, act, dl, OP, NP,
+    qz, doz, doT, kvT, bias, sbuf, mixT, dqT, dkv,
+    GP, GU, GD, vg,
+    SK1, RK1, SK2, RK2,
+    RO1, SO2, RO2, RN1, SN2, RN2,
+    SQ1, RQ1, SQ2, RQ2, SQ3, RQ3, SQ4, RQ4,
+    SP1, RP1, SP2, RP2, SP3, RP3, SP4, RP4,
+    SU1, RU1, SU2, RU2, SU3, RU3,
+    SD1, RD1, SD2, RD2,
+    NS1, NS2,
+    send_sems, recv_sems,
+):
+    tok = x.shape[0]
+    f = lax.axis_index("fsdp")
+    s = lax.axis_index("seq")
+    z = lax.div(s, 2)
+    y = lax.rem(s, 2)
+    yo = 1 - y
+    fc = f + 1 - 2 * lax.rem(f, 2)
+    fx = lax.rem(f + 2, 4)
+    fd = 3 - f
+    zk = (z, z + 1 - 2 * lax.rem(z, 2), lax.rem(z + 2, 4), 3 - z)
+    dev_c, dev_x, dev_d = (fc, s), (fx, s), (fd, s)
+    dev_y = (f, z * 2 + yo)
+    dev_z = tuple((f, zz * 2 + y) for zz in zk)
+    dev_zy = tuple((f, zz * 2 + yo) for zz in zk)
+    fsdp_devs = (dev_c, dev_x, dev_d)
+    seq_devs = dev_z[1:] + dev_zy
+
+    copies = Copies(send_sems, recv_sems)
+    make = copies.make
+
+    def seq_gather(ref):
+        to_z = [None] + [make(ref(z, y), ref(z, y), dev_z[k]) for k in (1, 2, 3)]
+        to_y = [make(ref(zk[k], y), ref(zk[k], y), dev_y) for k in range(4)]
+        return to_z, to_y
+
+    a_z, a_y = seq_gather(lambda i, j: A.at[f, i, j])
+    v_z, v_y = seq_gather(lambda i, j: VT.at[f, i, j])
+    u_z, u_y = seq_gather(lambda i, j: U.at[i, j])
+    d_z, d_y = seq_gather(lambda i, j: Dn.at[i, j])
+    k_z, k_y = seq_gather(lambda i, j: KV.at[i, j])
+
+    def fsdp_gather(ref):
+        to_x = [make(ref(f, j), ref(f, j), dev_x) for j in (y, yo)]
+        to_c = [make(ref(f, j), ref(f, j), dev_c) for j in (y, yo)]
+        on_c = [make(ref(fx, j), ref(fx, j), dev_c) for j in (y, yo)]
+        return to_x, to_c, on_c
+
+    a_x, a_c, a_xc = fsdp_gather(lambda i, j: A.at[i, :, j])
+    v_x, v_c, v_xc = fsdp_gather(lambda i, j: VT.at[i, :, j])
+
+    def token_gather(ref):
+        return (
+            make(ref.at[f], ref.at[f], dev_x),
+            make(ref.at[f], ref.at[f], dev_c),
+            make(ref.at[fx], ref.at[fx], dev_c),
+        )
+
+    x_x, x_c, x_xc = token_gather(X)
+    c_x, c_c, c_xc = token_gather(C)
+    u_f = [make(ub.at[g], U.at[z, y, f], dev) for g, dev in zip((fc, fx, fd), fsdp_devs)]
+
+    rk1 = make(SK1, RK1, dev_y)
+    rk2 = [make(SK2.at[k], RK2.at[k], dev_z[k + 1]) for k in range(3)]
+    out_c = [make(OP.at[g], RO1.at[i], dev_c) for i, g in enumerate((fc, fd))]
+    out_x = make(SO2, RO2, dev_x)
+    nrm_c = [make(NP.at[g], RN1.at[i], dev_c) for i, g in enumerate((fc, fd))]
+    nrm_x = make(SN2, RN2, dev_x)
+
+    def full_scatter(S1, R1, S2, R2, S3, R3, S4, R4):
+        return (
+            make(S1, R1, dev_c),
+            make(S2, R2, dev_x),
+            make(S3, R3, dev_y),
+            [make(S4.at[k], R4.at[k], dev_z[k + 1]) for k in range(3)],
+        )
+
+    q_sc = full_scatter(SQ1, RQ1, SQ2, RQ2, SQ3, RQ3, SQ4, RQ4)
+    p_sc = full_scatter(SP1, RP1, SP2, RP2, SP3, RP3, SP4, RP4)
+    su_y = [make(SU1.at[zz], RU1.at[zz], dev_y) for zz in zk]
+    su_z = [make(SU2.at[k], RU2.at[k], dev_z[k + 1]) for k in range(3)]
+    su_f = [make(SU3.at[g], RU3.at[i], dev) for i, (g, dev) in enumerate(zip((fc, fx, fd), fsdp_devs))]
+    sd_y = [make(SD1.at[zz], RD1.at[zz], dev_y) for zz in zk]
+    sd_z = [make(SD2.at[k], RD2.at[k], dev_z[k + 1]) for k in range(3)]
+    n_f = [make(NS1.at[f], NS1.at[f], dev) for dev in fsdp_devs]
+    n_s = [make(NS2.at[s], NS2.at[s], dev) for dev in seq_devs]
+
+    barrier = pltpu.get_barrier_semaphore()
+    for dev in fsdp_devs + seq_devs:
+        pl.semaphore_signal(barrier, inc=1, device_id=dev, device_id_type=pl.DeviceIdType.MESH)
+
+    for j in range(4):
+        ub[j] = uw[:, j * D : (j + 1) * D].astype(BF16)
+    U[z, y, f] = ub[f]
+    Dn[z, y] = dw[...].astype(BF16)
+    A[f, z, y, :, :D] = qw[...].astype(BF16)
+    A[f, z, y, :, D : D + 128] = kw[...].astype(BF16)
+    A[f, z, y, :, D + 128 :] = ow[...].astype(BF16)
+    vsq[...] = jnp.zeros((128, 128), F32)
+    vsq[0:11, 0:24] = vec[...]
+    vsq[11:12, 0:16] = kvb[...]
+    VT[f, z, y] = vsq[...].astype(BF16).astype(F32).T[:24, :]
+    X[f] = x[...]
+    C[f] = cot[...]
+
+    pl.semaphore_wait(barrier, 10)
+
+    for copy in u_f:
+        copy.start()
+    for k in (1, 2, 3):
+        v_z[k].start()
+    v_y[0].start()
+    for copy in (x_x, c_x, x_c, c_c):
+        copy.start()
+    for k in (1, 2, 3):
+        d_z[k].start()
+    d_y[0].start()
+    for copy in u_f:
+        copy.wait_recv()
+    for k in (1, 2, 3):
+        u_z[k].start()
+    u_y[0].start()
+    for k in (1, 2, 3):
+        v_z[k].wait_recv()
+        v_y[k].start()
+    v_x[0].start()
+    v_c[0].start()
+    for k in (1, 2, 3):
+        a_z[k].start()
+    a_y[0].start()
+    for k in range(4):
+        v_y[k].wait_recv()
+    v_x[1].start()
+    v_c[1].start()
+    for j in range(2):
+        v_x[j].wait_recv()
+        v_xc[j].start()
+    for k in (1, 2, 3):
+        d_z[k].wait_recv()
+        d_y[k].start()
+    x_x.wait_recv()
+    x_xc.start()
+    for k in (1, 2, 3):
+        u_z[k].wait_recv()
+        u_y[k].start()
+    c_x.wait_recv()
+    c_xc.start()
+    for k in (1, 2, 3):
+        a_z[k].wait_recv()
+        a_y[k].start()
+    a_x[0].start()
+    a_c[0].start()
+    for j in range(2):
+        v_c[j].wait_recv()
+        v_xc[j].wait_recv()
+
+    gains[...] = VT.reshape(D, 128)[...].T
+    vsq[...] = jnp.concatenate([VT[0, i // 2, i % 2][:16] for i in range(8)], 0).T
+    kv_shift = vsq[11:12, :]
+    hat, scale = normalise(x[...].astype(F32))
+    hat1[...] = hat
+    scale1[...] = jnp.broadcast_to(scale, (tok, 128))
+    n1[...] = (hat * gains[0:1, :] + gains[1:2, :]).astype(BF16)
+    vg[...] = jnp.zeros((128, D), F32)
+    csum = jnp.sum(cot[...].astype(F32), 0, keepdims=True)
+    vg[5:6, :] = csum
+    vg[6:7, :] = csum
+
+    for k in range(4):
+        d_y[k].wait_recv()
+    for k in range(4):
+        u_y[k].wait_recv()
+    for copy in (x_c, x_xc, c_c, c_xc):
+        copy.wait_recv()
+
+    for g in range(4):
+        for i in range(4):
+            pair = jnp.concatenate([U[i, j, g].astype(F32) for j in range(2)], 0)
+            WU[(g * 4 + i) * 48 : (g * 4 + i + 1) * 48, :] = pair.astype(BF16)
+    WD = Dn.reshape(D, D)
+    up_bias = gains[pl.ds(7 + f, 1), :]
+    vg[pl.ds(7 + f, 1), :] = jnp.zeros((1, D), F32)
+
+    def token_block(t, carry):
+        two_gain, two_shift, up_sum = carry
+        rows = pl.ds(pl.multiple_of(t * tok, tok), tok)
+        hat2, _ = normalise(X[t].astype(F32))
+        low2 = (hat2 * gains[2:3, :] + gains[3:4, :]).astype(BF16)
+        N2[rows, :] = low2
+        back = C[t]
+        sums = []
+        for c in range(3):
+            units = slice(c * 256, c * 256 + 256)
+            lifted = dot_nn(low2, WU[:, units]) + up_bias[:, units]
+            active_grad = dot_nt(back, WD[units, :])
+            half = 0.5 + 0.5 * lax.erf(lifted * (0.5**0.5))
+            act[rows, units] = (lifted * half).astype(BF16)
+            bell = jnp.exp(lifted * lifted * -0.5) * (1.0 / math.sqrt(2.0 * math.pi))
+            low = ((half + lifted * bell) * active_grad).astype(BF16)
+            dl[rows, units] = low
+            sums.append(jnp.sum(low.astype(F32), 0, keepdims=True))
+        OP[t] = dot_nn(act[rows, :], WD[...]).astype(BF16)
+        grad2 = dot_nt(dl[rows, :], WU[...])
+        NP[t] = grad2.astype(BF16)
+        return (
+            two_gain + jnp.sum(grad2 * hat2, 0, keepdims=True),
+            two_shift + jnp.sum(grad2, 0, keepdims=True),
+            up_sum + jnp.concatenate(sums, 1),
+        )
+
+    zero_row = jnp.zeros((1, D), F32)
+    two_gain, two_shift, up_sum = lax.fori_loop(0, 4, token_block, (zero_row,) * 3)
+    vg[2:3, :] = two_gain
+    vg[3:4, :] = two_shift
+    vg[pl.ds(7 + f, 1), :] = up_sum
+    for copy in out_c + nrm_c:
+        copy.start()
+
+    for k in range(4):
+        a_y[k].wait_recv()
+    a_x[1].start()
+    a_c[1].start()
+
+    CF = C.reshape(4 * tok, D)
+    for c in range(3):
+        units = slice(c * 256, c * 256 + 256)
+        GD[units, :] = dot_tn(act[:, units], CF[...])
+    for k in (1, 2, 3, 0):
+        for i in range(1):
+            SD1[zk[k]] = GD[pl.ds(pl.multiple_of((zk[k] * 2 + yo) * 96, 8), 96), :].astype(BF16)
+        sd_y[k].start()
+    a_x[0].wait_recv()
+    a_xc[0].start()
+    for c in range(3):
+        units = slice(c * 256, c * 256 + 256)
+        GU[units, :] = dot_tn(N2[:, units], dl[...])
+    for k in (1, 2, 3, 0):
+        for g in range(4):
+            SU1[zk[k], g] = GU[slab_rows(g, zk[k] * 2 + yo), :].astype(BF16)
+        su_y[k].start()
+    a_x[1].wait_recv()
+    a_xc[1].start()
+    for j in range(2):
+        a_c[j].wait_recv()
+        a_xc[j].wait_recv()
+
+    def join(i, carry):
+        g = lax.div(i, 4)
+        zz = lax.rem(i, 4)
+        pair = jnp.concatenate([A[g, zz, 0].astype(F32), A[g, zz, 1].astype(F32)], 0)
+        WA[pl.ds(pl.multiple_of(i * 48, 16), 48), :] = pair.astype(BF16)
+        return carry
+
+    lax.fori_loop(0, 16, join, 0)
+    own_span = span[0, s]
+    lane = lax.broadcasted_iota(jnp.int32, (tok, 128), 1)
+    spot = lax.broadcasted_iota(jnp.int32, (tok, 128), 0) + own_span * tok
+    in_head = lax.rem(lane, 64)
+    step = lax.rem(in_head, ROT_DIMS // 2).astype(F32)
+    inverse = jnp.exp(step * (-2.0 * math.log(10000.0) / ROT_DIMS))
+    angle = spot.astype(F32) * (0.25 * inverse)
+    sine = jnp.sin(angle)
+    cosine = jnp.where(in_head < ROT_DIMS, jnp.cos(angle), 1.0)
+    sine_low = jnp.where(in_head < ROT_DIMS // 2, sine, 0.0)
+    sine_high = jnp.where((in_head >= ROT_DIMS // 2) & (in_head < ROT_DIMS), sine, 0.0)
+    key_lane = lane < 64
+    key_cos = jnp.where(key_lane, cosine, 1.0)
+    key_low = jnp.where(key_lane, sine_low, 0.0)
+    key_high = jnp.where(key_lane, sine_high, 0.0)
+
+    def turn(block, cos_t, low_t, high_t):
+        up = pltpu.roll(block, 120, 1)
+        down = pltpu.roll(block, 8, 1)
+        return block * cos_t - up * low_t + down * high_t
+
+    def turn_back(block, cos_t, low_t, high_t):
+        up = pltpu.roll(block, 120, 1)
+        down = pltpu.roll(block, 8, 1)
+        return block * cos_t + up * low_t - down * high_t
+
+    kv_pre = dot_nn(n1[...], WA[:, D : D + 128]) + kv_shift
+    KV[z, y] = turn(kv_pre, key_cos, key_low, key_high).astype(BF16)
+    for k in (1, 2, 3):
+        k_z[k].start()
+    k_y[0].start()
+
+    q_pre = dot_nn(n1[...], WA[:, :D]) + gains[4:5, :]
+    gap = jnp.zeros((tok, 64), BF16)
+    for j in range(6):
+        cols = slice(j * 128, j * 128 + 128)
+        turned = turn(q_pre[:, cols], cosine, sine_low, sine_high).astype(BF16).astype(F32)
+        turned = (turned * HD ** (-0.5)).astype(BF16)
+        qz[2 * j] = jnp.concatenate([turned[:, :64], gap], 1)
+        qz[2 * j + 1] = jnp.concatenate([turned[:, 64:], gap], 1)
+    for k in (1, 2, 3):
+        k_z[k].wait_recv()
+        k_y[k].start()
+    mixed_back = dot_nt(cot[...], WA[:, D + 128 :]).astype(BF16)
+    for j in range(6):
+        pair = mixed_back[:, j * 128 : j * 128 + 128]
+        doz[2 * j] = jnp.concatenate([gap, pair[:, :64]], 1)
+        doz[2 * j + 1] = jnp.concatenate([gap, pair[:, 64:]], 1)
+    doT[...] = mixed_back.astype(F32).T.astype(BF16).reshape(HQ, HD, tok)
+    key_iota = lax.broadcasted_iota(jnp.int32, (tok, tok), 0)
+    row_iota = lax.broadcasted_iota(jnp.int32, (tok, tok), 1) + own_span * tok
+    for i in range(8):
+        bias[i * tok : (i + 1) * tok, :] = jnp.where(
+            key_iota + span[0, i] * tok <= row_iota, 0.0, MASKED
+        ).astype(F32)
+    dkv[...] = jnp.zeros((8 * tok, 128), F32)
+    for k in range(4):
+        k_y[k].wait_recv()
+    KVF = KV.reshape(8 * tok, 128)
+    kvT[...] = KVF[...].astype(F32).T.astype(BF16)
+
+    def scatter_step(k):
+        su_y[k].wait_recv()
+        sd_y[k].wait_recv()
+        own = zk[k]
+        rows = pl.ds(pl.multiple_of((own * 2 + y) * 96, 8), 96)
+        total = GD[rows, :] + RD1[own].astype(F32)
+        if k:
+            SD2[k - 1] = total.astype(BF16)
+            sd_z[k - 1].start()
+        else:
+            GD[rows, :] = total
+        for g in range(4):
+            rows = slab_rows(g, own * 2 + y)
+            total = GU[rows, :] + RU1[own, g].astype(F32)
+            if k:
+                SU2[k - 1, g] = total.astype(BF16)
+            else:
+                GU[rows, :] = total
+        if k:
+            su_z[k - 1].start()
+
+    def tokens_to_x():
+        for copy in out_c + nrm_c:
+            copy.wait_recv()
+        SO2[...] = (OP[fx].astype(F32) + RO1[1].astype(F32)).astype(BF16)
+        out_x.start()
+        SN2[...] = (NP[fx].astype(F32) + RN1[1].astype(F32)).astype(BF16)
+        nrm_x.start()
+
+    def attend(step_index, carry):
+        @pl.when(step_index == 0)
+        def _():
+            tokens_to_x()
+
+        for k, at in ((1, 1), (2, 2), (3, 3), (0, 4)):
+
+            @pl.when(step_index == at)
+            def _():
+                scatter_step(k)
+
+        heads = [step_index * 2, step_index * 2 + 1]
+        tops, shares, deltas = [], [], []
+        for j, h in enumerate(heads):
+            top = jnp.full((8, tok), MASKED, F32)
+            for i in range(8):
+                rows = pl.ds(i * tok, tok)
+                held = pl.ds((j * 8 + i) * tok, tok)
+                scores = dot_nt(KVF[rows, :], qz[h]) + bias[rows, :]
+                sbuf[held, :] = scores
+                top = jnp.maximum(top, jnp.max(scores.reshape(tok // 8, 8, tok), axis=0))
+            tops.append(jnp.max(top, axis=0, keepdims=True))
+        for j, h in enumerate(heads):
+            total = jnp.zeros((8, tok), F32)
+            for i in range(8):
+                held = pl.ds((j * 8 + i) * tok, tok)
+                weights = jnp.exp(sbuf[held, :] - tops[j])
+                sbuf[held, :] = weights
+                total = total + jnp.sum(weights.reshape(tok // 8, 8, tok), axis=0)
+            shares.append(1.0 / jnp.sum(total, axis=0, keepdims=True))
+        for j, h in enumerate(heads):
+            acc = jnp.zeros((128, tok), F32)
+            for i in range(8):
+                rows = pl.ds(i * tok, tok)
+                held = pl.ds((j * 8 + i) * tok, tok)
+                probs = sbuf[held, :] * shares[j]
+                probs_low = probs.astype(BF16)
+                sbuf[held, :] = probs
+                acc = acc + dot_nn(kvT[:, rows], probs_low)
+                dkv[rows, :] += dot_nn(probs_low, doz[h])
+            mixed = acc[64:, :]
+            mixT[h] = mixed.astype(BF16)
+            deltas.append(jnp.sum(mixed * doT[h].astype(F32), axis=0, keepdims=True))
+        for j, h in enumerate(heads):
+            acc = jnp.zeros((128, tok), F32)
+            for i in range(8):
+                rows = pl.ds(i * tok, tok)
+                held = pl.ds((j * 8 + i) * tok, tok)
+                prob_grad = dot_nt(KVF[rows, :], doz[h])
+                score_low = (sbuf[held, :] * (prob_grad - deltas[j])).astype(BF16)
+                acc = acc + dot_nn(kvT[:, rows], score_low)
+                dkv[rows, :] += dot_nn(score_low, qz[h])
+            dqT[h] = acc[:64, :] * HD ** (-0.5)
+        return carry
+
+    lax.fori_loop(0, HQ // 2, attend, 0)
+
+    for zz in range(4):
+        SK1[zz] = dkv[pl.ds(pl.multiple_of((2 * zz + yo) * tok, 8), tok), :].astype(BF16)
+    rk1.start()
+    mix_low = mixT.reshape(D, tok)[...]
+    for c in range(3):
+        sbuf[(3 + c) * D : (4 + c) * D, :] = dot_nn(mix_low, cot[:, c * 256 : c * 256 + 256])
+    q_back = dqT.reshape(D, tok)[...].T
+    parts = []
+    for j in range(6):
+        parts.append(
+            turn_back(q_back[:, j * 128 : j * 128 + 128], cosine, sine_low, sine_high).astype(BF16)
+        )
+    q_low = jnp.concatenate(parts, 1)
+    vg[4:5, :] = jnp.sum(q_low.astype(F32), 0, keepdims=True)
+    for c in range(3):
+        sbuf[c * D : (c + 1) * D, :] = dot_tn(n1[...], q_low[:, c * 256 : c * 256 + 256])
+    GQ = Panels(sbuf, D)
+    GPP = Panels(GP, D)
+
+    def scatter_c(G, S1, copy):
+        def put(i, carry):
+            for j, g in enumerate((fc, fd)):
+                S1[j, i] = G.get(g, i).astype(S1.dtype)
+            return carry
+
+        lax.fori_loop(0, 8, put, 0)
+        copy.start()
+
+    def scatter_x(G, R1, S2, copies_):
+        copies_[0].wait_recv()
+
+        def put(i, carry):
+            S2[i] = (G.get(fx, i) + R1[1, i].astype(F32)).astype(S2.dtype)
+            G.put(f, i, G.get(f, i) + R1[0, i].astype(F32))
+            return carry
+
+        lax.fori_loop(0, 8, put, 0)
+        copies_[1].start()
+
+    def scatter_y(G, R2, S3, copies_):
+        copies_[1].wait_recv()
+
+        def put(i, carry):
+            S3[i] = (G.get(f, 2 * i + yo) + R2[2 * i + yo].astype(F32)).astype(S3.dtype)
+            G.put(f, 2 * i + y, G.get(f, 2 * i + y) + R2[2 * i + y].astype(F32))
+            return carry
+
+        lax.fori_loop(0, 4, put, 0)
+        copies_[2].start()
+
+    def scatter_z(G, R3, S4, copies_):
+        copies_[2].wait_recv()
+        for k in (1, 2, 3):
+            total = G.get(f, 2 * zk[k] + y) + R3[zk[k]].astype(F32)
+            S4[k - 1] = total.astype(S4.dtype)
+            copies_[3][k - 1].start()
+
+    def scatter_end(G, R3, R4, copies_):
+        total = G.get(f, 2 * z + y) + R3[z].astype(F32)
+        for k in range(3):
+            copies_[3][k].wait_recv()
+            total = total + R4[k].astype(F32)
+        return total
+
+    scatter_c(GQ, SQ1, q_sc[0])
+    rk1.wait_recv()
+    for k in (1, 2, 3):
+        rows = pl.ds(pl.multiple_of((2 * zk[k] + y) * tok, 8), tok)
+        SK2[k - 1] = (dkv[rows, :] + RK1[zk[k]].astype(F32)).astype(BF16)
+        rk2[k - 1].start()
+    grad1 = dot_nt(q_low, WA[:, :D])
+    scatter_x(GQ, RQ1, SQ2, q_sc)
+    kv_back = dkv[pl.ds(pl.multiple_of((2 * z + y) * tok, 8), tok), :] + RK1[z].astype(F32)
+    for k in range(3):
+        rk2[k].wait_recv()
+        kv_back = kv_back + RK2[k].astype(F32)
+    kv_low = turn_back(kv_back, key_cos, key_low, key_high).astype(BF16)
+    grad1 = grad1 + dot_nt(kv_low, WA[:, D : D + 128])
+    vg[0:1, :] = jnp.sum(grad1 * hat1[...], 0, keepdims=True)
+    vg[1:2, :] = jnp.sum(grad1, 0, keepdims=True)
+    kv_sum = jnp.sum(kv_low.astype(F32), 0, keepdims=True)
+    short = jnp.zeros((1, 8), F32)
+    spread = jnp.concatenate(
+        [part for i in range(8) for part in (kv_sum[:, i * 16 : i * 16 + 16], short)], 1
+    )
+    vg[11:12, :] = jnp.concatenate([spread] * 4, 1)
+    GP[:, :128] = dot_tn(n1[...], kv_low)
+    GP[:, 128:] = vg[...].T
+    scatter_c(GPP, SP1, p_sc[0])
+
+    rows = pl.ds(pl.multiple_of(s * 96, 8), 96)
+    down_grad = GD[rows, :]
+    for k in range(3):
+        sd_z[k].wait_recv()
+        down_grad = down_grad + RD2[k].astype(F32)
+    g_dn[...] = down_grad
+    for k in range(3):
+        su_z[k].wait_recv()
+    for g in range(4):
+        total = GU[slab_rows(g, s), :]
+        for k in range(3):
+            total = total + RU2[k, g].astype(F32)
+        g_up[g] = total
+        SU3[g] = total.astype(BF16)
+    for copy in su_f:
+        copy.start()
+    scatter_x(GPP, RP1, SP2, p_sc)
+    scatter_y(GQ, RQ2, SQ3, q_sc)
+
+    mixed_rows = mix_low.astype(F32).T.astype(BF16)
+    out_x.wait_recv()
+    bo[...] = (
+        x[...].astype(F32)
+        + (dot_nn(mixed_rows, WA[:, D + 128 :]) + gains[5:6, :])
+        + (OP[f].astype(F32) + RO1[0].astype(F32) + RO2[...].astype(F32) + gains[6:7, :])
+    ).astype(BF16)
+    scatter_y(GPP, RP2, SP3, p_sc)
+    scatter_z(GQ, RQ3, SQ4, q_sc)
+    nrm_x.wait_recv()
+    grad2 = NP[f].astype(F32) + RN1[0].astype(F32) + RN2[...].astype(F32)
+    hat_rows = hat1[...]
+    scale_rows = scale1[:, 0:1]
+    ig[...] = (
+        cot[...].astype(F32)
+        + norm_back(grad1, hat_rows, scale_rows, gains[0:1, :])
+        + norm_back(grad2, hat_rows, scale_rows, gains[2:3, :])
+    )
+    scatter_z(GPP, RP3, SP4, p_sc)
+    for i, g in enumerate((fc, fx, fd)):
+        su_f[i].wait_recv()
+        g_up[g] = RU3[i].astype(F32)
+    qo_grad = scatter_end(GQ, RQ3, RQ4, q_sc)
+    g_qo[...] = qo_grad
+    vp_grad = scatter_end(GPP, RP3, RP4, p_sc)
+    g_vp[...] = vp_grad
+
+    def fold(values):
+        return jnp.sum(jnp.sum(values * values, 0, keepdims=True), 1, keepdims=True)
+
+    lanes = lax.broadcasted_iota(jnp.int32, (24, 256), 1)
+    squares = fold(qo_grad) + fold(jnp.where(lanes == 128 + 11, 0.0, vp_grad)) + fold(g_dn[...])
+    for g in range(4):
+        squares = squares + fold(g_up[g])
+    kv_rows = jnp.concatenate([vp_grad[:, 128:], jnp.zeros((104, 128), F32)], 0).T
+    line = lax.broadcasted_iota(jnp.int32, (8, 128), 0)
+    column = lax.broadcasted_iota(jnp.int32, (8, 128), 1)
+    kv_line = jnp.where(column < 16, jnp.broadcast_to(kv_rows[11:12, :], (8, 128)), 0.0)
+    NS1[f] = jnp.where(line == 0, squares, kv_line)
+    for copy in n_f:
+        copy.start()
+    for copy in n_f:
+        copy.wait_recv()
+    kv_piece = NS1[0][1:2, :]
+    chip = NS1[0] + NS1[1] + NS1[2] + NS1[3]
+    part = chip[0:1, 0:1] + jnp.sum(kv_piece * kv_piece, 1, keepdims=True)
+    NS2[s] = jnp.broadcast_to(part, (8, 128))
+    for copy in n_s:
+        copy.start()
+    for copy in n_s:
+        copy.wait_recv()
+    everything = NS2[0]
+    for i in range(1, 8):
+        everything = everything + NS2[i]
+    g_small[...] = jnp.where(line == 0, everything, jnp.broadcast_to(kv_piece, (8, 128)))
+    for copy in copies.all:
+        copy.wait_send()
+
+
+def update_kernel(
+    small, g_qo, g_vp, g_up, g_dn, bo_in, ig_in,
+    mq, mk, mo, mu, md, mv, mb,
+    fq, fk, fo, fu, fdn, fv, fb,
+    sq, sk, so, su, sd, sv, sb,
+    bo, ig, norm,
+    nmq, nmk, nmo, nmu, nmd, nmv, nmb,
+    nfq, nfk, nfo, nfu, nfd, nfv, nfb,
+    nsq, nsk, nso, nsu, nsd, nsv, nsb,
+    residual,
+):
+    bo[...] = bo_in[...]
+    ig[...] = ig_in[...]
+    size = jnp.sqrt(small[0:1, 0:1])
+    norm[...] = size
+    factor = jnp.minimum(1.0, CLIP_NORM / (size + 1e-06))
+
+    def update(grad, master, first, second, new_master, new_first, new_second, rate, decay):
+        clipped = grad * factor
+        values = adamw(master, clipped, first, second, rate, decay)
+        for ref, value in zip((new_master, new_first, new_second), values):
+            ref[...] = value
+
+    rates = (MATRIX_RATE, MATRIX_DECAY)
+    update(g_qo[:, :D], mq[...], fq[...], sq[...], nmq, nfq, nsq, *rates)
+    update(g_qo[:, D:], mo[...], fo[...], so[...], nmo, nfo, nso, *rates)
+    update(g_vp[:, :128], mk[...], fk[...], sk[...], nmk, nfk, nsk, *rates)
+    for g in range(4):
+        cols = slice(g * D, (g + 1) * D)
+        update(
+            g_up[g], mu[:, cols], fu[:, cols], su[:, cols],
+            nmu.at[:, cols], nfu.at[:, cols], nsu.at[:, cols], *rates,
+        )
+    update(g_dn[...], md[...], fdn[...], sd[...], nmd, nfd, nsd, *rates)
+    flipped = jnp.concatenate([g_vp[:, 128:], jnp.zeros((104, 128), F32)], 0).T
+    vector_grad = flipped[:11, :24]
+    update(vector_grad, mv[...], fv[...], sv[...], nmv, nfv, nsv, VECTOR_RATE, 0.0)
+    residual[...] = flipped[5:7, :24] * factor
+    update(small[1:2, :16], mb[...], fb[...], sb[...], nmb, nfb, nsb, VECTOR_RATE, 0.0)
+
+
+def fast_body(
+    inputs, cotangent, span_order,
+    query_weight, keyval_weight, output_weight, up_weight, down_weight, vectors, kv_bias,
+    *moments,
+):
+    tok = inputs.shape[0]
+    vmem = pl.BlockSpec(memory_space=pltpu.VMEM)
+    smem = pl.BlockSpec(memory_space=pltpu.SMEM)
+    shape = jax.ShapeDtypeStruct
+    V = pltpu.VMEM
+    scratch = [
+        V((4, 4, 2, 24, AW), BF16),
+        V((4, 2, 4, 24, D), BF16),
+        V((4, 2, 96, D), BF16),
+        V((4, 4, 2, 24, 128), F32),
+        V((4, tok, D), BF16),
+        V((4, tok, D), BF16),
+        V((4, 2, tok, 128), BF16),
+        V((4, 24, D), BF16),
+        V((D, AW), BF16),
+        V((D, D), BF16),
+        V((128, D), F32),
+        V((128, 128), F32),
+        V((tok, D), BF16),
+        V((tok, D), F32),
+        V((tok, 128), F32),
+        V((4 * tok, D), BF16),
+        V((4 * tok, D), BF16),
+        V((4 * tok, D), BF16),
+        V((4, tok, D), BF16),
+        V((4, tok, D), BF16),
+        V((HQ, tok, 128), BF16),
+        V((HQ, tok, 128), BF16),
+        V((HQ, HD, tok), BF16),
+        V((128, 8 * tok), BF16),
+        V((8 * tok, tok), F32),
+        V((QO // 256 * D, 256), F32),
+        V((HQ, HD, tok), BF16),
+        V((HQ, HD, tok), F32),
+        V((8 * tok, 128), F32),
+        V((D, 256), F32),
+        V((D, D), F32),
+        V((D, D), F32),
+        V((128, D), F32),
+        V((4, tok, 128), BF16), V((4, tok, 128), BF16),
+        V((3, tok, 128), BF16), V((3, tok, 128), BF16),
+        V((2, tok, D), BF16), V((tok, D), BF16), V((tok, D), BF16),
+        V((2, tok, D), BF16), V((tok, D), BF16), V((tok, D), BF16),
+    ]
+    for width, kind in ((QO, BF16), (256, F32)):
+        for lead in ((2, 8), (8,), (4,), (3,)):
+            scratch += [V(lead + (24, width), kind)] * 2
+    scratch += [V((4, 4, 24, D), BF16)] * 2 + [V((3, 4, 24, D), BF16)] * 2
+    scratch += [V((4, 24, D), BF16), V((3, 24, D), BF16)]
+    scratch += [V((4, 96, D), BF16)] * 2 + [V((3, 96, D), BF16)] * 2
+    scratch += [V((4, 8, 128), F32), V((8, 8, 128), F32)]
+    scratch += [pltpu.SemaphoreType.DMA((N_COPIES,))] * 2
+    kv_row = kv_bias.reshape(1, -1)
+    bo, ig, g_qo, g_vp, g_up, g_dn, small = pl.pallas_call(
+        layer_kernel,
+        name="layer",
+        out_shape=(
+            shape((tok, D), BF16),
+            shape((tok, D), F32),
+            shape((24, QO), F32),
+            shape((24, 256), F32),
+            shape((4, 24, D), F32),
+            shape((96, D), F32),
+            shape((8, 128), F32),
+        ),
+        in_specs=[smem] + [vmem] * 9,
+        out_specs=(vmem,) * 7,
+        scratch_shapes=scratch,
+        compiler_params=pltpu.CompilerParams(
+            collective_id=0, has_side_effects=True, vmem_limit_bytes=62 * 2**20
+        ),
+    )(
+        span_order, inputs, cotangent,
+        query_weight, keyval_weight, output_weight, up_weight, down_weight, vectors, kv_row,
+    )
+    masters = (query_weight, keyval_weight, output_weight, up_weight, down_weight, vectors, kv_row)
+    firsts = tuple(moments[:6]) + (moments[6].reshape(1, -1),)
+    seconds = tuple(moments[7:13]) + (moments[13].reshape(1, -1),)
+    state = [shape(a.shape, F32) for a in masters]
+    results = pl.pallas_call(
+        update_kernel,
+        name="update",
+        out_shape=[shape((tok, D), BF16), shape((tok, D), F32), shape((1, 1), F32)]
+        + state * 3
+        + [shape((2, vectors.shape[1]), F32)],
+        in_specs=[vmem] * 28,
+        out_specs=[vmem] * 25,
+        compiler_params=pltpu.CompilerParams(vmem_limit_bytes=48 * 2**20),
+    )(small, g_qo, g_vp, g_up, g_dn, bo, ig, *masters, *firsts, *seconds)
+    results = list(results)
+    results[2] = results[2].reshape(())
+    for i in (9, 16, 23):
+        results[i] = results[i].reshape(-1)
+    return tuple(results)
+
+
 def solution(mesh):
+    grid = (mesh.shape["fsdp"], mesh.shape["seq"])
     return jax.shard_map(
-        body,
+        fast_body if grid == (4, 8) else body,
         mesh=mesh,
         in_specs=(
             P(("fsdp", "seq"), None),

time: 1200 us -> 190 us (0.16)
  waiting for transfers between devices: 660 us -> 0 us
  blocking collectives: 266 us -> 0 us
  Pallas kernels: 0 us -> 170 us
  matrix products: 134 us -> 0 us
  other arithmetic: 64.9 us -> 0 us
  local copies, waits for them, and re-layouts: 41 us -> 17.2 us
  between operations: 23.2 us -> 0.98 us
    reduce_scatter x5 -> x0, waiting for transfers between devices: 478 us -> none  [the longest x1 139 us: body(): lax.psum_scatter(grad_down, ('fsdp', 'seq'), scatter_dimension=0, tiled=T...]
    pallas_call x0 -> x2, Pallas kernels: none -> 170 us  [the longest x1 168 us: fast_body(): pl.pallas_call(layer_kernel, name='layer', out_shape=(shape((tok, D), BF1...]
    all_gather x3 -> x0, blocking collectives: 167 us -> none  [the longest x1 70.7 us: body(): lax.all_gather(vectors.astype(jnp.bfloat16), ('fsdp', 'seq'), axis=1, til...]
    dot_general x43 -> x0, matrix products: 134 us -> none  [the longest x17 61.6 us: against(): lax.dot_general(left_side, right_side, (((1,), (1,)), ((), ())), preferre...]
    all_gather x4 -> x0, waiting for transfers between devices: 112 us -> none  [the longest x1 60.8 us: body(): lax.all_gather(down_weight.astype(jnp.bfloat16), ('fsdp', 'seq'), axis=0,...]
    unnamed x11 -> x0, waiting for transfers between devices: 69.8 us -> none
    unnamed x2 -> x0, blocking collectives: 59.7 us -> none
    psum x1 -> x0, blocking collectives: 40.1 us -> none  [body(): lax.psum((local_squares, kv_bias_part), ('fsdp', 'seq'))]
  transfers between devices with their start and end apart: 10 -> 0, of which waited for: 8 -> 0; matrix products, arithmetic and copies ran while one was open for 13% -> 0% of each run, Pallas kernels for 0% -> 0%
where the time goes in v1:
time: 190 us; the launch traced here: 189 us
  Pallas kernels  170 us (89%)
  local copies, waits for them, and re-layouts  17.2 us (9%)
    pallas_call x1, Pallas kernels, fast_body(): pl.pallas_call(layer_kernel, name='layer', out_shape=(shape((tok, D), BF1...  168 us
    unnamed x56, local copies, waits for them, and re-layouts  17.2 us

profile of v1, /device:TPU:0, one launch (start us, length us, event | category | flops | bytes accessed | tf_op | source)
XLA Modules:
  0.0 188.7 jit_solution(6511362306530438490)
XLA Ops:
  0.7 0.0 copy-start.17
  0.7 168.4 %layer.1 = (bf16[256,768]{1,0:T(8,128)(2,1)}, f32[256,768]{1,0:T(8,128)}, f32[24,1536]{1,0:T(8,128)}, f32[24,256]{1,0:T(8,128)}, f32[4,24,768]{2,1,0:T(8,128)}, /*index=5*/f32[96,768]{1,0:T(8,128)}, f32[8,128]{1,0:T(8,128)}) custom-call(s32[1,8]{1,0:T(1,128)} %span.1, bf16[256,768]{1,0:T(8,128)(2,1)} %x.1, bf16[256,768]{1,0:T(8,128)(2,1)} %cot.1, ...), custom_call_target="tpu_custom_call" | custom-call | tf_op jit(solution)/shard_map/layer/pallas_call | solution.py:1095
  169.3 1.1 copy-done.2
  170.4 1.0 copy-done.3
  171.4 1.0 copy-done.7
  172.4 1.0 copy-done.8
  173.3 1.0 copy-done.9
  174.3 0.9 copy-done.11
  175.2 0.9 copy-done.12
  176.1 0.9 copy-done.13
  177.0 0.9 copy-done.14
  177.8 0.9 copy-done.15
  178.7 0.9 copy-done.16
  179.6 0.7 copy-done.18
  180.3 0.7 copy-done.19
  181.1 0.7 copy-done.20
  181.8 0.7 copy-done.21
  182.5 0.7 copy-done.22
  183.2 0.7 copy-done.23
  183.9 0.7 copy-done.24
  184.5 0.7 copy-done.25
  185.2 0.7 copy-done.26
  185.9 0.7 copy-done.27
  186.5 2.0 %update.1 = (bf16[256,768]{1,0:T(8,128)(2,1)}, f32[256,768]{1,0:T(8,128)}, f32[1,1]{1,0:T(1,128)}, f32[24,768]{1,0:T(8,128)}, f32[24,128]{1,0:T(8,128)}, /*index...) custom-call(f32[8,128]{1,0:T(8,128)S(1)} %copy-done.24, ...), custom_call_target="tpu_custom_call" | custom-call | tf_op jit(solution)/shard_map/update/pallas_call | solution.py:1121
  (34 shorter events, 0.1 us)
Async XLA Ops:
  0.7 168.5 %copy-start.17 = (f32[24,128]{1,0:T(8,128)S(1)}, f32[24,128]{1,0:T(8,128)}, u32[]{:S(2)}) copy-start(f32[24,128]{1,0:T(8,128)} %mk.1) | copy-start | bytes 36868
  0.7 168.5 %copy-start = (f32[24,3072]{1,0:T(8,128)S(1)}, f32[24,3072]{1,0:T(8,128)}, u32[]{:S(2)}) copy-start(f32[24,3072]{1,0:T(8,128)} %mu.1) | copy-start | bytes 884740
  0.7 168.5 %copy-start.1 = (f32[96,768]{1,0:T(8,128)S(1)}, f32[96,768]{1,0:T(8,128)}, u32[]{:S(2)}) copy-start(f32[96,768]{1,0:T(8,128)} %md.1) | copy-start | bytes 884740
  0.7 168.5 %copy-start.4 = (f32[24,3072]{1,0:T(8,128)S(1)}, f32[24,3072]{1,0:T(8,128)}, u32[]{:S(2)}) copy-start(f32[24,3072]{1,0:T(8,128)} %fu.1) | copy-start | bytes 884740
  0.7 168.5 %copy-start.5 = (f32[96,768]{1,0:T(8,128)S(1)}, f32[96,768]{1,0:T(8,128)}, u32[]{:S(2)}) copy-start(f32[96,768]{1,0:T(8,128)} %fdn.1) | copy-start | bytes 884740
  0.7 168.5 %copy-start.6 = (f32[24,3072]{1,0:T(8,128)S(1)}, f32[24,3072]{1,0:T(8,128)}, u32[]{:S(2)}) copy-start(f32[24,3072]{1,0:T(8,128)} %su.1) | copy-start | bytes 884740
  0.7 168.5 %copy-start.10 = (f32[24,768]{1,0:T(8,128)S(1)}, f32[24,768]{1,0:T(8,128)}, u32[]{:S(2)}) copy-start(f32[24,768]{1,0:T(8,128)} %mq.1) | copy-start | bytes 221188
  169.3 1.1 copy-start.2
  170.4 1.0 copy-start.3
  171.4 1.0 copy-start.7
  172.4 1.0 copy-start.8
  173.3 1.0 copy-start.9
  174.3 0.9 copy-start.11
  175.2 0.9 copy-start.12
  176.1 0.9 copy-start.13
  177.0 0.9 copy-start.14
  177.8 0.9 copy-start.15
  178.7 0.9 copy-start.16
  179.6 0.7 copy-start.18
  180.3 0.7 copy-start.19
  181.1 0.7 copy-start.20
  181.8 0.7 copy-start.21
  182.5 0.7 copy-start.22
  183.2 0.7 copy-start.23
  (4 other events, 2.6 us)

commit v2 on v1

--- a/solution.py
+++ b/solution.py
@@ -376,22 +376,45 @@
     )
 
 
+class Copy:
+    def __init__(self, copy):
+        self.copy, self.started, self.received = copy, False, False
+
+    def start(self):
+        self.started = True
+        self.copy.start()
+
+    def wait_recv(self):
+        self.received = True
+        self.copy.wait_recv()
+
+    def wait_send(self):
+        self.copy.wait_send()
+
+
 class Copies:
     def __init__(self, send_sems, recv_sems):
         self.send_sems, self.recv_sems, self.all = send_sems, recv_sems, []
 
     def make(self, source, target, device):
         index = len(self.all)
-        copy = pltpu.make_async_remote_copy(
+        copy = Copy(pltpu.make_async_remote_copy(
             src_ref=source,
             dst_ref=target,
             send_sem=self.send_sems.at[index],
             recv_sem=self.recv_sems.at[index],
             device_id=device,
             device_id_type=pl.DeviceIdType.MESH,
-        )
+        ))
         self.all.append(copy)
         return copy
+
+    def finish(self):
+        for copy in self.all:
+            if copy.started:
+                if not copy.received:
+                    copy.wait_recv()
+                copy.wait_send()
 
 
 def slab_rows(block, index):
@@ -414,15 +437,14 @@
             self.ref[self.rows(p, block, index), :] = value[:, p * 256 : p * 256 + 256]
 
 
-N_COPIES = 130
+N_COPIES = 150
 QO = 1536
-AW = 1664
 
 
 def layer_kernel(
     span, x, cot, qw, kw, ow, uw, dw, vec, kvb,
     bo, ig, g_qo, g_vp, g_up, g_dn, g_small,
-    A, U, Dn, VT, X, C, KV, ub, WA, WU, gains, vsq,
+    KW, Q, O, U, Dn, X, C, KV, ub, WQ, WKV, WO, WU, gains, vsq,
     n1, hat1, scale1, N2, act, dl, OP, NP,
     qz, doz, doT, kvT, bias, sbuf, mixT, dqT, dkv,
     GP, GU, GD, vg,
@@ -451,17 +473,28 @@
     dev_zy = tuple((f, zz * 2 + yo) for zz in zk)
     fsdp_devs = (dev_c, dev_x, dev_d)
     seq_devs = dev_z[1:] + dev_zy
+    far = (1, 2, 3)
 
     copies = Copies(send_sems, recv_sems)
     make = copies.make
 
+    def start(*wanted):
+        for copy in wanted:
+            copy.start()
+
+    def arrive(*wanted):
+        for copy in wanted:
+            copy.wait_recv()
+
     def seq_gather(ref):
-        to_z = [None] + [make(ref(z, y), ref(z, y), dev_z[k]) for k in (1, 2, 3)]
+        to_z = [None] + [make(ref(z, y), ref(z, y), dev_z[k]) for k in far]
         to_y = [make(ref(zk[k], y), ref(zk[k], y), dev_y) for k in range(4)]
         return to_z, to_y
 
-    a_z, a_y = seq_gather(lambda i, j: A.at[f, i, j])
-    v_z, v_y = seq_gather(lambda i, j: VT.at[f, i, j])
+    w_z, w_y = seq_gather(lambda i, j: KW.at[f, i, j])
+    q_z, q_y = seq_gather(lambda i, j: Q.at[f, i, j])
+    o_z, o_y = seq_gather(lambda i, j: O.at[f, i, j])
+    p_z, p_y = seq_gather(lambda i, j: O.at[fx, i, j])
     u_z, u_y = seq_gather(lambda i, j: U.at[i, j])
     d_z, d_y = seq_gather(lambda i, j: Dn.at[i, j])
     k_z, k_y = seq_gather(lambda i, j: KV.at[i, j])
@@ -472,8 +505,11 @@
         on_c = [make(ref(fx, j), ref(fx, j), dev_c) for j in (y, yo)]
         return to_x, to_c, on_c
 
-    a_x, a_c, a_xc = fsdp_gather(lambda i, j: A.at[i, :, j])
-    v_x, v_c, v_xc = fsdp_gather(lambda i, j: VT.at[i, :, j])
+    w_x, w_c, w_xc = fsdp_gather(lambda i, j: KW.at[i, :, j])
+    q_x, q_c, q_xc = fsdp_gather(lambda i, j: Q.at[i, :, j])
+    o_x = make(O.at[f, z, y], O.at[f, z, y], dev_x)
+    o_c = [make(O.at[f, :, j], O.at[f, :, j], dev_c) for j in (y, yo)]
+    p_c = [make(O.at[fx, :, j], O.at[fx, :, j], dev_c) for j in (y, yo)]
 
     def token_gather(ref):
         return (
@@ -515,169 +551,29 @@
     for dev in fsdp_devs + seq_devs:
         pl.semaphore_signal(barrier, inc=1, device_id=dev, device_id_type=pl.DeviceIdType.MESH)
 
+    vsq[...] = jnp.zeros((128, 128), F32)
+    vsq[0:11, 0:24] = vec[...]
+    vsq[11:12, 0:16] = kvb[...]
+    KW[f, z, y, :, :128] = kw[...].astype(BF16)
+    KW[f, z, y, :, 128:] = vsq[...].T[:24, :].astype(BF16)
+    Q[f, z, y] = qw[...].astype(BF16)
+    O[f, z, y] = ow[...].astype(BF16)
     for j in range(4):
         ub[j] = uw[:, j * D : (j + 1) * D].astype(BF16)
     U[z, y, f] = ub[f]
     Dn[z, y] = dw[...].astype(BF16)
-    A[f, z, y, :, :D] = qw[...].astype(BF16)
-    A[f, z, y, :, D : D + 128] = kw[...].astype(BF16)
-    A[f, z, y, :, D + 128 :] = ow[...].astype(BF16)
-    vsq[...] = jnp.zeros((128, 128), F32)
-    vsq[0:11, 0:24] = vec[...]
-    vsq[11:12, 0:16] = kvb[...]
-    VT[f, z, y] = vsq[...].astype(BF16).astype(F32).T[:24, :]
     X[f] = x[...]
     C[f] = cot[...]
 
     pl.semaphore_wait(barrier, 10)
-
-    for copy in u_f:
-        copy.start()
-    for k in (1, 2, 3):
-        v_z[k].start()
-    v_y[0].start()
-    for copy in (x_x, c_x, x_c, c_c):
-        copy.start()
-    for k in (1, 2, 3):
-        d_z[k].start()
-    d_y[0].start()
-    for copy in u_f:
-        copy.wait_recv()
-    for k in (1, 2, 3):
-        u_z[k].start()
-    u_y[0].start()
-    for k in (1, 2, 3):
-        v_z[k].wait_recv()
-        v_y[k].start()
-    v_x[0].start()
-    v_c[0].start()
-    for k in (1, 2, 3):
-        a_z[k].start()
-    a_y[0].start()
-    for k in range(4):
-        v_y[k].wait_recv()
-    v_x[1].start()
-    v_c[1].start()
-    for j in range(2):
-        v_x[j].wait_recv()
-        v_xc[j].start()
-    for k in (1, 2, 3):
-        d_z[k].wait_recv()
-        d_y[k].start()
-    x_x.wait_recv()
-    x_xc.start()
-    for k in (1, 2, 3):
-        u_z[k].wait_recv()
-        u_y[k].start()
-    c_x.wait_recv()
-    c_xc.start()
-    for k in (1, 2, 3):
-        a_z[k].wait_recv()
-        a_y[k].start()
-    a_x[0].start()
-    a_c[0].start()
-    for j in range(2):
-        v_c[j].wait_recv()
-        v_xc[j].wait_recv()
-
-    gains[...] = VT.reshape(D, 128)[...].T
-    vsq[...] = jnp.concatenate([VT[0, i // 2, i % 2][:16] for i in range(8)], 0).T
-    kv_shift = vsq[11:12, :]
+    start(w_z[1], w_z[2], w_z[3], w_y[0])
+    start(o_x, q_z[1], q_z[2], q_z[3], q_y[0])
+    start(o_z[1], o_z[2], o_z[3], o_y[0])
+    start(*u_f)
+
     hat, scale = normalise(x[...].astype(F32))
     hat1[...] = hat
     scale1[...] = jnp.broadcast_to(scale, (tok, 128))
-    n1[...] = (hat * gains[0:1, :] + gains[1:2, :]).astype(BF16)
-    vg[...] = jnp.zeros((128, D), F32)
-    csum = jnp.sum(cot[...].astype(F32), 0, keepdims=True)
-    vg[5:6, :] = csum
-    vg[6:7, :] = csum
-
-    for k in range(4):
-        d_y[k].wait_recv()
-    for k in range(4):
-        u_y[k].wait_recv()
-    for copy in (x_c, x_xc, c_c, c_xc):
-        copy.wait_recv()
-
-    for g in range(4):
-        for i in range(4):
-            pair = jnp.concatenate([U[i, j, g].astype(F32) for j in range(2)], 0)
-            WU[(g * 4 + i) * 48 : (g * 4 + i + 1) * 48, :] = pair.astype(BF16)
-    WD = Dn.reshape(D, D)
-    up_bias = gains[pl.ds(7 + f, 1), :]
-    vg[pl.ds(7 + f, 1), :] = jnp.zeros((1, D), F32)
-
-    def token_block(t, carry):
-        two_gain, two_shift, up_sum = carry
-        rows = pl.ds(pl.multiple_of(t * tok, tok), tok)
-        hat2, _ = normalise(X[t].astype(F32))
-        low2 = (hat2 * gains[2:3, :] + gains[3:4, :]).astype(BF16)
-        N2[rows, :] = low2
-        back = C[t]
-        sums = []
-        for c in range(3):
-            units = slice(c * 256, c * 256 + 256)
-            lifted = dot_nn(low2, WU[:, units]) + up_bias[:, units]
-            active_grad = dot_nt(back, WD[units, :])
-            half = 0.5 + 0.5 * lax.erf(lifted * (0.5**0.5))
-            act[rows, units] = (lifted * half).astype(BF16)
-            bell = jnp.exp(lifted * lifted * -0.5) * (1.0 / math.sqrt(2.0 * math.pi))
-            low = ((half + lifted * bell) * active_grad).astype(BF16)
-            dl[rows, units] = low
-            sums.append(jnp.sum(low.astype(F32), 0, keepdims=True))
-        OP[t] = dot_nn(act[rows, :], WD[...]).astype(BF16)
-        grad2 = dot_nt(dl[rows, :], WU[...])
-        NP[t] = grad2.astype(BF16)
-        return (
-            two_gain + jnp.sum(grad2 * hat2, 0, keepdims=True),
-            two_shift + jnp.sum(grad2, 0, keepdims=True),
-            up_sum + jnp.concatenate(sums, 1),
-        )
-
-    zero_row = jnp.zeros((1, D), F32)
-    two_gain, two_shift, up_sum = lax.fori_loop(0, 4, token_block, (zero_row,) * 3)
-    vg[2:3, :] = two_gain
-    vg[3:4, :] = two_shift
-    vg[pl.ds(7 + f, 1), :] = up_sum
-    for copy in out_c + nrm_c:
-        copy.start()
-
-    for k in range(4):
-        a_y[k].wait_recv()
-    a_x[1].start()
-    a_c[1].start()
-
-    CF = C.reshape(4 * tok, D)
-    for c in range(3):
-        units = slice(c * 256, c * 256 + 256)
-        GD[units, :] = dot_tn(act[:, units], CF[...])
-    for k in (1, 2, 3, 0):
-        for i in range(1):
-            SD1[zk[k]] = GD[pl.ds(pl.multiple_of((zk[k] * 2 + yo) * 96, 8), 96), :].astype(BF16)
-        sd_y[k].start()
-    a_x[0].wait_recv()
-    a_xc[0].start()
-    for c in range(3):
-        units = slice(c * 256, c * 256 + 256)
-        GU[units, :] = dot_tn(N2[:, units], dl[...])
-    for k in (1, 2, 3, 0):
-        for g in range(4):
-            SU1[zk[k], g] = GU[slab_rows(g, zk[k] * 2 + yo), :].astype(BF16)
-        su_y[k].start()
-    a_x[1].wait_recv()
-    a_xc[1].start()
-    for j in range(2):
-        a_c[j].wait_recv()
-        a_xc[j].wait_recv()
-
-    def join(i, carry):
-        g = lax.div(i, 4)
-        zz = lax.rem(i, 4)
-        pair = jnp.concatenate([A[g, zz, 0].astype(F32), A[g, zz, 1].astype(F32)], 0)
-        WA[pl.ds(pl.multiple_of(i * 48, 16), 48), :] = pair.astype(BF16)
-        return carry
-
-    lax.fori_loop(0, 16, join, 0)
     own_span = span[0, s]
     lane = lax.broadcasted_iota(jnp.int32, (tok, 128), 1)
     spot = lax.broadcasted_iota(jnp.int32, (tok, 128), 0) + own_span * tok
@@ -704,13 +600,85 @@
         down = pltpu.roll(block, 8, 1)
         return block * cos_t + up * low_t - down * high_t
 
-    kv_pre = dot_nn(n1[...], WA[:, D : D + 128]) + kv_shift
+    for k in far:
+        arrive(w_z[k])
+        start(w_y[k])
+    start(w_x[0], w_c[0])
+    arrive(o_x)
+    start(p_z[1], p_z[2], p_z[3], p_y[0])
+    for k in far:
+        arrive(q_z[k])
+        start(q_y[k])
+    start(q_x[0], q_c[0])
+    arrive(*w_y)
+    start(w_x[1], w_c[1])
+    for k in far:
+        arrive(o_z[k])
+        start(o_y[k])
+    start(o_c[0])
+    arrive(w_x[0])
+    start(w_xc[0])
+    arrive(w_x[1])
+    start(w_xc[1])
+    for k in far:
+        arrive(p_z[k])
+        start(p_y[k])
+    start(p_c[0])
+    arrive(*q_y)
+    start(q_x[1], q_c[1])
+    arrive(*w_c, *w_xc)
+
+    slabs = [KW[g, i, j].astype(F32) for g in range(4) for i in range(4) for j in range(2)]
+    for i in range(16):
+        pair = jnp.concatenate([slabs[2 * i][:, :128], slabs[2 * i + 1][:, :128]], 0)
+        WKV[i * 48 : (i + 1) * 48, :] = pair.astype(BF16)
+    gains[...] = jnp.concatenate([slab[:, 128:] for slab in slabs], 0).T
+    vsq[...] = jnp.concatenate([slab[:16, 128:] for slab in slabs[:8]], 0).T
+    kv_shift = vsq[11:12, :]
+    n1[...] = (hat * gains[0:1, :] + gains[1:2, :]).astype(BF16)
+    kv_pre = dot_nn(n1[...], WKV[...]) + kv_shift
     KV[z, y] = turn(kv_pre, key_cos, key_low, key_high).astype(BF16)
-    for k in (1, 2, 3):
-        k_z[k].start()
-    k_y[0].start()
-
-    q_pre = dot_nn(n1[...], WA[:, :D]) + gains[4:5, :]
+    start(k_z[1], k_z[2], k_z[3], k_y[0])
+    arrive(q_x[0])
+    start(q_xc[0])
+    arrive(*u_f)
+    start(d_z[1], d_z[2], d_z[3], d_y[0])
+    vg[...] = jnp.zeros((128, D), F32)
+    csum = jnp.sum(cot[...].astype(F32), 0, keepdims=True)
+    vg[5:6, :] = csum
+    vg[6:7, :] = csum
+    key_iota = lax.broadcasted_iota(jnp.int32, (tok, tok), 0)
+    row_iota = lax.broadcasted_iota(jnp.int32, (tok, tok), 1) + own_span * tok
+    for i in range(8):
+        bias[i * tok : (i + 1) * tok, :] = jnp.where(
+            key_iota + span[0, i] * tok <= row_iota, 0.0, MASKED
+        ).astype(F32)
+    dkv[...] = jnp.zeros((8 * tok, 128), F32)
+    arrive(*o_y)
+    start(o_c[1])
+    arrive(*p_y)
+    start(p_c[1])
+    for k in far:
+        arrive(k_z[k])
+        start(k_y[k])
+    arrive(q_x[1])
+    start(q_xc[1])
+    start(x_x, c_x, x_c, c_c)
+    start(u_z[1], u_z[2], u_z[3], u_y[0])
+    arrive(*q_c, *q_xc)
+
+    def join(ref, whole):
+        def put(i, carry):
+            g = lax.div(i, 4)
+            zz = lax.rem(i, 4)
+            pair = jnp.concatenate([ref[g, zz, 0].astype(F32), ref[g, zz, 1].astype(F32)], 0)
+            whole[pl.ds(pl.multiple_of(i * 48, 16), 48), :] = pair.astype(BF16)
+            return carry
+
+        lax.fori_loop(0, 16, put, 0)
+
+    join(Q, WQ)
+    q_pre = dot_nn(n1[...], WQ[...]) + gains[4:5, :]
     gap = jnp.zeros((tok, 64), BF16)
     for j in range(6):
         cols = slice(j * 128, j * 128 + 128)
@@ -718,67 +686,19 @@
         turned = (turned * HD ** (-0.5)).astype(BF16)
         qz[2 * j] = jnp.concatenate([turned[:, :64], gap], 1)
         qz[2 * j + 1] = jnp.concatenate([turned[:, 64:], gap], 1)
-    for k in (1, 2, 3):
-        k_z[k].wait_recv()
-        k_y[k].start()
-    mixed_back = dot_nt(cot[...], WA[:, D + 128 :]).astype(BF16)
+    arrive(*o_c, *p_c)
+    join(O, WO)
+    mixed_back = dot_nt(cot[...], WO[...]).astype(BF16)
     for j in range(6):
         pair = mixed_back[:, j * 128 : j * 128 + 128]
         doz[2 * j] = jnp.concatenate([gap, pair[:, :64]], 1)
         doz[2 * j + 1] = jnp.concatenate([gap, pair[:, 64:]], 1)
     doT[...] = mixed_back.astype(F32).T.astype(BF16).reshape(HQ, HD, tok)
-    key_iota = lax.broadcasted_iota(jnp.int32, (tok, tok), 0)
-    row_iota = lax.broadcasted_iota(jnp.int32, (tok, tok), 1) + own_span * tok
-    for i in range(8):
-        bias[i * tok : (i + 1) * tok, :] = jnp.where(
-            key_iota + span[0, i] * tok <= row_iota, 0.0, MASKED
-        ).astype(F32)
-    dkv[...] = jnp.zeros((8 * tok, 128), F32)
-    for k in range(4):
-        k_y[k].wait_recv()
+    arrive(*k_y)
     KVF = KV.reshape(8 * tok, 128)
     kvT[...] = KVF[...].astype(F32).T.astype(BF16)
 
-    def scatter_step(k):
-        su_y[k].wait_recv()
-        sd_y[k].wait_recv()
-        own = zk[k]
-        rows = pl.ds(pl.multiple_of((own * 2 + y) * 96, 8), 96)
-        total = GD[rows, :] + RD1[own].astype(F32)
-        if k:
-            SD2[k - 1] = total.astype(BF16)
-            sd_z[k - 1].start()
-        else:
-            GD[rows, :] = total
-        for g in range(4):
-            rows = slab_rows(g, own * 2 + y)
-            total = GU[rows, :] + RU1[own, g].astype(F32)
-            if k:
-                SU2[k - 1, g] = total.astype(BF16)
-            else:
-                GU[rows, :] = total
-        if k:
-            su_z[k - 1].start()
-
-    def tokens_to_x():
-        for copy in out_c + nrm_c:
-            copy.wait_recv()
-        SO2[...] = (OP[fx].astype(F32) + RO1[1].astype(F32)).astype(BF16)
-        out_x.start()
-        SN2[...] = (NP[fx].astype(F32) + RN1[1].astype(F32)).astype(BF16)
-        nrm_x.start()
-
-    def attend(step_index, carry):
-        @pl.when(step_index == 0)
-        def _():
-            tokens_to_x()
-
-        for k, at in ((1, 1), (2, 2), (3, 3), (0, 4)):
-
-            @pl.when(step_index == at)
-            def _():
-                scatter_step(k)
-
+    def attend(step_index):
         heads = [step_index * 2, step_index * 2 + 1]
         tops, shares, deltas = [], [], []
         for j, h in enumerate(heads):
@@ -821,13 +741,124 @@
                 acc = acc + dot_nn(kvT[:, rows], score_low)
                 dkv[rows, :] += dot_nn(score_low, qz[h])
             dqT[h] = acc[:64, :] * HD ** (-0.5)
-        return carry
-
-    lax.fori_loop(0, HQ // 2, attend, 0)
+
+    def attend_all(first, last, meanwhile):
+        def body_step(step_index, carry):
+            for at, action in meanwhile:
+                pl.when(step_index == at)(action)
+            attend(step_index)
+            return carry
+
+        lax.fori_loop(first, last, body_step, 0)
+
+    def down_on():
+        for k in far:
+            arrive(d_z[k])
+            start(d_y[k])
+
+    def up_on():
+        for k in far:
+            arrive(u_z[k])
+            start(u_y[k])
+        arrive(x_x)
+        start(x_xc)
+
+    def back_on():
+        arrive(c_x)
+        start(c_xc)
+
+    attend_all(0, 3, ((0, down_on), (1, up_on), (2, back_on)))
+    arrive(*d_y, *u_y, x_c, x_xc, c_c, c_xc)
+
+    for g in range(4):
+        for i in range(4):
+            pair = jnp.concatenate([U[i, j, g].astype(F32) for j in range(2)], 0)
+            WU[(g * 4 + i) * 48 : (g * 4 + i + 1) * 48, :] = pair.astype(BF16)
+    WD = Dn.reshape(D, D)
+    up_bias = gains[pl.ds(7 + f, 1), :]
+
+    def token_block(t, carry):
+        two_gain, two_shift, up_sum = carry
+        rows = pl.ds(pl.multiple_of(t * tok, tok), tok)
+        hat2, _ = normalise(X[t].astype(F32))
+        low2 = (hat2 * gains[2:3, :] + gains[3:4, :]).astype(BF16)
+        N2[rows, :] = low2
+        back = C[t]
+        sums = []
+        for c in range(3):
+            units = slice(c * 256, c * 256 + 256)
+            lifted = dot_nn(low2, WU[:, units]) + up_bias[:, units]
+            active_grad = dot_nt(back, WD[units, :])
+            half = 0.5 + 0.5 * lax.erf(lifted * (0.5**0.5))
+            act[rows, units] = (lifted * half).astype(BF16)
+            bell = jnp.exp(lifted * lifted * -0.5) * (1.0 / math.sqrt(2.0 * math.pi))
+            low = ((half + lifted * bell) * active_grad).astype(BF16)
+            dl[rows, units] = low
+            sums.append(jnp.sum(low.astype(F32), 0, keepdims=True))
+        OP[t] = dot_nn(act[rows, :], WD[...]).astype(BF16)
+        grad2 = dot_nt(dl[rows, :], WU[...])
+        NP[t] = grad2.astype(BF16)
+        return (
+            two_gain + jnp.sum(grad2 * hat2, 0, keepdims=True),
+            two_shift + jnp.sum(grad2, 0, keepdims=True),
+            up_sum + jnp.concatenate(sums, 1),
+        )
+
+    zero_row = jnp.zeros((1, D), F32)
+    two_gain, two_shift, up_sum = lax.fori_loop(0, 4, token_block, (zero_row,) * 3)
+    vg[2:3, :] = two_gain
+    vg[3:4, :] = two_shift
+    vg[pl.ds(7 + f, 1), :] = up_sum
+    start(*out_c, *nrm_c)
+    CF = C.reshape(4 * tok, D)
+    for c in range(3):
+        units = slice(c * 256, c * 256 + 256)
+        GD[units, :] = dot_tn(act[:, units], CF[...])
+    for k in (1, 2, 3, 0):
+        SD1[zk[k]] = GD[pl.ds(pl.multiple_of((zk[k] * 2 + yo) * 96, 8), 96), :].astype(BF16)
+        start(sd_y[k])
+
+    def tokens_to_x():
+        arrive(*out_c, *nrm_c)
+        SO2[...] = (OP[fx].astype(F32) + RO1[1].astype(F32)).astype(BF16)
+        start(out_x)
+        SN2[...] = (NP[fx].astype(F32) + RN1[1].astype(F32)).astype(BF16)
+        start(nrm_x)
+
+    def down_step(k):
+        arrive(sd_y[k])
+        rows = pl.ds(pl.multiple_of((zk[k] * 2 + y) * 96, 8), 96)
+        total = GD[rows, :] + RD1[zk[k]].astype(F32)
+        if k:
+            SD2[k - 1] = total.astype(BF16)
+            start(sd_z[k - 1])
+        else:
+            GD[rows, :] = total
+
+    def up_step(k):
+        arrive(su_y[k])
+        for g in range(4):
+            rows = slab_rows(g, zk[k] * 2 + y)
+            total = GU[rows, :] + RU1[zk[k], g].astype(F32)
+            if k:
+                SU2[k - 1, g] = total.astype(BF16)
+            else:
+                GU[rows, :] = total
+        if k:
+            start(su_z[k - 1])
+
+    def down_rest():
+        down_step(3)
+        down_step(0)
+
+    attend_all(
+        3, HQ // 2,
+        ((3, tokens_to_x), (4, lambda: down_step(1)), (4, lambda: down_step(2)), (5, down_rest)),
+    )
 
     for zz in range(4):
         SK1[zz] = dkv[pl.ds(pl.multiple_of((2 * zz + yo) * tok, 8), tok), :].astype(BF16)
-    rk1.start()
+    start(rk1)
     mix_low = mixT.reshape(D, tok)[...]
     for c in range(3):
         sbuf[(3 + c) * D : (4 + c) * D, :] = dot_nn(mix_low, cot[:, c * 256 : c * 256 + 256])
@@ -851,10 +882,10 @@
             return carry
 
         lax.fori_loop(0, 8, put, 0)
-        copy.start()
+        start(copy)
 
     def scatter_x(G, R1, S2, copies_):
-        copies_[0].wait_recv()
+        arrive(copies_[0])
 
         def put(i, carry):
             S2[i] = (G.get(fx, i) + R1[1, i].astype(F32)).astype(S2.dtype)
@@ -862,10 +893,10 @@
             return carry
 
         lax.fori_loop(0, 8, put, 0)
-        copies_[1].start()
+        start(copies_[1])
 
     def scatter_y(G, R2, S3, copies_):
-        copies_[1].wait_recv()
+        arrive(copies_[1])
 
         def put(i, carry):
             S3[i] = (G.get(f, 2 * i + yo) + R2[2 * i + yo].astype(F32)).astype(S3.dtype)
@@ -873,36 +904,43 @@
             return carry
 
         lax.fori_loop(0, 4, put, 0)
-        copies_[2].start()
+        start(copies_[2])
 
     def scatter_z(G, R3, S4, copies_):
-        copies_[2].wait_recv()
-        for k in (1, 2, 3):
+        arrive(copies_[2])
+        for k in far:
             total = G.get(f, 2 * zk[k] + y) + R3[zk[k]].astype(F32)
             S4[k - 1] = total.astype(S4.dtype)
-            copies_[3][k - 1].start()
+            start(copies_[3][k - 1])
 
     def scatter_end(G, R3, R4, copies_):
         total = G.get(f, 2 * z + y) + R3[z].astype(F32)
         for k in range(3):
-            copies_[3][k].wait_recv()
+            arrive(copies_[3][k])
             total = total + R4[k].astype(F32)
         return total
 
     scatter_c(GQ, SQ1, q_sc[0])
-    rk1.wait_recv()
-    for k in (1, 2, 3):
+    arrive(rk1)
+    for k in far:
         rows = pl.ds(pl.multiple_of((2 * zk[k] + y) * tok, 8), tok)
         SK2[k - 1] = (dkv[rows, :] + RK1[zk[k]].astype(F32)).astype(BF16)
-        rk2[k - 1].start()
-    grad1 = dot_nt(q_low, WA[:, :D])
+        start(rk2[k - 1])
+    for c in range(3):
+        units = slice(c * 256, c * 256 + 256)
+        GU[units, :] = dot_tn(N2[:, units], dl[...])
+    for k in (1, 2, 3, 0):
+        for g in range(4):
+            SU1[zk[k], g] = GU[slab_rows(g, zk[k] * 2 + yo), :].astype(BF16)
+        start(su_y[k])
     scatter_x(GQ, RQ1, SQ2, q_sc)
+    grad1 = dot_nt(q_low, WQ[...])
     kv_back = dkv[pl.ds(pl.multiple_of((2 * z + y) * tok, 8), tok), :] + RK1[z].astype(F32)
     for k in range(3):
-        rk2[k].wait_recv()
+        arrive(rk2[k])
         kv_back = kv_back + RK2[k].astype(F32)
     kv_low = turn_back(kv_back, key_cos, key_low, key_high).astype(BF16)
-    grad1 = grad1 + dot_nt(kv_low, WA[:, D : D + 128])
+    grad1 = grad1 + dot_nt(kv_low, WKV[...])
     vg[0:1, :] = jnp.sum(grad1 * hat1[...], 0, keepdims=True)
     vg[1:2, :] = jnp.sum(grad1, 0, keepdims=True)
     kv_sum = jnp.sum(kv_low.astype(F32), 0, keepdims=True)
@@ -914,36 +952,30 @@
     GP[:, :128] = dot_tn(n1[...], kv_low)
     GP[:, 128:] = vg[...].T
     scatter_c(GPP, SP1, p_sc[0])
+    up_step(1)
 
     rows = pl.ds(pl.multiple_of(s * 96, 8), 96)
     down_grad = GD[rows, :]
     for k in range(3):
-        sd_z[k].wait_recv()
+        arrive(sd_z[k])
         down_grad = down_grad + RD2[k].astype(F32)
     g_dn[...] = down_grad
-    for k in range(3):
-        su_z[k].wait_recv()
-    for g in range(4):
-        total = GU[slab_rows(g, s), :]
-        for k in range(3):
-            total = total + RU2[k, g].astype(F32)
-        g_up[g] = total
-        SU3[g] = total.astype(BF16)
-    for copy in su_f:
-        copy.start()
     scatter_x(GPP, RP1, SP2, p_sc)
+    up_step(2)
     scatter_y(GQ, RQ2, SQ3, q_sc)
+    up_step(3)
 
     mixed_rows = mix_low.astype(F32).T.astype(BF16)
-    out_x.wait_recv()
+    arrive(out_x)
     bo[...] = (
         x[...].astype(F32)
-        + (dot_nn(mixed_rows, WA[:, D + 128 :]) + gains[5:6, :])
+        + (dot_nn(mixed_rows, WO[...]) + gains[5:6, :])
         + (OP[f].astype(F32) + RO1[0].astype(F32) + RO2[...].astype(F32) + gains[6:7, :])
     ).astype(BF16)
     scatter_y(GPP, RP2, SP3, p_sc)
+    up_step(0)
     scatter_z(GQ, RQ3, SQ4, q_sc)
-    nrm_x.wait_recv()
+    arrive(nrm_x)
     grad2 = NP[f].astype(F32) + RN1[0].astype(F32) + RN2[...].astype(F32)
     hat_rows = hat1[...]
     scale_rows = scale1[:, 0:1]
@@ -953,13 +985,21 @@
         + norm_back(grad2, hat_rows, scale_rows, gains[2:3, :])
     )
     scatter_z(GPP, RP3, SP4, p_sc)
-    for i, g in enumerate((fc, fx, fd)):
-        su_f[i].wait_recv()
-        g_up[g] = RU3[i].astype(F32)
+    arrive(*su_z)
+    for g in range(4):
+        total = GU[slab_rows(g, s), :]
+        for k in range(3):
+            total = total + RU2[k, g].astype(F32)
+        g_up[g] = total
+        SU3[g] = total.astype(BF16)
+    start(*su_f)
     qo_grad = scatter_end(GQ, RQ3, RQ4, q_sc)
     g_qo[...] = qo_grad
     vp_grad = scatter_end(GPP, RP3, RP4, p_sc)
     g_vp[...] = vp_grad
+    for i, g in enumerate((fc, fx, fd)):
+        arrive(su_f[i])
+        g_up[g] = RU3[i].astype(F32)
 
     def fold(values):
         return jnp.sum(jnp.sum(values * values, 0, keepdims=True), 1, keepdims=True)
@@ -973,24 +1013,19 @@
     column = lax.broadcasted_iota(jnp.int32, (8, 128), 1)
     kv_line = jnp.where(column < 16, jnp.broadcast_to(kv_rows[11:12, :], (8, 128)), 0.0)
     NS1[f] = jnp.where(line == 0, squares, kv_line)
-    for copy in n_f:
-        copy.start()
-    for copy in n_f:
-        copy.wait_recv()
+    start(*n_f)
+    arrive(*n_f)
     kv_piece = NS1[0][1:2, :]
     chip = NS1[0] + NS1[1] + NS1[2] + NS1[3]
     part = chip[0:1, 0:1] + jnp.sum(kv_piece * kv_piece, 1, keepdims=True)
     NS2[s] = jnp.broadcast_to(part, (8, 128))
-    for copy in n_s:
-        copy.start()
-    for copy in n_s:
-        copy.wait_recv()
+    start(*n_s)
+    arrive(*n_s)
     everything = NS2[0]
     for i in range(1, 8):
         everything = everything + NS2[i]
     g_small[...] = jnp.where(line == 0, everything, jnp.broadcast_to(kv_piece, (8, 128)))
-    for copy in copies.all:
-        copy.wait_send()
+    copies.finish()
 
 
 def update_kernel(
@@ -1045,15 +1080,18 @@
     shape = jax.ShapeDtypeStruct
     V = pltpu.VMEM
     scratch = [
-        V((4, 4, 2, 24, AW), BF16),
+        V((4, 4, 2, 24, 256), BF16),
+        V((4, 4, 2, 24, D), BF16),
+        V((4, 4, 2, 24, D), BF16),
         V((4, 2, 4, 24, D), BF16),
         V((4, 2, 96, D), BF16),
-        V((4, 4, 2, 24, 128), F32),
         V((4, tok, D), BF16),
         V((4, tok, D), BF16),
         V((4, 2, tok, 128), BF16),
         V((4, 24, D), BF16),
-        V((D, AW), BF16),
+        V((D, D), BF16),
+        V((D, 128), BF16),
+        V((D, D), BF16),
         V((D, D), BF16),
         V((128, D), F32),
         V((128, 128), F32),
@@ -1083,7 +1121,7 @@
         V((2, tok, D), BF16), V((tok, D), BF16), V((tok, D), BF16),
         V((2, tok, D), BF16), V((tok, D), BF16), V((tok, D), BF16),
     ]
-    for width, kind in ((QO, BF16), (256, F32)):
+    for width, kind in ((QO, BF16), (256, BF16)):
         for lead in ((2, 8), (8,), (4,), (3,)):
             scratch += [V(lead + (24, width), kind)] * 2
     scratch += [V((4, 4, 24, D), BF16)] * 2 + [V((3, 4, 24, D), BF16)] * 2
@@ -1118,16 +1156,22 @@
     firsts = tuple(moments[:6]) + (moments[6].reshape(1, -1),)
     seconds = tuple(moments[7:13]) + (moments[13].reshape(1, -1),)
     state = [shape(a.shape, F32) for a in masters]
+    operands = (small, g_qo, g_vp, g_up, g_dn, bo, ig) + masters + firsts + seconds
+    outcomes = [shape((tok, D), BF16), shape((tok, D), F32), shape((1, 1), F32)]
+    outcomes += state * 3 + [shape((2, vectors.shape[1]), F32)]
+
+    def whole(a):
+        return pl.BlockSpec(a.shape, lambda i: (0,) * len(a.shape))
+
     results = pl.pallas_call(
         update_kernel,
         name="update",
-        out_shape=[shape((tok, D), BF16), shape((tok, D), F32), shape((1, 1), F32)]
-        + state * 3
-        + [shape((2, vectors.shape[1]), F32)],
-        in_specs=[vmem] * 28,
-        out_specs=[vmem] * 25,
-        compiler_params=pltpu.CompilerParams(vmem_limit_bytes=48 * 2**20),
-    )(small, g_qo, g_vp, g_up, g_dn, bo, ig, *masters, *firsts, *seconds)
+        grid=(1,),
+        out_shape=outcomes,
+        in_specs=[whole(a) for a in operands],
+        out_specs=[whole(a) for a in outcomes],
+        compiler_params=pltpu.CompilerParams(vmem_limit_bytes=62 * 2**20),
+    )(*operands)
     results = list(results)
     results[2] = results[2].reshape(())
     for i in (9, 16, 23):

time: 190 us -> 147 us (0.77)
  Pallas kernels: 170 us -> 146 us
  local copies, waits for them, and re-layouts: 17.2 us -> 0 us
    pallas_call x1, Pallas kernels: 168 us -> 142 us  [fast_body(): pl.pallas_call(layer_kernel, name='layer', out_shape=(shape((tok, D), BF1...]
    unnamed x56 -> x0, local copies, waits for them, and re-layouts: 17.2 us -> none
    pallas_call x1, Pallas kernels: 2.03 us -> 4.29 us  [fast_body(): pl.pallas_call(update_kernel, name='update', grid=(1,), out_shape=outcome...]
where the time goes in v2:
time: 147 us
  Pallas kernels  146 us (99%)
    pallas_call x1, Pallas kernels, fast_body(): pl.pallas_call(layer_kernel, name='layer', out_shape=(shape((tok, D), BF1...  142 us
    pallas_call x1, Pallas kernels, fast_body(): pl.pallas_call(update_kernel, name='update', grid=(1,), out_shape=outcome...  4.29 us

profile of v2, /device:TPU:0, one launch (start us, length us, event | category | flops | bytes accessed | tf_op | source)
XLA Modules:
  0.0 146.7 jit_solution(16751844497095969648)
XLA Ops:
  0.7 141.5 %layer.1 = (bf16[256,768]{1,0:T(8,128)(2,1)}, f32[256,768]{1,0:T(8,128)}, f32[24,1536]{1,0:T(8,128)}, f32[24,256]{1,0:T(8,128)}, f32[4,24,768]{2,1,0:T(8,128)}, /*index=5*/f32[96,768]{1,0:T(8,128)}, f32[8,128]{1,0:T(8,128)}) custom-call(s32[1,8]{1,0:T(1,128)} %span.1, bf16[256,768]{1,0:T(8,128)(2,1)} %x.1, bf16[256,768]{1,0:T(8,128)(2,1)} %cot.1, ...), custom_call_target="tpu_custom_call" | custom-call | tf_op jit(solution)/shard_map/layer/pallas_call | solution.py:1133
  142.2 4.3 %update.1 = (bf16[256,768]{1,0:T(8,128)(2,1)}, f32[256,768]{1,0:T(8,128)}, f32[1,1]{1,0:T(1,128)}, f32[24,768]{1,0:T(8,128)}, f32[24,128]{1,0:T(8,128)}, /*index...) custom-call(f32[8,128]{1,0:T(8,128)} %get-tuple-element.57.small, ...), custom_call_target="tpu_custom_call" | custom-call | tf_op jit(solution)/shard_map/update/pallas_call | solution.py:1166

commit v3 on v2

--- a/solution.py
+++ b/solution.py
@@ -378,7 +378,7 @@
 
 class Copy:
     def __init__(self, copy):
-        self.copy, self.started, self.received = copy, False, False
+        self.copy, self.started, self.received, self.sent = copy, False, False, False
 
     def start(self):
         self.started = True
@@ -389,6 +389,7 @@
         self.copy.wait_recv()
 
     def wait_send(self):
+        self.sent = True
         self.copy.wait_send()
 
 
@@ -409,12 +410,16 @@
         self.all.append(copy)
         return copy
 
+    def settle(self):
+        for copy in self.all:
+            if copy.started and not copy.sent:
+                copy.wait_send()
+
     def finish(self):
         for copy in self.all:
-            if copy.started:
-                if not copy.received:
-                    copy.wait_recv()
-                copy.wait_send()
+            if copy.started and not copy.received:
+                copy.wait_recv()
+        self.settle()
 
 
 def slab_rows(block, index):
@@ -422,11 +427,11 @@
 
 
 class Panels:
-    def __init__(self, ref, height):
-        self.ref, self.height, self.count = ref, height, ref.shape[0] // height
+    def __init__(self, ref, height, first, count):
+        self.ref, self.height, self.first, self.count = ref, height, first, count
 
     def rows(self, panel, block, index):
-        return pl.ds(pl.multiple_of(panel * self.height + (block * 8 + index) * 24, 8), 24)
+        return pl.ds(pl.multiple_of((self.first + panel) * self.height + (block * 8 + index) * 24, 8), 24)
 
     def get(self, block, index):
         parts = [self.ref[self.rows(p, block, index), :] for p in range(self.count)]
@@ -437,25 +442,28 @@
             self.ref[self.rows(p, block, index), :] = value[:, p * 256 : p * 256 + 256]
 
 
-N_COPIES = 150
-QO = 1536
+N_COPIES = 151
 
 
 def layer_kernel(
-    span, x, cot, qw, kw, ow, uw, dw, vec, kvb,
-    bo, ig, g_qo, g_vp, g_up, g_dn, g_small,
+    span, x_in, cot_in, qw_in, kw_in, ow_in, uw_in, dw_in, vec_in, kvb_in,
+    to_bo, to_ig, to_q, to_o, to_kv, to_vec, to_up, to_dn, to_small,
+    x, cot, qw, kw, ow, uw, dw, vec, kvb,
+    bo, ig, g_q, g_o, g_kv, g_vec, g_up, g_dn, g_small,
     KW, Q, O, U, Dn, X, C, KV, ub, WQ, WKV, WO, WU, gains, vsq,
     n1, hat1, scale1, N2, act, dl, OP, NP,
     qz, doz, doT, kvT, bias, sbuf, mixT, dqT, dkv,
-    GP, GU, GD, vg,
+    GP, GV, GU, GD, vg,
     SK1, RK1, SK2, RK2,
     RO1, SO2, RO2, RN1, SN2, RN2,
     SQ1, RQ1, SQ2, RQ2, SQ3, RQ3, SQ4, RQ4,
-    SP1, RP1, SP2, RP2, SP3, RP3, SP4, RP4,
+    SO1, QO1, SO2b, RO2b, SO3, RO3, SO4, RO4,
+    SP1, RP1, SP2, RP2, SP3, RP3,
+    SV1, RV1, SV2, RV2, SV3, RV3,
     SU1, RU1, SU2, RU2, SU3, RU3,
     SD1, RD1, SD2, RD2,
     NS1, NS2,
-    send_sems, recv_sems,
+    send_sems, recv_sems, save_sems, load_sems,
 ):
     tok = x.shape[0]
     f = lax.axis_index("fsdp")
@@ -473,7 +481,7 @@
     dev_zy = tuple((f, zz * 2 + yo) for zz in zk)
     fsdp_devs = (dev_c, dev_x, dev_d)
     seq_devs = dev_z[1:] + dev_zy
-    far = (1, 2, 3)
+    far = (3, 2, 1)
 
     copies = Copies(send_sems, recv_sems)
     make = copies.make
@@ -486,8 +494,15 @@
         for copy in wanted:
             copy.wait_recv()
 
+    saved = []
+
+    def save(source, target):
+        copy = pltpu.make_async_copy(source, target, save_sems.at[len(saved)])
+        copy.start()
+        saved.append(copy)
+
     def seq_gather(ref):
-        to_z = [None] + [make(ref(z, y), ref(z, y), dev_z[k]) for k in far]
+        to_z = [None] + [make(ref(z, y), ref(z, y), dev_z[k]) for k in (1, 2, 3)]
         to_y = [make(ref(zk[k], y), ref(zk[k], y), dev_y) for k in range(4)]
         return to_z, to_y
 
@@ -507,9 +522,10 @@
 
     w_x, w_c, w_xc = fsdp_gather(lambda i, j: KW.at[i, :, j])
     q_x, q_c, q_xc = fsdp_gather(lambda i, j: Q.at[i, :, j])
+    q_xs = [make(Q.at[f, zz, yo], Q.at[f, zz, yo], dev_x) for zz in zk]
     o_x = make(O.at[f, z, y], O.at[f, z, y], dev_x)
     o_c = [make(O.at[f, :, j], O.at[f, :, j], dev_c) for j in (y, yo)]
-    p_c = [make(O.at[fx, :, j], O.at[fx, :, j], dev_c) for j in (y, yo)]
+    op_c = [make(O.at[fx, :, j], O.at[fx, :, j], dev_c) for j in (y, yo)]
 
     def token_gather(ref):
         return (
@@ -522,7 +538,7 @@
     c_x, c_c, c_xc = token_gather(C)
     u_f = [make(ub.at[g], U.at[z, y, f], dev) for g, dev in zip((fc, fx, fd), fsdp_devs)]
 
-    rk1 = make(SK1, RK1, dev_y)
+    rk1 = [make(SK1.at[zz], RK1.at[zz], dev_y) for zz in zk]
     rk2 = [make(SK2.at[k], RK2.at[k], dev_z[k + 1]) for k in range(3)]
     out_c = [make(OP.at[g], RO1.at[i], dev_c) for i, g in enumerate((fc, fd))]
     out_x = make(SO2, RO2, dev_x)
@@ -532,13 +548,19 @@
     def full_scatter(S1, R1, S2, R2, S3, R3, S4, R4):
         return (
             make(S1, R1, dev_c),
-            make(S2, R2, dev_x),
+            [make(S2.at[i], R2.at[i], dev_x) for i in range(2)],
             make(S3, R3, dev_y),
             [make(S4.at[k], R4.at[k], dev_z[k + 1]) for k in range(3)],
         )
 
     q_sc = full_scatter(SQ1, RQ1, SQ2, RQ2, SQ3, RQ3, SQ4, RQ4)
-    p_sc = full_scatter(SP1, RP1, SP2, RP2, SP3, RP3, SP4, RP4)
+    p_c = make(SP1, RP1, dev_c)
+    p_x = make(SP2, RP2, dev_x)
+    p_s = [make(SP3.at[i], RP3.at[i], dev) for i, dev in enumerate(seq_devs)]
+    v_c = make(SV1, RV1, dev_c)
+    v_x = make(SV2, RV2, dev_x)
+    v_s = [make(SV3, RV3.at[i], dev) for i, dev in enumerate(seq_devs)]
+    o_sc = full_scatter(SO1, QO1, SO2b, RO2b, SO3, RO3, SO4, RO4)
     su_y = [make(SU1.at[zz], RU1.at[zz], dev_y) for zz in zk]
     su_z = [make(SU2.at[k], RU2.at[k], dev_z[k + 1]) for k in range(3)]
     su_f = [make(SU3.at[g], RU3.at[i], dev) for i, (g, dev) in enumerate(zip((fc, fx, fd), fsdp_devs))]
@@ -550,6 +572,18 @@
     barrier = pltpu.get_barrier_semaphore()
     for dev in fsdp_devs + seq_devs:
         pl.semaphore_signal(barrier, inc=1, device_id=dev, device_id_type=pl.DeviceIdType.MESH)
+
+    loads = []
+    pairs = (
+        (vec_in, vec), (kvb_in, kvb), (kw_in, kw), (qw_in, qw), (ow_in, ow),
+        (x_in, x), (cot_in, cot), (uw_in, uw), (dw_in, dw),
+    )
+    for i, (source, target) in enumerate(pairs):
+        copy = pltpu.make_async_copy(source, target, load_sems.at[i])
+        copy.start()
+        loads.append(copy)
+    for copy in loads:
+        copy.wait()
 
     vsq[...] = jnp.zeros((128, 128), F32)
     vsq[0:11, 0:24] = vec[...]
@@ -566,10 +600,9 @@
     C[f] = cot[...]
 
     pl.semaphore_wait(barrier, 10)
-    start(w_z[1], w_z[2], w_z[3], w_y[0])
-    start(o_x, q_z[1], q_z[2], q_z[3], q_y[0])
-    start(o_z[1], o_z[2], o_z[3], o_y[0])
-    start(*u_f)
+    start(w_z[3], w_z[2], w_z[1], w_y[0])
+    start(o_x, q_z[3], q_z[2], q_z[1], q_y[0])
+    start(o_z[3], o_z[2], o_z[1], o_y[0])
 
     hat, scale = normalise(x[...].astype(F32))
     hat1[...] = hat
@@ -600,34 +633,24 @@
         down = pltpu.roll(block, 8, 1)
         return block * cos_t + up * low_t - down * high_t
 
-    for k in far:
-        arrive(w_z[k])
-        start(w_y[k])
+    def forward(to_z, to_y, *which):
+        for k in which:
+            arrive(to_z[k])
+            start(to_y[k])
+
+    forward(w_z, w_y, *far)
     start(w_x[0], w_c[0])
     arrive(o_x)
-    start(p_z[1], p_z[2], p_z[3], p_y[0])
-    for k in far:
-        arrive(q_z[k])
-        start(q_y[k])
-    start(q_x[0], q_c[0])
+    start(p_z[3], p_z[2], p_z[1], p_y[0])
     arrive(*w_y)
     start(w_x[1], w_c[1])
-    for k in far:
-        arrive(o_z[k])
-        start(o_y[k])
-    start(o_c[0])
+    forward(q_z, q_y, *far)
+    start(q_x[0], q_c[0])
     arrive(w_x[0])
     start(w_xc[0])
     arrive(w_x[1])
     start(w_xc[1])
-    for k in far:
-        arrive(p_z[k])
-        start(p_y[k])
-    start(p_c[0])
-    arrive(*q_y)
-    start(q_x[1], q_c[1])
     arrive(*w_c, *w_xc)
-
     slabs = [KW[g, i, j].astype(F32) for g in range(4) for i in range(4) for j in range(2)]
     for i in range(16):
         pair = jnp.concatenate([slabs[2 * i][:, :128], slabs[2 * i + 1][:, :128]], 0)
@@ -638,11 +661,17 @@
     n1[...] = (hat * gains[0:1, :] + gains[1:2, :]).astype(BF16)
     kv_pre = dot_nn(n1[...], WKV[...]) + kv_shift
     KV[z, y] = turn(kv_pre, key_cos, key_low, key_high).astype(BF16)
-    start(k_z[1], k_z[2], k_z[3], k_y[0])
+    start(k_z[3], k_z[2], k_z[1], k_y[0])
+    for k in range(4):
+        arrive(q_y[k])
+        start(q_xs[k])
+    start(q_c[1])
+    forward(o_z, o_y, *far)
+    start(o_c[0])
+    forward(p_z, p_y, *far)
+    start(op_c[0])
     arrive(q_x[0])
     start(q_xc[0])
-    arrive(*u_f)
-    start(d_z[1], d_z[2], d_z[3], d_y[0])
     vg[...] = jnp.zeros((128, D), F32)
     csum = jnp.sum(cot[...].astype(F32), 0, keepdims=True)
     vg[5:6, :] = csum
@@ -654,17 +683,17 @@
             key_iota + span[0, i] * tok <= row_iota, 0.0, MASKED
         ).astype(F32)
     dkv[...] = jnp.zeros((8 * tok, 128), F32)
+    start(*u_f)
+    forward(k_z, k_y, *far)
+    arrive(*q_xs)
+    start(q_xc[1])
     arrive(*o_y)
     start(o_c[1])
     arrive(*p_y)
-    start(p_c[1])
-    for k in far:
-        arrive(k_z[k])
-        start(k_y[k])
-    arrive(q_x[1])
-    start(q_xc[1])
+    start(op_c[1])
+    arrive(*u_f)
     start(x_x, c_x, x_c, c_c)
-    start(u_z[1], u_z[2], u_z[3], u_y[0])
+    start(u_z[3], u_z[2], u_z[1], u_y[0])
     arrive(*q_c, *q_xc)
 
     def join(ref, whole):
@@ -686,7 +715,7 @@
         turned = (turned * HD ** (-0.5)).astype(BF16)
         qz[2 * j] = jnp.concatenate([turned[:, :64], gap], 1)
         qz[2 * j + 1] = jnp.concatenate([turned[:, 64:], gap], 1)
-    arrive(*o_c, *p_c)
+    arrive(*o_c, *op_c)
     join(O, WO)
     mixed_back = dot_nt(cot[...], WO[...]).astype(BF16)
     for j in range(6):
@@ -698,49 +727,71 @@
     KVF = KV.reshape(8 * tok, 128)
     kvT[...] = KVF[...].astype(F32).T.astype(BF16)
 
+    span_rows = 2 * tok
+    chunks = 8 * tok // span_rows
+
+    def fold(values, reduce):
+        return reduce(values.reshape(span_rows // 8, 8, tok), axis=0)
+
     def attend(step_index):
         heads = [step_index * 2, step_index * 2 + 1]
-        tops, shares, deltas = [], [], []
-        for j, h in enumerate(heads):
-            top = jnp.full((8, tok), MASKED, F32)
-            for i in range(8):
-                rows = pl.ds(i * tok, tok)
-                held = pl.ds((j * 8 + i) * tok, tok)
-                scores = dot_nt(KVF[rows, :], qz[h]) + bias[rows, :]
-                sbuf[held, :] = scores
-                top = jnp.maximum(top, jnp.max(scores.reshape(tok // 8, 8, tok), axis=0))
-            tops.append(jnp.max(top, axis=0, keepdims=True))
-        for j, h in enumerate(heads):
-            total = jnp.zeros((8, tok), F32)
-            for i in range(8):
-                held = pl.ds((j * 8 + i) * tok, tok)
-                weights = jnp.exp(sbuf[held, :] - tops[j])
-                sbuf[held, :] = weights
-                total = total + jnp.sum(weights.reshape(tok // 8, 8, tok), axis=0)
-            shares.append(1.0 / jnp.sum(total, axis=0, keepdims=True))
-        for j, h in enumerate(heads):
-            acc = jnp.zeros((128, tok), F32)
-            for i in range(8):
-                rows = pl.ds(i * tok, tok)
-                held = pl.ds((j * 8 + i) * tok, tok)
-                probs = sbuf[held, :] * shares[j]
-                probs_low = probs.astype(BF16)
-                sbuf[held, :] = probs
-                acc = acc + dot_nn(kvT[:, rows], probs_low)
-                dkv[rows, :] += dot_nn(probs_low, doz[h])
-            mixed = acc[64:, :]
-            mixT[h] = mixed.astype(BF16)
-            deltas.append(jnp.sum(mixed * doT[h].astype(F32), axis=0, keepdims=True))
-        for j, h in enumerate(heads):
-            acc = jnp.zeros((128, tok), F32)
-            for i in range(8):
-                rows = pl.ds(i * tok, tok)
-                held = pl.ds((j * 8 + i) * tok, tok)
-                prob_grad = dot_nt(KVF[rows, :], doz[h])
-                score_low = (sbuf[held, :] * (prob_grad - deltas[j])).astype(BF16)
-                acc = acc + dot_nn(kvT[:, rows], score_low)
-                dkv[rows, :] += dot_nn(score_low, qz[h])
-            dqT[h] = acc[:64, :] * HD ** (-0.5)
+        top, total, share, delta, acc = {}, {}, {}, {}, {}
+
+        def rows_of(i):
+            return pl.ds(i * span_rows, span_rows)
+
+        def held_of(j, i):
+            return pl.ds((j * chunks + i) * span_rows, span_rows)
+
+        def score(j, i):
+            scores = dot_nt(KVF[rows_of(i), :], qz[heads[j]]) + bias[rows_of(i), :]
+            sbuf[held_of(j, i), :] = scores
+            here = fold(scores, jnp.max)
+            top[j] = here if i == 0 else jnp.maximum(top[j], here)
+            if i == chunks - 1:
+                top[j] = jnp.max(top[j], axis=0, keepdims=True)
+
+        def weigh(j, i):
+            weights = jnp.exp(sbuf[held_of(j, i), :] - top[j])
+            sbuf[held_of(j, i), :] = weights
+            here = fold(weights, jnp.sum)
+            total[j] = here if i == 0 else total[j] + here
+            if i == chunks - 1:
+                share[j] = 1.0 / jnp.sum(total[j], axis=0, keepdims=True)
+
+        def mix(j, i):
+            rows = rows_of(i)
+            probs = sbuf[held_of(j, i), :] * share[j]
+            probs_low = probs.astype(BF16)
+            sbuf[held_of(j, i), :] = probs
+            here = dot_nn(kvT[:, rows], probs_low)
+            acc[j] = here if i == 0 else acc[j] + here
+            dkv[rows, :] += dot_nn(probs_low, doz[heads[j]])
+            if i == chunks - 1:
+                mixed = acc[j][64:, :]
+                mixT[heads[j]] = mixed.astype(BF16)
+                delta[j] = jnp.sum(mixed * doT[heads[j]].astype(F32), axis=0, keepdims=True)
+
+        def back(j, i):
+            rows = rows_of(i)
+            prob_grad = dot_nt(KVF[rows, :], doz[heads[j]])
+            score_low = (sbuf[held_of(j, i), :] * (prob_grad - delta[j])).astype(BF16)
+            here = dot_nn(kvT[:, rows], score_low)
+            acc[j] = here if i == 0 else acc[j] + here
+            dkv[rows, :] += dot_nn(score_low, qz[heads[j]])
+            if i == chunks - 1:
+                dqT[heads[j]] = acc[j][:64, :] * HD ** (-0.5)
+
+        for stage in (
+            ((score, 0),),
+            ((weigh, 0), (score, 1)),
+            ((mix, 0), (weigh, 1)),
+            ((back, 0), (mix, 1)),
+            ((back, 1),),
+        ):
+            for i in range(chunks):
+                for part, j in stage:
+                    part(j, i)
 
     def attend_all(first, last, meanwhile):
         def body_step(step_index, carry):
@@ -751,72 +802,110 @@
 
         lax.fori_loop(first, last, body_step, 0)
 
-    def down_on():
-        for k in far:
-            arrive(d_z[k])
-            start(d_y[k])
-
-    def up_on():
-        for k in far:
-            arrive(u_z[k])
-            start(u_y[k])
+
+    def pump_one():
+        start(d_z[3], d_z[2], d_z[1], d_y[0])
+
+    def pump_two():
+        forward(u_z, u_y, 3)
         arrive(x_x)
         start(x_xc)
 
-    def back_on():
+    def pump_three():
+        forward(u_z, u_y, 2, 1)
+
+    def pump_four():
+        forward(d_z, d_y, 3)
         arrive(c_x)
         start(c_xc)
 
-    attend_all(0, 3, ((0, down_on), (1, up_on), (2, back_on)))
-    arrive(*d_y, *u_y, x_c, x_xc, c_c, c_xc)
-
-    for g in range(4):
+    def pump_five():
+        forward(d_z, d_y, 2)
+
+    attend_all(
+        0, HQ // 2,
+        ((0, pump_one), (2, pump_two), (3, pump_three), (4, pump_four), (5, pump_five)),
+    )
+
+    for k in (3, 2, 1, 0):
+        rows = pl.ds(pl.multiple_of((2 * zk[k] + yo) * tok, 8), tok)
+        SK1[zk[k]] = dkv[rows, :].astype(BF16)
+        start(rk1[k])
+    mix_low = mixT.reshape(D, tok)[...]
+    for c in range(3):
+        sbuf[(3 + c) * D : (4 + c) * D, :] = dot_nn(mix_low, cot[:, c * 256 : c * 256 + 256])
+    GQ = Panels(sbuf, D, 0, 3)
+    GO = Panels(sbuf, D, 3, 3)
+
+    def scatter_c(G, S1, copy):
+        def put(i, carry):
+            for j, g in enumerate((fc, fd)):
+                S1[j, i] = G.get(g, i).astype(S1.dtype)
+            return carry
+
+        lax.fori_loop(0, 8, put, 0)
+        start(copy)
+
+    def scatter_x(G, R1, S2, copies_):
+        arrive(copies_[0])
+        for j, yy in enumerate((yo, y)):
+            for i in range(4):
+                slab = 2 * i + yy
+                S2[j, i] = (G.get(fx, slab) + R1[1, slab].astype(F32)).astype(S2.dtype)
+                G.put(f, slab, G.get(f, slab) + R1[0, slab].astype(F32))
+            start(copies_[1][j])
+
+    def scatter_y(G, R2, S3, copies_):
+        arrive(copies_[1][0])
         for i in range(4):
-            pair = jnp.concatenate([U[i, j, g].astype(F32) for j in range(2)], 0)
-            WU[(g * 4 + i) * 48 : (g * 4 + i + 1) * 48, :] = pair.astype(BF16)
-    WD = Dn.reshape(D, D)
-    up_bias = gains[pl.ds(7 + f, 1), :]
-
-    def token_block(t, carry):
-        two_gain, two_shift, up_sum = carry
-        rows = pl.ds(pl.multiple_of(t * tok, tok), tok)
-        hat2, _ = normalise(X[t].astype(F32))
-        low2 = (hat2 * gains[2:3, :] + gains[3:4, :]).astype(BF16)
-        N2[rows, :] = low2
-        back = C[t]
-        sums = []
-        for c in range(3):
-            units = slice(c * 256, c * 256 + 256)
-            lifted = dot_nn(low2, WU[:, units]) + up_bias[:, units]
-            active_grad = dot_nt(back, WD[units, :])
-            half = 0.5 + 0.5 * lax.erf(lifted * (0.5**0.5))
-            act[rows, units] = (lifted * half).astype(BF16)
-            bell = jnp.exp(lifted * lifted * -0.5) * (1.0 / math.sqrt(2.0 * math.pi))
-            low = ((half + lifted * bell) * active_grad).astype(BF16)
-            dl[rows, units] = low
-            sums.append(jnp.sum(low.astype(F32), 0, keepdims=True))
-        OP[t] = dot_nn(act[rows, :], WD[...]).astype(BF16)
-        grad2 = dot_nt(dl[rows, :], WU[...])
-        NP[t] = grad2.astype(BF16)
-        return (
-            two_gain + jnp.sum(grad2 * hat2, 0, keepdims=True),
-            two_shift + jnp.sum(grad2, 0, keepdims=True),
-            up_sum + jnp.concatenate(sums, 1),
+            S3[i] = (G.get(f, 2 * i + yo) + R2[0, i].astype(F32)).astype(S3.dtype)
+        start(copies_[2])
+
+    def scatter_z(G, R2, R3, S4, copies_):
+        arrive(copies_[1][1], copies_[2])
+        for k in far:
+            total = G.get(f, 2 * zk[k] + y) + R2[1, zk[k]].astype(F32) + R3[zk[k]].astype(F32)
+            S4[k - 1] = total.astype(S4.dtype)
+            start(copies_[3][k - 1])
+
+    def scatter_end(G, R2, R3, R4, copies_):
+        total = G.get(f, 2 * z + y) + R2[1, z].astype(F32) + R3[z].astype(F32)
+        for k in range(3):
+            arrive(copies_[3][k])
+            total = total + R4[k].astype(F32)
+        return total
+
+    scatter_c(GO, SO1, o_sc[0])
+    q_back = dqT.reshape(D, tok)[...].T
+    parts = []
+    for j in range(6):
+        parts.append(
+            turn_back(q_back[:, j * 128 : j * 128 + 128], cosine, sine_low, sine_high).astype(BF16)
         )
-
-    zero_row = jnp.zeros((1, D), F32)
-    two_gain, two_shift, up_sum = lax.fori_loop(0, 4, token_block, (zero_row,) * 3)
-    vg[2:3, :] = two_gain
-    vg[3:4, :] = two_shift
-    vg[pl.ds(7 + f, 1), :] = up_sum
-    start(*out_c, *nrm_c)
-    CF = C.reshape(4 * tok, D)
+    q_low = jnp.concatenate(parts, 1)
+    vg[4:5, :] = jnp.sum(q_low.astype(F32), 0, keepdims=True)
     for c in range(3):
-        units = slice(c * 256, c * 256 + 256)
-        GD[units, :] = dot_tn(act[:, units], CF[...])
-    for k in (1, 2, 3, 0):
-        SD1[zk[k]] = GD[pl.ds(pl.multiple_of((zk[k] * 2 + yo) * 96, 8), 96), :].astype(BF16)
-        start(sd_y[k])
+        sbuf[c * D : (c + 1) * D, :] = dot_tn(n1[...], q_low[:, c * 256 : c * 256 + 256])
+    scatter_c(GQ, SQ1, q_sc[0])
+    forward(d_z, d_y, 1)
+    arrive(*u_y, x_c, x_xc)
+
+    def pair_step(k):
+        arrive(rk1[k])
+        rows = pl.ds(pl.multiple_of((2 * zk[k] + y) * tok, 8), tok)
+        SK2[k - 1] = (dkv[rows, :] + RK1[zk[k]].astype(F32)).astype(BF16)
+        start(rk2[k - 1])
+
+    def lift_one():
+        pair_step(3)
+
+    def lift_two():
+        pair_step(2)
+        scatter_x(GO, QO1, SO2b, o_sc)
+
+    def lift_three():
+        pair_step(1)
+        scatter_x(GQ, RQ1, SQ2, q_sc)
 
     def tokens_to_x():
         arrive(*out_c, *nrm_c)
@@ -847,94 +936,104 @@
         if k:
             start(su_z[k - 1])
 
-    def down_rest():
+    up_totals = []
+
+    def up_end():
+        arrive(*su_z)
+        for g in range(4):
+            total = GU[slab_rows(g, s), :]
+            for k in range(3):
+                total = total + RU2[k, g].astype(F32)
+            up_totals.append(total)
+            g_up[g] = total
+            SU3[g] = total.astype(BF16)
+        start(*su_f)
+
+    for g in range(4):
+        for i in range(4):
+            pair = jnp.concatenate([U[i, j, g].astype(F32) for j in range(2)], 0)
+            WU[(g * 4 + i) * 48 : (g * 4 + i + 1) * 48, :] = pair.astype(BF16)
+    WD = Dn.reshape(D, D)
+    up_bias = gains[pl.ds(7 + f, 1), :]
+
+    def slope_rows(c, t):
+        return pl.ds(pl.multiple_of(c * 4 * tok + t * tok, tok), tok)
+
+    def lift_block(t, carry):
+        for at, action in ((1, lift_one), (2, lift_two), (3, lift_three)):
+            pl.when(t == at)(action)
+        rows = pl.ds(pl.multiple_of(t * tok, tok), tok)
+        hat2, _ = normalise(X[t].astype(F32))
+        low2 = (hat2 * gains[2:3, :] + gains[3:4, :]).astype(BF16)
+        N2[rows, :] = low2
+        for c in range(3):
+            units = slice(c * 256, c * 256 + 256)
+            lifted = dot_nn(low2, WU[:, units]) + up_bias[:, units]
+            half = 0.5 + 0.5 * lax.erf(lifted * (0.5**0.5))
+            act[rows, units] = (lifted * half).astype(BF16)
+            bell = jnp.exp(lifted * lifted * -0.5) * (1.0 / math.sqrt(2.0 * math.pi))
+            bias[slope_rows(c, t), :] = half + lifted * bell
+        return carry
+
+    lax.fori_loop(0, 4, lift_block, 0)
+    arrive(c_c, c_xc)
+    CF = C.reshape(4 * tok, D)
+    for c in range(3):
+        units = slice(c * 256, c * 256 + 256)
+        GD[units, :] = dot_tn(act[:, units], CF[...])
+    for k in (3, 2, 1, 0):
+        SD1[zk[k]] = GD[pl.ds(pl.multiple_of((zk[k] * 2 + yo) * 96, 8), 96), :].astype(BF16)
+        start(sd_y[k])
+    arrive(*d_y)
+
+    def back_one():
+        scatter_y(GO, RO2b, SO3, o_sc)
+
+    def back_two():
         down_step(3)
-        down_step(0)
-
-    attend_all(
-        3, HQ // 2,
-        ((3, tokens_to_x), (4, lambda: down_step(1)), (4, lambda: down_step(2)), (5, down_rest)),
-    )
-
-    for zz in range(4):
-        SK1[zz] = dkv[pl.ds(pl.multiple_of((2 * zz + yo) * tok, 8), tok), :].astype(BF16)
-    start(rk1)
-    mix_low = mixT.reshape(D, tok)[...]
-    for c in range(3):
-        sbuf[(3 + c) * D : (4 + c) * D, :] = dot_nn(mix_low, cot[:, c * 256 : c * 256 + 256])
-    q_back = dqT.reshape(D, tok)[...].T
-    parts = []
-    for j in range(6):
-        parts.append(
-            turn_back(q_back[:, j * 128 : j * 128 + 128], cosine, sine_low, sine_high).astype(BF16)
+
+    def back_three():
+        scatter_y(GQ, RQ2, SQ3, q_sc)
+
+    def back_block(t, carry):
+        for at, action in ((1, back_one), (2, back_two), (3, back_three)):
+            pl.when(t == at)(action)
+        two_gain, two_shift, up_sum = carry
+        rows = pl.ds(pl.multiple_of(t * tok, tok), tok)
+        back = C[t]
+        sums = []
+        for c in range(3):
+            units = slice(c * 256, c * 256 + 256)
+            low = (bias[slope_rows(c, t), :] * dot_nt(back, WD[units, :])).astype(BF16)
+            dl[rows, units] = low
+            sums.append(jnp.sum(low.astype(F32), 0, keepdims=True))
+        OP[t] = dot_nn(act[rows, :], WD[...]).astype(BF16)
+        grad2 = dot_nt(dl[rows, :], WU[...])
+        NP[t] = grad2.astype(BF16)
+        hat2, _ = normalise(X[t].astype(F32))
+        return (
+            two_gain + jnp.sum(grad2 * hat2, 0, keepdims=True),
+            two_shift + jnp.sum(grad2, 0, keepdims=True),
+            up_sum + jnp.concatenate(sums, 1),
         )
-    q_low = jnp.concatenate(parts, 1)
-    vg[4:5, :] = jnp.sum(q_low.astype(F32), 0, keepdims=True)
-    for c in range(3):
-        sbuf[c * D : (c + 1) * D, :] = dot_tn(n1[...], q_low[:, c * 256 : c * 256 + 256])
-    GQ = Panels(sbuf, D)
-    GPP = Panels(GP, D)
-
-    def scatter_c(G, S1, copy):
-        def put(i, carry):
-            for j, g in enumerate((fc, fd)):
-                S1[j, i] = G.get(g, i).astype(S1.dtype)
-            return carry
-
-        lax.fori_loop(0, 8, put, 0)
-        start(copy)
-
-    def scatter_x(G, R1, S2, copies_):
-        arrive(copies_[0])
-
-        def put(i, carry):
-            S2[i] = (G.get(fx, i) + R1[1, i].astype(F32)).astype(S2.dtype)
-            G.put(f, i, G.get(f, i) + R1[0, i].astype(F32))
-            return carry
-
-        lax.fori_loop(0, 8, put, 0)
-        start(copies_[1])
-
-    def scatter_y(G, R2, S3, copies_):
-        arrive(copies_[1])
-
-        def put(i, carry):
-            S3[i] = (G.get(f, 2 * i + yo) + R2[2 * i + yo].astype(F32)).astype(S3.dtype)
-            G.put(f, 2 * i + y, G.get(f, 2 * i + y) + R2[2 * i + y].astype(F32))
-            return carry
-
-        lax.fori_loop(0, 4, put, 0)
-        start(copies_[2])
-
-    def scatter_z(G, R3, S4, copies_):
-        arrive(copies_[2])
-        for k in far:
-            total = G.get(f, 2 * zk[k] + y) + R3[zk[k]].astype(F32)
-            S4[k - 1] = total.astype(S4.dtype)
-            start(copies_[3][k - 1])
-
-    def scatter_end(G, R3, R4, copies_):
-        total = G.get(f, 2 * z + y) + R3[z].astype(F32)
-        for k in range(3):
-            arrive(copies_[3][k])
-            total = total + R4[k].astype(F32)
-        return total
-
-    scatter_c(GQ, SQ1, q_sc[0])
-    arrive(rk1)
-    for k in far:
-        rows = pl.ds(pl.multiple_of((2 * zk[k] + y) * tok, 8), tok)
-        SK2[k - 1] = (dkv[rows, :] + RK1[zk[k]].astype(F32)).astype(BF16)
-        start(rk2[k - 1])
+
+    zero_row = jnp.zeros((1, D), F32)
+    two_gain, two_shift, up_sum = lax.fori_loop(0, 4, back_block, (zero_row,) * 3)
+    vg[2:3, :] = two_gain
+    vg[3:4, :] = two_shift
+    vg[pl.ds(7 + f, 1), :] = up_sum
+    start(*out_c, *nrm_c)
+    down_step(2)
     for c in range(3):
         units = slice(c * 256, c * 256 + 256)
         GU[units, :] = dot_tn(N2[:, units], dl[...])
-    for k in (1, 2, 3, 0):
+    for k in (3, 2, 1, 0):
         for g in range(4):
             SU1[zk[k], g] = GU[slab_rows(g, zk[k] * 2 + yo), :].astype(BF16)
         start(su_y[k])
-    scatter_x(GQ, RQ1, SQ2, q_sc)
+    down_step(1)
     grad1 = dot_nt(q_low, WQ[...])
+    arrive(rk1[0])
     kv_back = dkv[pl.ds(pl.multiple_of((2 * z + y) * tok, 8), tok), :] + RK1[z].astype(F32)
     for k in range(3):
         arrive(rk2[k])
@@ -949,22 +1048,44 @@
         [part for i in range(8) for part in (kv_sum[:, i * 16 : i * 16 + 16], short)], 1
     )
     vg[11:12, :] = jnp.concatenate([spread] * 4, 1)
-    GP[:, :128] = dot_tn(n1[...], kv_low)
-    GP[:, 128:] = vg[...].T
-    scatter_c(GPP, SP1, p_sc[0])
+    GP[...] = dot_tn(n1[...], kv_low)
+    flipped = vg[...].T
+
+    def packed(g):
+        parts = [flipped[(g * 8 + i) * 24 : (g * 8 + i + 1) * 24, :16] for i in range(8)]
+        return jnp.concatenate(parts, 1)
+
+    for g in range(4):
+        GV[g] = packed(g)
+    for i in range(8):
+        for j, g in enumerate((fc, fd)):
+            SP1[j, i] = GP[slab_rows(g, i), :].astype(BF16)
+    for j, g in enumerate((fc, fd)):
+        SV1[j] = GV[g]
+    start(p_c, v_c)
+    down_step(0)
+    arrive(p_c, v_c)
+    for i in range(8):
+        SP2[i] = (GP[slab_rows(fx, i), :] + RP1[1, i].astype(F32)).astype(BF16)
+    SV2[...] = GV[fx] + RV1[1]
+    start(p_x, v_x)
+    tokens_to_x()
+    scatter_z(GO, RO2b, RO3, SO4, o_sc)
+    arrive(p_x, v_x)
+
+    def kv_sum_of(slab):
+        return GP[slab_rows(f, slab), :] + RP1[0, slab].astype(F32) + RP2[slab].astype(F32)
+
+    seq_slabs = [2 * zk[k] + y for k in (1, 2, 3)] + [2 * zk[k] + yo for k in range(4)]
+    for i, slab in enumerate(seq_slabs):
+        SP3[i] = kv_sum_of(slab).astype(BF16)
+    SV3[...] = GV[f] + RV1[0] + RV2[...]
+    start(*p_s, *v_s)
+    up_step(3)
+    scatter_z(GQ, RQ2, RQ3, SQ4, q_sc)
+    up_step(2)
     up_step(1)
-
-    rows = pl.ds(pl.multiple_of(s * 96, 8), 96)
-    down_grad = GD[rows, :]
-    for k in range(3):
-        arrive(sd_z[k])
-        down_grad = down_grad + RD2[k].astype(F32)
-    g_dn[...] = down_grad
-    scatter_x(GPP, RP1, SP2, p_sc)
-    up_step(2)
-    scatter_y(GQ, RQ2, SQ3, q_sc)
-    up_step(3)
-
+    up_step(0)
     mixed_rows = mix_low.astype(F32).T.astype(BF16)
     arrive(out_x)
     bo[...] = (
@@ -972,9 +1093,7 @@
         + (dot_nn(mixed_rows, WO[...]) + gains[5:6, :])
         + (OP[f].astype(F32) + RO1[0].astype(F32) + RO2[...].astype(F32) + gains[6:7, :])
     ).astype(BF16)
-    scatter_y(GPP, RP2, SP3, p_sc)
-    up_step(0)
-    scatter_z(GQ, RQ3, SQ4, q_sc)
+    save(bo, to_bo)
     arrive(nrm_x)
     grad2 = NP[f].astype(F32) + RN1[0].astype(F32) + RN2[...].astype(F32)
     hat_rows = hat1[...]
@@ -984,31 +1103,46 @@
         + norm_back(grad1, hat_rows, scale_rows, gains[0:1, :])
         + norm_back(grad2, hat_rows, scale_rows, gains[2:3, :])
     )
-    scatter_z(GPP, RP3, SP4, p_sc)
-    arrive(*su_z)
-    for g in range(4):
-        total = GU[slab_rows(g, s), :]
-        for k in range(3):
-            total = total + RU2[k, g].astype(F32)
-        g_up[g] = total
-        SU3[g] = total.astype(BF16)
-    start(*su_f)
-    qo_grad = scatter_end(GQ, RQ3, RQ4, q_sc)
-    g_qo[...] = qo_grad
-    vp_grad = scatter_end(GPP, RP3, RP4, p_sc)
-    g_vp[...] = vp_grad
-    for i, g in enumerate((fc, fx, fd)):
-        arrive(su_f[i])
-        g_up[g] = RU3[i].astype(F32)
-
-    def fold(values):
+    save(ig, to_ig)
+    copies.settle()
+    q_grad = scatter_end(GQ, RQ2, RQ3, RQ4, q_sc)
+    g_q[...] = q_grad
+    save(g_q, to_q)
+    o_grad = scatter_end(GO, RO2b, RO3, RO4, o_sc)
+    g_o[...] = o_grad
+    save(g_o, to_o)
+    kv_grad = kv_sum_of(s)
+    vec_sum = SV3[...]
+    for i in range(7):
+        arrive(p_s[i], v_s[i])
+        kv_grad = kv_grad + RP3[i].astype(F32)
+        vec_sum = vec_sum + RV3[i]
+    vec_own = jnp.zeros((24, 16), F32)
+    for i in range(8):
+        vec_own = vec_own + jnp.where(s == i, vec_sum[:, i * 16 : i * 16 + 16], 0.0)
+    vec_grad = jnp.concatenate([vec_own, jnp.zeros((24, 112), F32)], 1)
+    g_kv[...] = kv_grad
+    g_vec[...] = vec_grad
+    save(g_kv, to_kv)
+    save(g_vec, to_vec)
+    rows = pl.ds(pl.multiple_of(s * 96, 8), 96)
+    down_grad = GD[rows, :]
+    for k in range(3):
+        arrive(sd_z[k])
+        down_grad = down_grad + RD2[k].astype(F32)
+    g_dn[...] = down_grad
+    save(g_dn, to_dn)
+    up_end()
+    save(g_up.at[f], to_up.at[f])
+
+    def energy(values):
         return jnp.sum(jnp.sum(values * values, 0, keepdims=True), 1, keepdims=True)
 
-    lanes = lax.broadcasted_iota(jnp.int32, (24, 256), 1)
-    squares = fold(qo_grad) + fold(jnp.where(lanes == 128 + 11, 0.0, vp_grad)) + fold(g_dn[...])
-    for g in range(4):
-        squares = squares + fold(g_up[g])
-    kv_rows = jnp.concatenate([vp_grad[:, 128:], jnp.zeros((104, 128), F32)], 0).T
+    lanes = lax.broadcasted_iota(jnp.int32, (24, 128), 1)
+    squares = energy(q_grad) + energy(o_grad) + energy(kv_grad) + energy(jnp.where(lanes == 11, 0.0, vec_grad)) + energy(g_dn[...])
+    for total in up_totals:
+        squares = squares + energy(total)
+    kv_rows = jnp.concatenate([vec_grad, jnp.zeros((104, 128), F32)], 0).T
     line = lax.broadcasted_iota(jnp.int32, (8, 128), 0)
     column = lax.broadcasted_iota(jnp.int32, (8, 128), 1)
     kv_line = jnp.where(column < 16, jnp.broadcast_to(kv_rows[11:12, :], (8, 128)), 0.0)
@@ -1020,16 +1154,24 @@
     part = chip[0:1, 0:1] + jnp.sum(kv_piece * kv_piece, 1, keepdims=True)
     NS2[s] = jnp.broadcast_to(part, (8, 128))
     start(*n_s)
+    for i, g in enumerate((fc, fx, fd)):
+        arrive(su_f[i])
+        g_up[g] = RU3[i].astype(F32)
+        save(g_up.at[g], to_up.at[g])
     arrive(*n_s)
     everything = NS2[0]
     for i in range(1, 8):
         everything = everything + NS2[i]
     g_small[...] = jnp.where(line == 0, everything, jnp.broadcast_to(kv_piece, (8, 128)))
+    save(g_small, to_small)
     copies.finish()
+    assert len(copies.all) == N_COPIES, len(copies.all)
+    for copy in saved:
+        copy.wait()
 
 
 def update_kernel(
-    small, g_qo, g_vp, g_up, g_dn, bo_in, ig_in,
+    small, g_q, g_o, g_kv, g_vec, g_up, g_dn, bo_in, ig_in,
     mq, mk, mo, mu, md, mv, mb,
     fq, fk, fo, fu, fdn, fv, fb,
     sq, sk, so, su, sd, sv, sb,
@@ -1052,9 +1194,9 @@
             ref[...] = value
 
     rates = (MATRIX_RATE, MATRIX_DECAY)
-    update(g_qo[:, :D], mq[...], fq[...], sq[...], nmq, nfq, nsq, *rates)
-    update(g_qo[:, D:], mo[...], fo[...], so[...], nmo, nfo, nso, *rates)
-    update(g_vp[:, :128], mk[...], fk[...], sk[...], nmk, nfk, nsk, *rates)
+    update(g_q[...], mq[...], fq[...], sq[...], nmq, nfq, nsq, *rates)
+    update(g_o[...], mo[...], fo[...], so[...], nmo, nfo, nso, *rates)
+    update(g_kv[...], mk[...], fk[...], sk[...], nmk, nfk, nsk, *rates)
     for g in range(4):
         cols = slice(g * D, (g + 1) * D)
         update(
@@ -1062,7 +1204,7 @@
             nmu.at[:, cols], nfu.at[:, cols], nsu.at[:, cols], *rates,
         )
     update(g_dn[...], md[...], fdn[...], sd[...], nmd, nfd, nsd, *rates)
-    flipped = jnp.concatenate([g_vp[:, 128:], jnp.zeros((104, 128), F32)], 0).T
+    flipped = jnp.concatenate([g_vec[...], jnp.zeros((104, 128), F32)], 0).T
     vector_grad = flipped[:11, :24]
     update(vector_grad, mv[...], fv[...], sv[...], nmv, nfv, nsv, VECTOR_RATE, 0.0)
     residual[...] = flipped[5:7, :24] * factor
@@ -1075,11 +1217,26 @@
     *moments,
 ):
     tok = inputs.shape[0]
-    vmem = pl.BlockSpec(memory_space=pltpu.VMEM)
     smem = pl.BlockSpec(memory_space=pltpu.SMEM)
     shape = jax.ShapeDtypeStruct
     V = pltpu.VMEM
-    scratch = [
+    results_here = (
+        shape((tok, D), BF16),
+        shape((tok, D), F32),
+        shape((24, D), F32),
+        shape((24, D), F32),
+        shape((24, 128), F32),
+        shape((24, 128), F32),
+        shape((4, 24, D), F32),
+        shape((96, D), F32),
+        shape((8, 128), F32),
+    )
+    operands_here = (
+        inputs, cotangent, query_weight, keyval_weight, output_weight, up_weight, down_weight,
+        vectors, kv_bias.reshape(1, -1),
+    )
+    scratch = [V(a.shape, a.dtype) for a in operands_here + results_here]
+    scratch += [
         V((4, 4, 2, 24, 256), BF16),
         V((4, 4, 2, 24, D), BF16),
         V((4, 4, 2, 24, D), BF16),
@@ -1107,12 +1264,13 @@
         V((HQ, tok, 128), BF16),
         V((HQ, HD, tok), BF16),
         V((128, 8 * tok), BF16),
-        V((8 * tok, tok), F32),
-        V((QO // 256 * D, 256), F32),
+        V((12 * tok, tok), F32),
+        V((6 * D, 256), F32),
         V((HQ, HD, tok), BF16),
         V((HQ, HD, tok), F32),
         V((8 * tok, 128), F32),
-        V((D, 256), F32),
+        V((D, 128), F32),
+        V((4, 24, 128), F32),
         V((D, D), F32),
         V((D, D), F32),
         V((128, D), F32),
@@ -1121,29 +1279,29 @@
         V((2, tok, D), BF16), V((tok, D), BF16), V((tok, D), BF16),
         V((2, tok, D), BF16), V((tok, D), BF16), V((tok, D), BF16),
     ]
-    for width, kind in ((QO, BF16), (256, BF16)):
-        for lead in ((2, 8), (8,), (4,), (3,)):
-            scratch += [V(lead + (24, width), kind)] * 2
+    def scatter_buffers(width):
+        found = []
+        for lead in ((2, 8), (2, 4), (4,), (3,)):
+            found += [V(lead + (24, width), BF16)] * 2
+        return found
+
+    scratch += scatter_buffers(D)
+    scratch += scatter_buffers(D)
+    for lead in ((2, 8), (8,), (7,)):
+        scratch += [V(lead + (24, 128), BF16)] * 2
+    scratch += [V((2, 24, 128), F32)] * 2 + [V((24, 128), F32)] * 3 + [V((7, 24, 128), F32)]
     scratch += [V((4, 4, 24, D), BF16)] * 2 + [V((3, 4, 24, D), BF16)] * 2
     scratch += [V((4, 24, D), BF16), V((3, 24, D), BF16)]
     scratch += [V((4, 96, D), BF16)] * 2 + [V((3, 96, D), BF16)] * 2
     scratch += [V((4, 8, 128), F32), V((8, 8, 128), F32)]
-    scratch += [pltpu.SemaphoreType.DMA((N_COPIES,))] * 2
+    scratch += [pltpu.SemaphoreType.DMA((N_COPIES,))] * 2 + [pltpu.SemaphoreType.DMA((12,)), pltpu.SemaphoreType.DMA((9,))]
     kv_row = kv_bias.reshape(1, -1)
-    bo, ig, g_qo, g_vp, g_up, g_dn, small = pl.pallas_call(
+    bo, ig, g_q, g_o, g_kv, g_vec, g_up, g_dn, small = pl.pallas_call(
         layer_kernel,
         name="layer",
-        out_shape=(
-            shape((tok, D), BF16),
-            shape((tok, D), F32),
-            shape((24, QO), F32),
-            shape((24, 256), F32),
-            shape((4, 24, D), F32),
-            shape((96, D), F32),
-            shape((8, 128), F32),
-        ),
-        in_specs=[smem] + [vmem] * 9,
-        out_specs=(vmem,) * 7,
+        out_shape=results_here,
+        in_specs=[smem] + [pl.BlockSpec(memory_space=pl.ANY)] * 9,
+        out_specs=(pl.BlockSpec(memory_space=pl.ANY),) * 9,
         scratch_shapes=scratch,
         compiler_params=pltpu.CompilerParams(
             collective_id=0, has_side_effects=True, vmem_limit_bytes=62 * 2**20
@@ -1156,7 +1314,7 @@
     firsts = tuple(moments[:6]) + (moments[6].reshape(1, -1),)
     seconds = tuple(moments[7:13]) + (moments[13].reshape(1, -1),)
     state = [shape(a.shape, F32) for a in masters]
-    operands = (small, g_qo, g_vp, g_up, g_dn, bo, ig) + masters + firsts + seconds
+    operands = (small, g_q, g_o, g_kv, g_vec, g_up, g_dn, bo, ig) + masters + firsts + seconds
     outcomes = [shape((tok, D), BF16), shape((tok, D), F32), shape((1, 1), F32)]
     outcomes += state * 3 + [shape((2, vectors.shape[1]), F32)]
 

time: 147 us -> 127 us (0.86)
  Pallas kernels: 146 us -> 126 us
    pallas_call x1, Pallas kernels: 142 us -> 122 us  [fast_body(): pl.pallas_call(layer_kernel, name='layer', out_shape=results_here, in_spe...]
where the time goes in v3:
time: 127 us
  Pallas kernels  126 us (99%)
    pallas_call x1, Pallas kernels, fast_body(): pl.pallas_call(layer_kernel, name='layer', out_shape=results_here, in_spe...  122 us
    pallas_call x1, Pallas kernels, fast_body(): pl.pallas_call(update_kernel, name='update', grid=(1,), out_shape=outcome...  4.27 us

profile of v3, /device:TPU:0, one launch (start us, length us, event | category | flops | bytes accessed | tf_op | source)
XLA Modules:
  0.0 126.7 jit_solution(16537764930703893073)
XLA Ops:
  0.7 121.6 %layer.1 = (bf16[256,768]{1,0:T(8,128)(2,1)}, f32[256,768]{1,0:T(8,128)}, f32[24,768]{1,0:T(8,128)}, f32[24,768]{1,0:T(8,128)}, f32[24,128]{1,0:T(8,128)}, /*ind...) custom-call(s32[1,8]{1,0:T(1,128)} %span.1, bf16[256,768]{1,0:T(8,128)(2,1)} %x_in.1, ...), custom_call_target="tpu_custom_call" | custom-call | tf_op jit(solution)/shard_map/layer/pallas_call | solution.py:1299
  122.2 4.3 %update.1 = (bf16[256,768]{1,0:T(8,128)(2,1)}, f32[256,768]{1,0:T(8,128)}, f32[1,1]{1,0:T(1,128)}, f32[24,768]{1,0:T(8,128)}, f32[24,128]{1,0:T(8,128)}, /*index...) custom-call(f32[8,128]{1,0:T(8,128)} %get-tuple-element.59.small, ...), custom_call_target="tpu_custom_call" | custom-call | tf_op jit(solution)/shard_map/update/pallas_call | solution.py:1324

commit v4 on v3

--- a/solution.py
+++ b/solution.py
@@ -376,28 +376,36 @@
     )
 
 
+def where(condition, action):
+    if condition is None:
+        action()
+    else:
+        pl.when(condition)(lambda: action())
+
+
 class Copy:
-    def __init__(self, copy):
-        self.copy, self.started, self.received, self.sent = copy, False, False, False
+    def __init__(self, copy, send_if, recv_if):
+        self.copy, self.send_if, self.recv_if = copy, send_if, recv_if
+        self.started = self.received = self.sent = False
 
     def start(self):
         self.started = True
-        self.copy.start()
+        where(self.send_if, self.copy.start)
 
     def wait_recv(self):
         self.received = True
-        self.copy.wait_recv()
+        where(self.recv_if, self.copy.wait_recv)
 
     def wait_send(self):
         self.sent = True
-        self.copy.wait_send()
+        where(self.send_if, self.copy.wait_send)
 
 
 class Copies:
     def __init__(self, send_sems, recv_sems):
         self.send_sems, self.recv_sems, self.all = send_sems, recv_sems, []
 
-    def make(self, source, target, device):
+    def make(self, source, target, device, send_if=None, recv_if=None):
         index = len(self.all)
         copy = Copy(pltpu.make_async_remote_copy(
             src_ref=source,
@@ -406,7 +414,7 @@
             recv_sem=self.recv_sems.at[index],
             device_id=device,
             device_id_type=pl.DeviceIdType.MESH,
-        ))
+        ), send_if, recv_if)
         self.all.append(copy)
         return copy
 
@@ -442,7 +450,7 @@
             self.ref[self.rows(p, block, index), :] = value[:, p * 256 : p * 256 + 256]
 
 
-N_COPIES = 151
+N_COPIES = 153
 
 
 def layer_kernel(
@@ -460,8 +468,8 @@
     SO1, QO1, SO2b, RO2b, SO3, RO3, SO4, RO4,
     SP1, RP1, SP2, RP2, SP3, RP3,
     SV1, RV1, SV2, RV2, SV3, RV3,
-    SU1, RU1, SU2, RU2, SU3, RU3,
-    SD1, RD1, SD2, RD2,
+    SU1, RU1, SU2, RU2, SU3, RU3, RXU,
+    SD1, RD1, SD2, RD2, RXD,
     NS1, NS2,
     send_sems, recv_sems, save_sems, load_sems,
 ):
@@ -562,10 +570,18 @@
     v_s = [make(SV3, RV3.at[i], dev) for i, dev in enumerate(seq_devs)]
     o_sc = full_scatter(SO1, QO1, SO2b, RO2b, SO3, RO3, SO4, RO4)
     su_y = [make(SU1.at[zz], RU1.at[zz], dev_y) for zz in zk]
-    su_z = [make(SU2.at[k], RU2.at[k], dev_z[k + 1]) for k in range(3)]
+    inner = lax.div(z + 1, 2) == 1
+    outer = lax.div(z + 1, 2) != 1
+
+    def relayed(S2, R2, RX):
+        to_z = [make(S2.at[k], R2.at[k], dev_z[k + 1]) for k in range(2)]
+        to_z.append(make(S2.at[2], R2.at[2], dev_z[3], inner, inner))
+        return to_z, make(S2.at[2], RX, dev_z[1], outer, inner)
+
+    su_z, su_r = relayed(SU2, RU2, RXU)
     su_f = [make(SU3.at[g], RU3.at[i], dev) for i, (g, dev) in enumerate(zip((fc, fx, fd), fsdp_devs))]
     sd_y = [make(SD1.at[zz], RD1.at[zz], dev_y) for zz in zk]
-    sd_z = [make(SD2.at[k], RD2.at[k], dev_z[k + 1]) for k in range(3)]
+    sd_z, sd_r = relayed(SD2, RD2, RXD)
     n_f = [make(NS1.at[f], NS1.at[f], dev) for dev in fsdp_devs]
     n_s = [make(NS2.at[s], NS2.at[s], dev) for dev in seq_devs]
 
@@ -598,6 +614,11 @@
     Dn[z, y] = dw[...].astype(BF16)
     X[f] = x[...]
     C[f] = cot[...]
+
+    @pl.when(outer)
+    def _():
+        RU2[2] = jnp.zeros((4, 24, D), BF16)
+        RD2[2] = jnp.zeros((96, D), BF16)
 
     pl.semaphore_wait(barrier, 10)
     start(w_z[3], w_z[2], w_z[1], w_y[0])
@@ -692,8 +713,8 @@
     arrive(*p_y)
     start(op_c[1])
     arrive(*u_f)
+    start(u_z[3], u_z[2], u_z[1], u_y[0])
     start(x_x, c_x, x_c, c_c)
-    start(u_z[3], u_z[2], u_z[1], u_y[0])
     arrive(*q_c, *q_xc)
 
     def join(ref, whole):
@@ -803,28 +824,26 @@
         lax.fori_loop(first, last, body_step, 0)
 
 
-    def pump_one():
-        start(d_z[3], d_z[2], d_z[1], d_y[0])
-
     def pump_two():
-        forward(u_z, u_y, 3)
-        arrive(x_x)
-        start(x_xc)
+        forward(u_z, u_y, 1)
 
     def pump_three():
-        forward(u_z, u_y, 2, 1)
+        forward(u_z, u_y, 3, 2)
 
     def pump_four():
+        forward(d_z, d_y, 1)
+        arrive(x_x, c_x)
+        start(x_xc, c_xc)
+
+    def pump_five():
         forward(d_z, d_y, 3)
-        arrive(c_x)
-        start(c_xc)
-
-    def pump_five():
-        forward(d_z, d_y, 2)
 
     attend_all(
         0, HQ // 2,
-        ((0, pump_one), (2, pump_two), (3, pump_three), (4, pump_four), (5, pump_five)),
+        (
+            (1, lambda: start(d_z[3], d_z[2], d_z[1], d_y[0])),
+            (2, pump_two), (3, pump_three), (4, pump_four), (5, pump_five),
+        ),
     )
 
     for k in (3, 2, 1, 0):
@@ -887,7 +906,7 @@
     for c in range(3):
         sbuf[c * D : (c + 1) * D, :] = dot_tn(n1[...], q_low[:, c * 256 : c * 256 + 256])
     scatter_c(GQ, SQ1, q_sc[0])
-    forward(d_z, d_y, 1)
+    forward(d_z, d_y, 2)
     arrive(*u_y, x_c, x_xc)
 
     def pair_step(k):
@@ -914,27 +933,56 @@
         SN2[...] = (NP[fx].astype(F32) + RN1[1].astype(F32)).astype(BF16)
         start(nrm_x)
 
+    def down_rows(k):
+        return pl.ds(pl.multiple_of((zk[k] * 2 + y) * 96, 8), 96)
+
     def down_step(k):
         arrive(sd_y[k])
-        rows = pl.ds(pl.multiple_of((zk[k] * 2 + y) * 96, 8), 96)
-        total = GD[rows, :] + RD1[zk[k]].astype(F32)
+        total = GD[down_rows(k), :] + RD1[zk[k]].astype(F32)
+        if k in (0, 2):
+            GD[down_rows(k), :] = total
         if k:
             SD2[k - 1] = total.astype(BF16)
+        if k == 2:
+            pl.when(outer)(lambda: start(sd_z[1]))
+        elif k:
             start(sd_z[k - 1])
-        else:
-            GD[rows, :] = total
+        if k == 3:
+            start(sd_r)
+
+    def down_relay():
+        arrive(sd_r)
+
+        @pl.when(inner)
+        def _():
+            SD2[1] = (GD[down_rows(2), :] + RXD[...].astype(F32)).astype(BF16)
+            start(sd_z[1])
 
     def up_step(k):
         arrive(su_y[k])
         for g in range(4):
             rows = slab_rows(g, zk[k] * 2 + y)
             total = GU[rows, :] + RU1[zk[k], g].astype(F32)
+            if k in (0, 2):
+                GU[rows, :] = total
             if k:
                 SU2[k - 1, g] = total.astype(BF16)
-            else:
-                GU[rows, :] = total
-        if k:
+        if k == 2:
+            pl.when(outer)(lambda: start(su_z[1]))
+        elif k:
             start(su_z[k - 1])
+        if k == 3:
+            start(su_r)
+
+    def up_relay():
+        arrive(su_r)
+
+        @pl.when(inner)
+        def _():
+            for g in range(4):
+                total = GU[slab_rows(g, zk[2] * 2 + y), :] + RXU[g].astype(F32)
+                SU2[1, g] = total.astype(BF16)
+            start(su_z[1])
 
     up_totals = []
 
@@ -1063,6 +1111,7 @@
     for j, g in enumerate((fc, fd)):
         SV1[j] = GV[g]
     start(p_c, v_c)
+    down_relay()
     down_step(0)
     arrive(p_c, v_c)
     for i in range(8):
@@ -1085,6 +1134,7 @@
     scatter_z(GQ, RQ2, RQ3, SQ4, q_sc)
     up_step(2)
     up_step(1)
+    up_relay()
     up_step(0)
     mixed_rows = mix_low.astype(F32).T.astype(BF16)
     arrive(out_x)
@@ -1291,8 +1341,8 @@
         scratch += [V(lead + (24, 128), BF16)] * 2
     scratch += [V((2, 24, 128), F32)] * 2 + [V((24, 128), F32)] * 3 + [V((7, 24, 128), F32)]
     scratch += [V((4, 4, 24, D), BF16)] * 2 + [V((3, 4, 24, D), BF16)] * 2
-    scratch += [V((4, 24, D), BF16), V((3, 24, D), BF16)]
-    scratch += [V((4, 96, D), BF16)] * 2 + [V((3, 96, D), BF16)] * 2
+    scratch += [V((4, 24, D), BF16), V((3, 24, D), BF16), V((4, 24, D), BF16)]
+    scratch += [V((4, 96, D), BF16)] * 2 + [V((3, 96, D), BF16)] * 2 + [V((96, D), BF16)]
     scratch += [V((4, 8, 128), F32), V((8, 8, 128), F32)]
     scratch += [pltpu.SemaphoreType.DMA((N_COPIES,))] * 2 + [pltpu.SemaphoreType.DMA((12,)), pltpu.SemaphoreType.DMA((9,))]
     kv_row = kv_bias.reshape(1, -1)

time: 127 us -> 124 us (0.976)
  Pallas kernels: 126 us -> 123 us
    pallas_call x1, Pallas kernels: 122 us -> 118 us  [fast_body(): pl.pallas_call(layer_kernel, name='layer', out_shape=results_here, in_spe...]
where the time goes in v4:
time: 124 us
  Pallas kernels  123 us (99%)
    pallas_call x1, Pallas kernels, fast_body(): pl.pallas_call(layer_kernel, name='layer', out_shape=results_here, in_spe...  118 us
    pallas_call x1, Pallas kernels, fast_body(): pl.pallas_call(update_kernel, name='update', grid=(1,), out_shape=outcome...  4.27 us

profile of v4, /device:TPU:0, one launch (start us, length us, event | category | flops | bytes accessed | tf_op | source)
XLA Modules:
  0.0 123.5 jit_solution(9521000553701954215)
XLA Ops:
  0.7 118.4 %layer.1 = (bf16[256,768]{1,0:T(8,128)(2,1)}, f32[256,768]{1,0:T(8,128)}, f32[24,768]{1,0:T(8,128)}, f32[24,768]{1,0:T(8,128)}, f32[24,128]{1,0:T(8,128)}, /*ind...) custom-call(s32[1,8]{1,0:T(1,128)} %span.1, bf16[256,768]{1,0:T(8,128)(2,1)} %x_in.1, ...), custom_call_target="tpu_custom_call" | custom-call | tf_op jit(solution)/shard_map/layer/pallas_call | solution.py:1349
  119.1 4.3 %update.1 = (bf16[256,768]{1,0:T(8,128)(2,1)}, f32[256,768]{1,0:T(8,128)}, f32[1,1]{1,0:T(1,128)}, f32[24,768]{1,0:T(8,128)}, f32[24,128]{1,0:T(8,128)}, /*index...) custom-call(f32[8,128]{1,0:T(8,128)} %get-tuple-element.59.small, ...), custom_call_target="tpu_custom_call" | custom-call | tf_op jit(solution)/shard_map/update/pallas_call | solution.py:1374

commit v5 on v4

--- a/solution.py
+++ b/solution.py
@@ -401,20 +401,54 @@
         where(self.send_if, self.copy.wait_send)
 
 
+class Group:
+    def __init__(self, whole, sem):
+        self.whole, self.sem, self.members, self.waited = whole, sem, [], False
+
+    def wait_recv(self):
+        self.waited = True
+        for copy in self.members:
+            copy.received = True
+        pltpu.make_async_copy(self.whole, self.whole, self.sem).wait()
+
+    def wait_send(self):
+        self.waited = True
+        pltpu.make_async_copy(self.whole, self.whole, self.sem).wait()
+
+
 class Copies:
     def __init__(self, send_sems, recv_sems):
-        self.send_sems, self.recv_sems, self.all = send_sems, recv_sems, []
-
-    def make(self, source, target, device, send_if=None, recv_if=None):
-        index = len(self.all)
+        self.send_sems, self.recv_sems, self.all, self.groups = send_sems, recv_sems, [], []
+        self.sends = self.recvs = 0
+
+    def next_send(self):
+        self.sends += 1
+        return self.send_sems.at[self.sends - 1]
+
+    def next_recv(self):
+        self.recvs += 1
+        return self.recv_sems.at[self.recvs - 1]
+
+    def leaving(self, whole):
+        self.groups.append(Group(whole, self.next_send()))
+        return self.groups[-1]
+
+    def arriving(self, whole):
+        return Group(whole, self.next_recv())
+
+    def make(self, source, target, device, send_if=None, recv_if=None, out=None, into=None):
         copy = Copy(pltpu.make_async_remote_copy(
             src_ref=source,
             dst_ref=target,
-            send_sem=self.send_sems.at[index],
-            recv_sem=self.recv_sems.at[index],
+            send_sem=out.sem if out else self.next_send(),
+            recv_sem=into.sem if into else self.next_recv(),
             device_id=device,
             device_id_type=pl.DeviceIdType.MESH,
         ), send_if, recv_if)
+        copy.sent = out is not None
+        for group in (out, into):
+            if group:
+                group.members.append(copy)
         self.all.append(copy)
         return copy
 
@@ -422,12 +456,9 @@
         for copy in self.all:
             if copy.started and not copy.sent:
                 copy.wait_send()
-
-    def finish(self):
-        for copy in self.all:
-            if copy.started and not copy.received:
-                copy.wait_recv()
-        self.settle()
+        for group in self.groups:
+            if not group.waited and all(copy.started for copy in group.members):
+                group.wait_send()
 
 
 def slab_rows(block, index):
@@ -450,7 +481,7 @@
             self.ref[self.rows(p, block, index), :] = value[:, p * 256 : p * 256 + 256]
 
 
-N_COPIES = 153
+N_SEMS = (54, 93)
 
 
 def layer_kernel(
@@ -509,67 +540,111 @@
         copy.start()
         saved.append(copy)
 
-    def seq_gather(ref):
-        to_z = [None] + [make(ref(z, y), ref(z, y), dev_z[k]) for k in (1, 2, 3)]
-        to_y = [make(ref(zk[k], y), ref(zk[k], y), dev_y) for k in range(4)]
-        return to_z, to_y
-
-    w_z, w_y = seq_gather(lambda i, j: KW.at[f, i, j])
-    q_z, q_y = seq_gather(lambda i, j: Q.at[f, i, j])
-    o_z, o_y = seq_gather(lambda i, j: O.at[f, i, j])
-    p_z, p_y = seq_gather(lambda i, j: O.at[fx, i, j])
-    u_z, u_y = seq_gather(lambda i, j: U.at[i, j])
-    d_z, d_y = seq_gather(lambda i, j: Dn.at[i, j])
-    k_z, k_y = seq_gather(lambda i, j: KV.at[i, j])
-
-    def fsdp_gather(ref):
-        to_x = [make(ref(f, j), ref(f, j), dev_x) for j in (y, yo)]
-        to_c = [make(ref(f, j), ref(f, j), dev_c) for j in (y, yo)]
-        on_c = [make(ref(fx, j), ref(fx, j), dev_c) for j in (y, yo)]
-        return to_x, to_c, on_c
-
-    w_x, w_c, w_xc = fsdp_gather(lambda i, j: KW.at[i, :, j])
-    q_x, q_c, q_xc = fsdp_gather(lambda i, j: Q.at[i, :, j])
-    q_xs = [make(Q.at[f, zz, yo], Q.at[f, zz, yo], dev_x) for zz in zk]
+    leaving, arriving = copies.leaving, copies.arriving
+    three, four = pl.ds(0, 3), pl.ds(0, 4)
+
+    def seq_gather(ref, some, together=True):
+        to_z, to_y = [None], []
+        out = leaving(some(three))
+        for k in (1, 2, 3):
+            to_z.append(make(ref(z, y), ref(z, y), dev_z[k], out=out))
+        out, into = leaving(some(four)), arriving(some(four)) if together else None
+        for k in range(4):
+            to_y.append(make(ref(zk[k], y), ref(zk[k], y), dev_y, out=out, into=into))
+        return to_z, to_y, into
+
+    w_z, w_y, w_yin = seq_gather(lambda i, j: KW.at[f, i, j], lambda n: KW.at[0, n, 0])
+    q_z, q_y, _ = seq_gather(lambda i, j: Q.at[f, i, j], lambda n: Q.at[0, n, 0], False)
+    o_z, o_y, o_yin = seq_gather(lambda i, j: O.at[f, i, j], lambda n: O.at[0, n, 0])
+    p_z, p_y, p_yin = seq_gather(lambda i, j: O.at[fx, i, j], lambda n: O.at[0, n, 0])
+    u_z, u_y, u_yin = seq_gather(lambda i, j: U.at[i, j], lambda n: U.at[n, 0])
+    d_z, d_y, d_yin = seq_gather(lambda i, j: Dn.at[i, j], lambda n: Dn.at[n, 0])
+    k_z, k_y, k_yin = seq_gather(lambda i, j: KV.at[i, j], lambda n: KV.at[n, 0])
+
+    def fsdp_gather(ref, some):
+        out, into = leaving(some(three)), arriving(some(pl.ds(0, 2)))
+        to_x = [make(ref(f, j), ref(f, j), dev_x, out=out) for j in (y, yo)]
+        to_c = [make(ref(f, j), ref(f, j), dev_c, out=out, into=into) for j in (y, yo)]
+        on_c = [make(ref(fx, j), ref(fx, j), dev_c, out=out, into=into) for j in (y, yo)]
+        return to_x, to_c, on_c, into
+
+    w_x, w_c, w_xc, w_in = fsdp_gather(lambda i, j: KW.at[i, :, j], lambda n: KW.at[n])
+    q_out, q_in = leaving(Q.at[three]), arriving(Q.at[pl.ds(0, 2)])
+
+    def q_copy(g, j, device, into):
+        return make(Q.at[g, :, j], Q.at[g, :, j], device, out=q_out, into=into)
+
+    q_x0 = q_copy(f, y, dev_x, None)
+    q_c = [q_copy(f, j, dev_c, q_in) for j in (y, yo)]
+    q_xc = [q_copy(fx, j, dev_c, q_in) for j in (y, yo)]
+    q_xs = [make(Q.at[f, zz, yo], Q.at[f, zz, yo], dev_x, out=q_out) for zz in zk]
     o_x = make(O.at[f, z, y], O.at[f, z, y], dev_x)
-    o_c = [make(O.at[f, :, j], O.at[f, :, j], dev_c) for j in (y, yo)]
-    op_c = [make(O.at[fx, :, j], O.at[fx, :, j], dev_c) for j in (y, yo)]
+    o_out, o_in = leaving(O.at[pl.ds(0, 2)]), arriving(O.at[pl.ds(0, 2)])
+
+    def o_copy(g, j):
+        return make(O.at[g, :, j], O.at[g, :, j], dev_c, out=o_out, into=o_in)
+
+    o_c = [o_copy(f, j) for j in (y, yo)]
+    op_c = [o_copy(fx, j) for j in (y, yo)]
 
     def token_gather(ref):
+        out = leaving(ref.at[three])
         return (
-            make(ref.at[f], ref.at[f], dev_x),
-            make(ref.at[f], ref.at[f], dev_c),
-            make(ref.at[fx], ref.at[fx], dev_c),
+            make(ref.at[f], ref.at[f], dev_x, out=out),
+            make(ref.at[f], ref.at[f], dev_c, out=out),
+            make(ref.at[fx], ref.at[fx], dev_c, out=out),
         )
 
     x_x, x_c, x_xc = token_gather(X)
     c_x, c_c, c_xc = token_gather(C)
-    u_f = [make(ub.at[g], U.at[z, y, f], dev) for g, dev in zip((fc, fx, fd), fsdp_devs)]
-
-    rk1 = [make(SK1.at[zz], RK1.at[zz], dev_y) for zz in zk]
-    rk2 = [make(SK2.at[k], RK2.at[k], dev_z[k + 1]) for k in range(3)]
-    out_c = [make(OP.at[g], RO1.at[i], dev_c) for i, g in enumerate((fc, fd))]
+    uf_out, uf_in = leaving(ub.at[three]), arriving(U.at[0, 0, three])
+    u_f = [
+        make(ub.at[g], U.at[z, y, f], dev, out=uf_out, into=uf_in)
+        for g, dev in zip((fc, fx, fd), fsdp_devs)
+    ]
+
+    out = leaving(SK1)
+    rk1 = [make(SK1.at[zz], RK1.at[zz], dev_y, out=out) for zz in zk]
+
+    def to_z_peers(S, R):
+        out, into = leaving(S), arriving(R)
+        return [make(S.at[k], R.at[k], dev_z[k + 1], out=out, into=into) for k in range(3)], into
+
+    rk2, rk2_in = to_z_peers(SK2, RK2)
+
+    def to_core(ref, R):
+        out, into = leaving(ref.at[pl.ds(0, 2)]), arriving(R)
+        found = [
+            make(ref.at[g], R.at[i], dev_c, out=out, into=into) for i, g in enumerate((fc, fd))
+        ]
+        return found, into
+
+    out_c, out_in = to_core(OP, RO1)
     out_x = make(SO2, RO2, dev_x)
-    nrm_c = [make(NP.at[g], RN1.at[i], dev_c) for i, g in enumerate((fc, fd))]
+    nrm_c, nrm_in = to_core(NP, RN1)
     nrm_x = make(SN2, RN2, dev_x)
 
     def full_scatter(S1, R1, S2, R2, S3, R3, S4, R4):
-        return (
-            make(S1, R1, dev_c),
-            [make(S2.at[i], R2.at[i], dev_x) for i in range(2)],
-            make(S3, R3, dev_y),
-            [make(S4.at[k], R4.at[k], dev_z[k + 1]) for k in range(3)],
-        )
+        c_copy = make(S1, R1, dev_c)
+        out = leaving(S2)
+        x_copies = [make(S2.at[i], R2.at[i], dev_x, out=out) for i in range(2)]
+        y_copy = make(S3, R3, dev_y)
+        return (c_copy, x_copies, y_copy, *to_z_peers(S4, R4))
 
     q_sc = full_scatter(SQ1, RQ1, SQ2, RQ2, SQ3, RQ3, SQ4, RQ4)
+    o_sc = full_scatter(SO1, QO1, SO2b, RO2b, SO3, RO3, SO4, RO4)
     p_c = make(SP1, RP1, dev_c)
     p_x = make(SP2, RP2, dev_x)
-    p_s = [make(SP3.at[i], RP3.at[i], dev) for i, dev in enumerate(seq_devs)]
+    out, p_in = leaving(SP3), arriving(RP3)
+    p_s = [
+        make(SP3.at[i], RP3.at[i], dev, out=out, into=p_in) for i, dev in enumerate(seq_devs)
+    ]
     v_c = make(SV1, RV1, dev_c)
     v_x = make(SV2, RV2, dev_x)
-    v_s = [make(SV3, RV3.at[i], dev) for i, dev in enumerate(seq_devs)]
-    o_sc = full_scatter(SO1, QO1, SO2b, RO2b, SO3, RO3, SO4, RO4)
-    su_y = [make(SU1.at[zz], RU1.at[zz], dev_y) for zz in zk]
+    out, v_in = leaving(RV3), arriving(RV3)
+    v_s = [make(SV3, RV3.at[i], dev, out=out, into=v_in) for i, dev in enumerate(seq_devs)]
+    out = leaving(SU1)
+    su_y = [make(SU1.at[zz], RU1.at[zz], dev_y, out=out) for zz in zk]
     inner = lax.div(z + 1, 2) == 1
     outer = lax.div(z + 1, 2) != 1
 
@@ -579,11 +654,19 @@
         return to_z, make(S2.at[2], RX, dev_z[1], outer, inner)
 
     su_z, su_r = relayed(SU2, RU2, RXU)
-    su_f = [make(SU3.at[g], RU3.at[i], dev) for i, (g, dev) in enumerate(zip((fc, fx, fd), fsdp_devs))]
-    sd_y = [make(SD1.at[zz], RD1.at[zz], dev_y) for zz in zk]
+    out, su_fin = leaving(SU3.at[three]), arriving(RU3)
+    su_f = [
+        make(SU3.at[g], RU3.at[i], dev, out=out, into=su_fin)
+        for i, (g, dev) in enumerate(zip((fc, fx, fd), fsdp_devs))
+    ]
+    out = leaving(SD1)
+    sd_y = [make(SD1.at[zz], RD1.at[zz], dev_y, out=out) for zz in zk]
     sd_z, sd_r = relayed(SD2, RD2, RXD)
-    n_f = [make(NS1.at[f], NS1.at[f], dev) for dev in fsdp_devs]
-    n_s = [make(NS2.at[s], NS2.at[s], dev) for dev in seq_devs]
+    out, nf_in = leaving(NS1.at[three]), arriving(NS1.at[three])
+    n_f = [make(NS1.at[f], NS1.at[f], dev, out=out, into=nf_in) for dev in fsdp_devs]
+    seven = pl.ds(0, 7)
+    out, ns_in = leaving(NS2.at[seven]), arriving(NS2.at[seven])
+    n_s = [make(NS2.at[s], NS2.at[s], dev, out=out, into=ns_in) for dev in seq_devs]
 
     barrier = pltpu.get_barrier_semaphore()
     for dev in fsdp_devs + seq_devs:
@@ -663,15 +746,15 @@
     start(w_x[0], w_c[0])
     arrive(o_x)
     start(p_z[3], p_z[2], p_z[1], p_y[0])
-    arrive(*w_y)
+    arrive(w_yin)
     start(w_x[1], w_c[1])
     forward(q_z, q_y, *far)
-    start(q_x[0], q_c[0])
+    start(q_x0, q_c[0])
     arrive(w_x[0])
     start(w_xc[0])
     arrive(w_x[1])
     start(w_xc[1])
-    arrive(*w_c, *w_xc)
+    arrive(w_in)
     slabs = [KW[g, i, j].astype(F32) for g in range(4) for i in range(4) for j in range(2)]
     for i in range(16):
         pair = jnp.concatenate([slabs[2 * i][:, :128], slabs[2 * i + 1][:, :128]], 0)
@@ -691,7 +774,7 @@
     start(o_c[0])
     forward(p_z, p_y, *far)
     start(op_c[0])
-    arrive(q_x[0])
+    arrive(q_x0)
     start(q_xc[0])
     vg[...] = jnp.zeros((128, D), F32)
     csum = jnp.sum(cot[...].astype(F32), 0, keepdims=True)
@@ -708,14 +791,14 @@
     forward(k_z, k_y, *far)
     arrive(*q_xs)
     start(q_xc[1])
-    arrive(*o_y)
+    arrive(o_yin)
     start(o_c[1])
-    arrive(*p_y)
+    arrive(p_yin)
     start(op_c[1])
-    arrive(*u_f)
+    arrive(uf_in)
     start(u_z[3], u_z[2], u_z[1], u_y[0])
     start(x_x, c_x, x_c, c_c)
-    arrive(*q_c, *q_xc)
+    arrive(q_in)
 
     def join(ref, whole):
         def put(i, carry):
@@ -736,7 +819,7 @@
         turned = (turned * HD ** (-0.5)).astype(BF16)
         qz[2 * j] = jnp.concatenate([turned[:, :64], gap], 1)
         qz[2 * j + 1] = jnp.concatenate([turned[:, 64:], gap], 1)
-    arrive(*o_c, *op_c)
+    arrive(o_in)
     join(O, WO)
     mixed_back = dot_nt(cot[...], WO[...]).astype(BF16)
     for j in range(6):
@@ -744,7 +827,7 @@
         doz[2 * j] = jnp.concatenate([gap, pair[:, :64]], 1)
         doz[2 * j + 1] = jnp.concatenate([gap, pair[:, 64:]], 1)
     doT[...] = mixed_back.astype(F32).T.astype(BF16).reshape(HQ, HD, tok)
-    arrive(*k_y)
+    arrive(k_yin)
     KVF = KV.reshape(8 * tok, 128)
     kvT[...] = KVF[...].astype(F32).T.astype(BF16)
 
@@ -889,8 +972,8 @@
 
     def scatter_end(G, R2, R3, R4, copies_):
         total = G.get(f, 2 * z + y) + R2[1, z].astype(F32) + R3[z].astype(F32)
+        arrive(copies_[4])
         for k in range(3):
-            arrive(copies_[3][k])
             total = total + R4[k].astype(F32)
         return total
 
@@ -907,7 +990,7 @@
         sbuf[c * D : (c + 1) * D, :] = dot_tn(n1[...], q_low[:, c * 256 : c * 256 + 256])
     scatter_c(GQ, SQ1, q_sc[0])
     forward(d_z, d_y, 2)
-    arrive(*u_y, x_c, x_xc)
+    arrive(u_yin, x_c, x_xc)
 
     def pair_step(k):
         arrive(rk1[k])
@@ -927,7 +1010,7 @@
         scatter_x(GQ, RQ1, SQ2, q_sc)
 
     def tokens_to_x():
-        arrive(*out_c, *nrm_c)
+        arrive(out_in, nrm_in)
         SO2[...] = (OP[fx].astype(F32) + RO1[1].astype(F32)).astype(BF16)
         start(out_x)
         SN2[...] = (NP[fx].astype(F32) + RN1[1].astype(F32)).astype(BF16)
@@ -1032,7 +1115,7 @@
     for k in (3, 2, 1, 0):
         SD1[zk[k]] = GD[pl.ds(pl.multiple_of((zk[k] * 2 + yo) * 96, 8), 96), :].astype(BF16)
         start(sd_y[k])
-    arrive(*d_y)
+    arrive(d_yin)
 
     def back_one():
         scatter_y(GO, RO2b, SO3, o_sc)
@@ -1083,8 +1166,8 @@
     grad1 = dot_nt(q_low, WQ[...])
     arrive(rk1[0])
     kv_back = dkv[pl.ds(pl.multiple_of((2 * z + y) * tok, 8), tok), :] + RK1[z].astype(F32)
+    arrive(rk2_in)
     for k in range(3):
-        arrive(rk2[k])
         kv_back = kv_back + RK2[k].astype(F32)
     kv_low = turn_back(kv_back, key_cos, key_low, key_high).astype(BF16)
     grad1 = grad1 + dot_nt(kv_low, WKV[...])
@@ -1163,8 +1246,8 @@
     save(g_o, to_o)
     kv_grad = kv_sum_of(s)
     vec_sum = SV3[...]
+    arrive(p_in, v_in)
     for i in range(7):
-        arrive(p_s[i], v_s[i])
         kv_grad = kv_grad + RP3[i].astype(F32)
         vec_sum = vec_sum + RV3[i]
     vec_own = jnp.zeros((24, 16), F32)
@@ -1198,24 +1281,24 @@
     kv_line = jnp.where(column < 16, jnp.broadcast_to(kv_rows[11:12, :], (8, 128)), 0.0)
     NS1[f] = jnp.where(line == 0, squares, kv_line)
     start(*n_f)
-    arrive(*n_f)
+    arrive(nf_in)
     kv_piece = NS1[0][1:2, :]
     chip = NS1[0] + NS1[1] + NS1[2] + NS1[3]
     part = chip[0:1, 0:1] + jnp.sum(kv_piece * kv_piece, 1, keepdims=True)
     NS2[s] = jnp.broadcast_to(part, (8, 128))
     start(*n_s)
+    arrive(su_fin)
     for i, g in enumerate((fc, fx, fd)):
-        arrive(su_f[i])
         g_up[g] = RU3[i].astype(F32)
         save(g_up.at[g], to_up.at[g])
-    arrive(*n_s)
+    arrive(ns_in)
     everything = NS2[0]
     for i in range(1, 8):
         everything = everything + NS2[i]
     g_small[...] = jnp.where(line == 0, everything, jnp.broadcast_to(kv_piece, (8, 128)))
     save(g_small, to_small)
-    copies.finish()
-    assert len(copies.all) == N_COPIES, len(copies.all)
+    copies.settle()
+    assert (copies.sends, copies.recvs) == N_SEMS, (copies.sends, copies.recvs)
     for copy in saved:
         copy.wait()
 
@@ -1344,7 +1427,7 @@
     scratch += [V((4, 24, D), BF16), V((3, 24, D), BF16), V((4, 24, D), BF16)]
     scratch += [V((4, 96, D), BF16)] * 2 + [V((3, 96, D), BF16)] * 2 + [V((96, D), BF16)]
     scratch += [V((4, 8, 128), F32), V((8, 8, 128), F32)]
-    scratch += [pltpu.SemaphoreType.DMA((N_COPIES,))] * 2 + [pltpu.SemaphoreType.DMA((12,)), pltpu.SemaphoreType.DMA((9,))]
+    scratch += [pltpu.SemaphoreType.DMA((n,)) for n in N_SEMS] + [pltpu.SemaphoreType.DMA((12,)), pltpu.SemaphoreType.DMA((9,))]
     kv_row = kv_bias.reshape(1, -1)
     bo, ig, g_q, g_o, g_kv, g_vec, g_up, g_dn, small = pl.pallas_call(
         layer_kernel,

time: 124 us -> 122 us (0.984)
  Pallas kernels: 123 us -> 121 us
    pallas_call x1, Pallas kernels: 118 us -> 117 us  [fast_body(): pl.pallas_call(layer_kernel, name='layer', out_shape=results_here, in_spe...]
where the time goes in v5:
time: 122 us
  Pallas kernels  121 us (99%)
    pallas_call x1, Pallas kernels, fast_body(): pl.pallas_call(layer_kernel, name='layer', out_shape=results_here, in_spe...  117 us
    pallas_call x1, Pallas kernels, fast_body(): pl.pallas_call(update_kernel, name='update', grid=(1,), out_shape=outcome...  4.27 us

profile of v5, /device:TPU:0, one launch (start us, length us, event | category | flops | bytes accessed | tf_op | source)
XLA Modules:
  0.0 122.1 jit_solution(1998000731950242324)
XLA Ops:
  0.7 117.0 %layer.1 = (bf16[256,768]{1,0:T(8,128)(2,1)}, f32[256,768]{1,0:T(8,128)}, f32[24,768]{1,0:T(8,128)}, f32[24,768]{1,0:T(8,128)}, f32[24,128]{1,0:T(8,128)}, /*ind...) custom-call(s32[1,8]{1,0:T(1,128)} %span.1, bf16[256,768]{1,0:T(8,128)(2,1)} %x_in.1, ...), custom_call_target="tpu_custom_call" | custom-call | tf_op jit(solution)/shard_map/layer/pallas_call | solution.py:1432
  117.7 4.3 %update.1 = (bf16[256,768]{1,0:T(8,128)(2,1)}, f32[256,768]{1,0:T(8,128)}, f32[1,1]{1,0:T(1,128)}, f32[24,768]{1,0:T(8,128)}, f32[24,128]{1,0:T(8,128)}, /*index...) custom-call(f32[8,128]{1,0:T(8,128)} %get-tuple-element.59.small, ...), custom_call_target="tpu_custom_call" | custom-call | tf_op jit(solution)/shard_map/update/pallas_call | solution.py:1457

commit v6 on v5

--- a/solution.py
+++ b/solution.py
@@ -481,7 +481,7 @@
             self.ref[self.rows(p, block, index), :] = value[:, p * 256 : p * 256 + 256]
 
 
-N_SEMS = (54, 93)
+N_SEMS = (53, 92)
 
 
 def layer_kernel(
@@ -501,7 +501,7 @@
     SV1, RV1, SV2, RV2, SV3, RV3,
     SU1, RU1, SU2, RU2, SU3, RU3, RXU,
     SD1, RD1, SD2, RD2, RXD,
-    NS1, NS2,
+    NS1,
     send_sems, recv_sems, save_sems, load_sems,
 ):
     tok = x.shape[0]
@@ -662,14 +662,15 @@
     out = leaving(SD1)
     sd_y = [make(SD1.at[zz], RD1.at[zz], dev_y, out=out) for zz in zk]
     sd_z, sd_r = relayed(SD2, RD2, RXD)
-    out, nf_in = leaving(NS1.at[three]), arriving(NS1.at[three])
-    n_f = [make(NS1.at[f], NS1.at[f], dev, out=out, into=nf_in) for dev in fsdp_devs]
-    seven = pl.ds(0, 7)
-    out, ns_in = leaving(NS2.at[seven]), arriving(NS2.at[seven])
-    n_s = [make(NS2.at[s], NS2.at[s], dev, out=out, into=ns_in) for dev in seq_devs]
+    me = f * 8 + s
+    others = [lax.rem(me + i, 32) for i in range(1, 32)]
+    everyone = [(lax.div(i, 8), lax.rem(i, 8)) for i in others]
+    most = pl.ds(0, 31)
+    out, n_in = leaving(NS1.at[most]), arriving(NS1.at[most])
+    n_all = [make(NS1.at[me], NS1.at[me], dev, out=out, into=n_in) for dev in everyone]
 
     barrier = pltpu.get_barrier_semaphore()
-    for dev in fsdp_devs + seq_devs:
+    for dev in everyone:
         pl.semaphore_signal(barrier, inc=1, device_id=dev, device_id_type=pl.DeviceIdType.MESH)
 
     loads = []
@@ -703,7 +704,7 @@
         RU2[2] = jnp.zeros((4, 24, D), BF16)
         RD2[2] = jnp.zeros((96, D), BF16)
 
-    pl.semaphore_wait(barrier, 10)
+    pl.semaphore_wait(barrier, 31)
     start(w_z[3], w_z[2], w_z[1], w_y[0])
     start(o_x, q_z[3], q_z[2], q_z[1], q_y[0])
     start(o_z[3], o_z[2], o_z[1], o_y[0])
@@ -1279,23 +1280,23 @@
     line = lax.broadcasted_iota(jnp.int32, (8, 128), 0)
     column = lax.broadcasted_iota(jnp.int32, (8, 128), 1)
     kv_line = jnp.where(column < 16, jnp.broadcast_to(kv_rows[11:12, :], (8, 128)), 0.0)
-    NS1[f] = jnp.where(line == 0, squares, kv_line)
-    start(*n_f)
-    arrive(nf_in)
-    kv_piece = NS1[0][1:2, :]
-    chip = NS1[0] + NS1[1] + NS1[2] + NS1[3]
-    part = chip[0:1, 0:1] + jnp.sum(kv_piece * kv_piece, 1, keepdims=True)
-    NS2[s] = jnp.broadcast_to(part, (8, 128))
-    start(*n_s)
+    NS1[me] = jnp.where(line == 0, squares, kv_line)
+    start(*n_all)
     arrive(su_fin)
     for i, g in enumerate((fc, fx, fd)):
         g_up[g] = RU3[i].astype(F32)
         save(g_up.at[g], to_up.at[g])
-    arrive(ns_in)
-    everything = NS2[0]
-    for i in range(1, 8):
-        everything = everything + NS2[i]
-    g_small[...] = jnp.where(line == 0, everything, jnp.broadcast_to(kv_piece, (8, 128)))
+    arrive(n_in)
+    everything = NS1[0]
+    pieces = jnp.zeros((1, 128), F32)
+    for i in range(8):
+        kv_piece = NS1[i][1:2, :]
+        pieces = pieces + kv_piece * kv_piece
+    for i in range(1, 32):
+        everything = everything + NS1[i]
+    whole = everything[0:1, 0:1] + jnp.sum(pieces, 1, keepdims=True)
+    kv_piece = NS1[s][1:2, :]
+    g_small[...] = jnp.where(line == 0, whole, jnp.broadcast_to(kv_piece, (8, 128)))
     save(g_small, to_small)
     copies.settle()
     assert (copies.sends, copies.recvs) == N_SEMS, (copies.sends, copies.recvs)
@@ -1426,7 +1427,7 @@
     scratch += [V((4, 4, 24, D), BF16)] * 2 + [V((3, 4, 24, D), BF16)] * 2
     scratch += [V((4, 24, D), BF16), V((3, 24, D), BF16), V((4, 24, D), BF16)]
     scratch += [V((4, 96, D), BF16)] * 2 + [V((3, 96, D), BF16)] * 2 + [V((96, D), BF16)]
-    scratch += [V((4, 8, 128), F32), V((8, 8, 128), F32)]
+    scratch += [V((32, 8, 128), F32)]
     scratch += [pltpu.SemaphoreType.DMA((n,)) for n in N_SEMS] + [pltpu.SemaphoreType.DMA((12,)), pltpu.SemaphoreType.DMA((9,))]
     kv_row = kv_bias.reshape(1, -1)
     bo, ig, g_q, g_o, g_kv, g_vec, g_up, g_dn, small = pl.pallas_call(

time: 122 us -> 120 us (0.984)
  Pallas kernels: 121 us -> 119 us
    pallas_call x1, Pallas kernels: 117 us -> 115 us  [fast_body(): pl.pallas_call(layer_kernel, name='layer', out_shape=results_here, in_spe...]
where the time goes in v6:
time: 120 us
  Pallas kernels  119 us (99%)
    pallas_call x1, Pallas kernels, fast_body(): pl.pallas_call(layer_kernel, name='layer', out_shape=results_here, in_spe...  115 us
    pallas_call x1, Pallas kernels, fast_body(): pl.pallas_call(update_kernel, name='update', grid=(1,), out_shape=outcome...  4.27 us

profile of v6, /device:TPU:0, one launch (start us, length us, event | category | flops | bytes accessed | tf_op | source)
XLA Modules:
  0.0 120.2 jit_solution(7062335103648511168)
XLA Ops:
  0.7 115.1 %layer.1 = (bf16[256,768]{1,0:T(8,128)(2,1)}, f32[256,768]{1,0:T(8,128)}, f32[24,768]{1,0:T(8,128)}, f32[24,768]{1,0:T(8,128)}, f32[24,128]{1,0:T(8,128)}, /*ind...) custom-call(s32[1,8]{1,0:T(1,128)} %span.1, bf16[256,768]{1,0:T(8,128)(2,1)} %x_in.1, ...), custom_call_target="tpu_custom_call" | custom-call | tf_op jit(solution)/shard_map/layer/pallas_call | solution.py:1433
  115.8 4.3 %update.1 = (bf16[256,768]{1,0:T(8,128)(2,1)}, f32[256,768]{1,0:T(8,128)}, f32[1,1]{1,0:T(1,128)}, f32[24,768]{1,0:T(8,128)}, f32[24,128]{1,0:T(8,128)}, /*index...) custom-call(f32[8,128]{1,0:T(8,128)} %get-tuple-element.59.small, ...), custom_call_target="tpu_custom_call" | custom-call | tf_op jit(solution)/shard_map/update/pallas_call | solution.py:1458

commit v7 on v6

--- a/solution.py
+++ b/solution.py
@@ -663,8 +663,9 @@
     sd_y = [make(SD1.at[zz], RD1.at[zz], dev_y, out=out) for zz in zk]
     sd_z, sd_r = relayed(SD2, RD2, RXD)
     me = f * 8 + s
-    others = [lax.rem(me + i, 32) for i in range(1, 32)]
-    everyone = [(lax.div(i, 8), lax.rem(i, 8)) for i in others]
+    everyone = [
+        (g, zk[k] * 2 + yy) for k in (3, 2, 1, 0) for yy in (yo, y) for g in (fd, fx, fc, f)
+    ][:-1]
     most = pl.ds(0, 31)
     out, n_in = leaving(NS1.at[most]), arriving(NS1.at[most])
     n_all = [make(NS1.at[me], NS1.at[me], dev, out=out, into=n_in) for dev in everyone]
@@ -1266,20 +1267,20 @@
         down_grad = down_grad + RD2[k].astype(F32)
     g_dn[...] = down_grad
     save(g_dn, to_dn)
-    up_end()
-    save(g_up.at[f], to_up.at[f])
-
     def energy(values):
         return jnp.sum(jnp.sum(values * values, 0, keepdims=True), 1, keepdims=True)
 
     lanes = lax.broadcasted_iota(jnp.int32, (24, 128), 1)
     squares = energy(q_grad) + energy(o_grad) + energy(kv_grad) + energy(jnp.where(lanes == 11, 0.0, vec_grad)) + energy(g_dn[...])
-    for total in up_totals:
-        squares = squares + energy(total)
     kv_rows = jnp.concatenate([vec_grad, jnp.zeros((104, 128), F32)], 0).T
     line = lax.broadcasted_iota(jnp.int32, (8, 128), 0)
     column = lax.broadcasted_iota(jnp.int32, (8, 128), 1)
     kv_line = jnp.where(column < 16, jnp.broadcast_to(kv_rows[11:12, :], (8, 128)), 0.0)
+    up_end()
+    save(g_up.at[f], to_up.at[f])
+
+    for total in up_totals:
+        squares = squares + energy(total)
     NS1[me] = jnp.where(line == 0, squares, kv_line)
     start(*n_all)
     arrive(su_fin)

time: 120 us -> 121 us (level)
  no operation moved by 1% of the time
where the time goes in v7:
time: 121 us; the launch traced here: 120 us
  Pallas kernels  120 us (99%)
    pallas_call x1, Pallas kernels, fast_body(): pl.pallas_call(layer_kernel, name='layer', out_shape=results_here, in_spe...  115 us
    pallas_call x1, Pallas kernels, fast_body(): pl.pallas_call(update_kernel, name='update', grid=(1,), out_shape=outcome...  4.27 us

profile of v7, /device:TPU:0, one launch (start us, length us, event | category | flops | bytes accessed | tf_op | source)
XLA Modules:
  0.0 120.4 jit_solution(3252371752229590460)
XLA Ops:
  0.7 115.3 %layer.1 = (bf16[256,768]{1,0:T(8,128)(2,1)}, f32[256,768]{1,0:T(8,128)}, f32[24,768]{1,0:T(8,128)}, f32[24,768]{1,0:T(8,128)}, f32[24,128]{1,0:T(8,128)}, /*ind...) custom-call(s32[1,8]{1,0:T(1,128)} %span.1, bf16[256,768]{1,0:T(8,128)(2,1)} %x_in.1, ...), custom_call_target="tpu_custom_call" | custom-call | tf_op jit(solution)/shard_map/layer/pallas_call | solution.py:1434
  115.9 4.3 %update.1 = (bf16[256,768]{1,0:T(8,128)(2,1)}, f32[256,768]{1,0:T(8,128)}, f32[1,1]{1,0:T(1,128)}, f32[24,768]{1,0:T(8,128)}, f32[24,128]{1,0:T(8,128)}, /*index...) custom-call(f32[8,128]{1,0:T(8,128)} %get-tuple-element.59.small, ...), custom_call_target="tpu_custom_call" | custom-call | tf_op jit(solution)/shard_map/update/pallas_call | solution.py:1459
